TPU v7x, 32 devices: a whole 2x2x4 slice. The times are simulated.
32 devices in a mesh: wide: 8 (over y, x, core), narrow: 4 (over z).
Axes of the slice: x: 2, y: 2, z: 4, core: 2. Of those that a mesh axis runs over, the one named last changes fastest.
Arguments:
- inputs: bfloat16 [10240, 768], P(('wide', 'narrow')), may hold values from -6 to 6
- memory: bfloat16 [32768, 768], P(('wide', 'narrow')), may hold values from -6 to 6
- targets: int32 [10240], P(('wide', 'narrow')), may hold values from 0 to 32127
- tgt_lengths: int32 [32, 2], P(('wide', 'narrow')), may hold values from 0 to 320, as said below
- src_lengths: int32 [32, 2], P(('wide', 'narrow')), may hold values from 0 to 1024, as said below
- self_gain: bfloat16 [768], P(('wide', 'narrow')), may hold values from 0.5 to 1.5
- self_query: bfloat16 [768, 768], P(('wide', 'narrow')), may hold values from -0.0546875 to 0.0546875
- self_key: bfloat16 [768, 768], P(('wide', 'narrow')), may hold values from -0.21875 to 0.21875
- self_value: bfloat16 [768, 768], P(('wide', 'narrow')), may hold values from -0.21875 to 0.21875
- self_out: bfloat16 [768, 768], P(('wide', 'narrow')), may hold values from -0.875 to 0.875
- cross_gain: bfloat16 [768], P(('wide', 'narrow')), may hold values from 0.5 to 1.5
- cross_query: bfloat16 [768, 768], P(('wide', 'narrow')), may hold values from -0.0546875 to 0.0546875
- cross_key: bfloat16 [768, 768], P(('wide', 'narrow')), may hold values from -0.21875 to 0.21875
- cross_value: bfloat16 [768, 768], P(('wide', 'narrow')), may hold values from -0.21875 to 0.21875
- cross_out: bfloat16 [768, 768], P(('wide', 'narrow')), may hold values from -0.875 to 0.875
- mlp_gain: bfloat16 [768], P(('wide', 'narrow')), may hold values from 0.5 to 1.5
- mlp_gate: bfloat16 [768, 2048], P(('wide', 'narrow')), may hold values from -0.21875 to 0.21875
- mlp_up: bfloat16 [768, 2048], P(('wide', 'narrow')), may hold values from -0.21875 to 0.21875
- mlp_down: bfloat16 [2048, 768], P(('wide', 'narrow')), may hold values from -0.125 to 0.125
- exit_gain: bfloat16 [768], P(('wide', 'narrow')), may hold values from 0.5 to 1.5
- embedding: bfloat16 [32128, 768], P('wide', 'narrow'), may hold values from -15 to 15
Outputs:
- activations: bfloat16 [10240, 768], P(('wide', 'narrow'))
- mean_loss: float32 [], replicated
- inputs_grad: float32 [10240, 768], P(('wide', 'narrow'))
- memory_grad: float32 [32768, 768], P(('wide', 'narrow'))
- self_gain_grad: float32 [768], P(('wide', 'narrow'))
- self_query_grad: float32 [768, 768], P(('wide', 'narrow'))
- self_key_grad: float32 [768, 768], P(('wide', 'narrow'))
- self_value_grad: float32 [768, 768], P(('wide', 'narrow'))
- self_out_grad: float32 [768, 768], P(('wide', 'narrow'))
- cross_gain_grad: float32 [768], P(('wide', 'narrow'))
- cross_query_grad: float32 [768, 768], P(('wide', 'narrow'))
- cross_key_grad: float32 [768, 768], P(('wide', 'narrow'))
- cross_value_grad: float32 [768, 768], P(('wide', 'narrow'))
- cross_out_grad: float32 [768, 768], P(('wide', 'narrow'))
- mlp_gain_grad: float32 [768], P(('wide', 'narrow'))
- mlp_gate_grad: float32 [768, 2048], P(('wide', 'narrow'))
- mlp_up_grad: float32 [768, 2048], P(('wide', 'narrow'))
- mlp_down_grad: float32 [2048, 768], P(('wide', 'narrow'))
- exit_gain_grad: float32 [768], P(('wide', 'narrow'))
- embedding_grad: float32 [32128, 768], P('wide', 'narrow')
Inputs may be any that keep to these rules, and one draw needn't show every extreme that they name: `tgt_lengths`: row b describes bucket b (the device at that place in the order wide, narrow): it holds one pair or 2 pairs, a missing pair having length 0; a row sums to at least 1 and at most 320, and the last row holds one pair of exactly 320. `src_lengths`: source lengths of the same pairs: a pair has a source of length 1 or more exactly when it has a target; a row sums to at most 1024, and some row holds one source of exactly 1024.
All inputs are finite; a program needn't handle non-finite values.
Results may differ from a plain program's by a relative error of at most 0.034.
The roundings to bfloat16 on the way count: a program that leaves them out, or rounds other values in their place, can miss the bound.
Values may be sent and summed in bfloat16 or wider, within the bound.
No kernel may reach another device: no remote copies, remote signals or barrier semaphores. Data moves between devices by JAX's collectives and lax.ppermute only.
A program may use at most 320 MiB of HBM per device.

v0:
```python
import math

import jax
import jax.numpy as jnp
from jax import lax
from jax.sharding import PartitionSpec as P

HEADS = 12


EPSILON = 1e-06
NEGATIVE = -1e30


def rms_norm(values, norm_gain):
    return (
        values * lax.rsqrt(jnp.mean(values * values, axis=-1, keepdims=True) + EPSILON) * norm_gain
    )


def segments(lengths, length):
    boundary = jnp.cumsum(lengths)
    places = jnp.arange(length, dtype=jnp.int32)
    return jnp.sum((places[:, None] >= boundary[None, :]).astype(jnp.int32), axis=1)


def matmul(left_side, right_side):
    return jnp.dot(left_side, right_side, preferred_element_type=jnp.float32)


def left_matmul(left_side, right_side):
    return lax.dot_general(
        left_side, right_side, (((0,), (0,)), ((), ())), preferred_element_type=jnp.float32
    )


def right_matmul(left_side, right_side):
    return lax.dot_general(
        left_side, right_side, (((1,), (1,)), ((), ())), preferred_element_type=jnp.float32
    )


def to_heads(values):
    return values.reshape(values.shape[0], HEADS, -1).transpose(1, 0, 2)


def from_heads(values):
    return values.transpose(1, 0, 2).reshape(values.shape[1], -1)


def gelu_mix(gate_pre, up_pre):
    return jax.nn.gelu(gate_pre, approximate=True) * up_pre


def attend(queries, key_rows, value_rows, allowed):

    def one_head(head_items):
        query_head, key_head, value_head = head_items
        scores = jnp.where(allowed, right_matmul(query_head, key_head), NEGATIVE)
        highest = jnp.max(scores, axis=1, keepdims=True)
        summed = jnp.sum(jnp.exp(scores - highest), axis=1, keepdims=True)
        log_total = highest + jnp.log(summed)
        weights_low = jnp.exp(scores - log_total).astype(jnp.bfloat16)
        return (matmul(weights_low, value_head), log_total[:, 0])

    outputs, log_totals = lax.map(
        one_head, (to_heads(queries), to_heads(key_rows), to_heads(value_rows))
    )
    return (from_heads(outputs).astype(jnp.bfloat16), log_totals)


def attend_back(queries, key_rows, value_rows, allowed, log_totals, out_grad):

    def one_head(head_items):
        query_head, key_head, value_head, log_head, grad_head = head_items
        scores = jnp.where(allowed, right_matmul(query_head, key_head), NEGATIVE)
        probs_full = jnp.exp(scores - log_head[:, None])
        prob_grad = right_matmul(grad_head, value_head)
        value_grad = left_matmul(probs_full.astype(jnp.bfloat16), grad_head)
        centre = jnp.sum(probs_full * prob_grad, axis=1, keepdims=True)
        score_grad = (probs_full * (prob_grad - centre)).astype(jnp.bfloat16)
        return (matmul(score_grad, key_head), left_matmul(score_grad, query_head), value_grad)

    query_grad, key_grad, value_grad = lax.map(
        one_head,
        (
            to_heads(queries),
            to_heads(key_rows),
            to_heads(value_rows),
            log_totals,
            to_heads(out_grad),
        ),
    )
    return (from_heads(query_grad), from_heads(key_grad), from_heads(value_grad))


def per_device(
    inputs,
    memory,
    targets,
    tgt_lengths,
    src_lengths,
    self_gain,
    self_query,
    self_key,
    self_value,
    self_out,
    cross_gain,
    cross_query,
    cross_key,
    cross_value,
    cross_out,
    mlp_gain,
    mlp_gate,
    mlp_up,
    mlp_down,
    exit_gain,
    embedding,
):
    token_count = inputs.shape[0]
    model_width = inputs.shape[1]
    memory_count = memory.shape[0]
    pair_slots = tgt_lengths.shape[1]
    wide_count = lax.axis_size("wide")
    slot_total = token_count * wide_count * lax.axis_size("narrow")
    logit_scale = 1.0 / math.sqrt(model_width)
    target_seg = segments(tgt_lengths[0], token_count)
    memory_seg = segments(src_lengths[0], memory_count)
    places = jnp.arange(token_count, dtype=jnp.int32)
    self_mask = (target_seg[:, None] == target_seg[None, :]) & (places[None, :] <= places[:, None])
    cross_mask = (target_seg[:, None] == memory_seg[None, :]) | (target_seg[:, None] == pair_slots)
    loss_weight = (target_seg < pair_slots).astype(jnp.float32)

    def collect(first_part, second_part, third_part, fourth_part, fifth_part):
        return (
            lax.all_gather(first_part, ("wide", "narrow"), axis=0, tiled=True),
            lax.all_gather(second_part, ("wide", "narrow"), axis=0, tiled=True),
            lax.all_gather(third_part, ("wide", "narrow"), axis=0, tiled=True),
            lax.all_gather(fourth_part, ("wide", "narrow"), axis=0, tiled=True),
            lax.all_gather(fifth_part, ("wide", "narrow"), axis=0, tiled=True),
        )

    def spread(first_part, second_part, third_part, fourth_part, fifth_part):
        return (
            lax.psum_scatter(first_part, ("wide", "narrow"), scatter_dimension=0, tiled=True),
            lax.psum_scatter(second_part, ("wide", "narrow"), scatter_dimension=0, tiled=True),
            lax.psum_scatter(third_part, ("wide", "narrow"), scatter_dimension=0, tiled=True),
            lax.psum_scatter(fourth_part, ("wide", "narrow"), scatter_dimension=0, tiled=True),
            lax.psum_scatter(fifth_part, ("wide", "narrow"), scatter_dimension=0, tiled=True),
        )

    stream_zero = inputs.astype(jnp.float32)
    self_set = collect(self_gain, self_query, self_key, self_value, self_out)
    normed_one = rms_norm(stream_zero, self_set[0].astype(jnp.float32)).astype(jnp.bfloat16)
    query_one = matmul(normed_one, self_set[1]).astype(jnp.bfloat16)
    key_one = matmul(normed_one, self_set[2]).astype(jnp.bfloat16)
    value_one = matmul(normed_one, self_set[3]).astype(jnp.bfloat16)
    attended_one, log_one = attend(query_one, key_one, value_one, self_mask)
    stream_one = stream_zero + matmul(attended_one, self_set[4])
    cross_set = collect(cross_gain, cross_query, cross_key, cross_value, cross_out)
    normed_two = rms_norm(stream_one, cross_set[0].astype(jnp.float32)).astype(jnp.bfloat16)
    query_two = matmul(normed_two, cross_set[1]).astype(jnp.bfloat16)
    key_two = matmul(memory, cross_set[2]).astype(jnp.bfloat16)
    value_two = matmul(memory, cross_set[3]).astype(jnp.bfloat16)
    attended_two, log_two = attend(query_two, key_two, value_two, cross_mask)
    stream_two = stream_one + matmul(attended_two, cross_set[4])
    mlp_set = collect(mlp_gain, mlp_gate, mlp_up, mlp_down, exit_gain)
    normed_three = rms_norm(stream_two, mlp_set[0].astype(jnp.float32)).astype(jnp.bfloat16)
    gate_pre = matmul(normed_three, mlp_set[1])
    up_pre = matmul(normed_three, mlp_set[2])
    hidden = gelu_mix(gate_pre, up_pre).astype(jnp.bfloat16)
    stream_three = stream_two + matmul(hidden, mlp_set[3])
    exit_scale = mlp_set[4].astype(jnp.float32)
    normed_four = rms_norm(stream_three, exit_scale).astype(jnp.bfloat16)
    columns = lax.all_gather(embedding, "narrow", axis=1, tiled=True)
    vocab_rows = columns.shape[0]
    vocab_ids = lax.axis_index("wide") * vocab_rows + jnp.arange(vocab_rows, dtype=jnp.int32)
    block_rows = lax.all_gather(columns, "wide", axis=0, tiled=True)
    peak = jnp.full((token_count,), NEGATIVE, jnp.float32)
    logits = right_matmul(normed_four, block_rows) * logit_scale
    block_ids = jnp.arange(block_rows.shape[0], dtype=jnp.int32)
    new_peak = jnp.maximum(peak, jnp.max(logits, axis=1))
    exp_sum = jnp.sum(jnp.exp(logits - new_peak[:, None]), axis=1)
    picked = jnp.sum(jnp.where(block_ids[None, :] == targets[:, None], logits, 0.0), axis=1)
    peak, exp_sum, picked = (new_peak, exp_sum, picked)
    log_total = peak + jnp.log(exp_sum)
    loss_all = lax.psum(jnp.sum(loss_weight * (log_total - picked)), ("wide", "narrow"))
    mean_loss = loss_all / slot_total
    block_rows = lax.all_gather(columns, "wide", axis=0, tiled=True)
    logits = right_matmul(normed_four, block_rows) * logit_scale
    block_ids = jnp.arange(block_rows.shape[0], dtype=jnp.int32)
    chosen = (block_ids[None, :] == targets[:, None]).astype(jnp.float32)
    logit_grad = (jnp.exp(logits - log_total[:, None]) - chosen) * loss_weight[:, None]
    normed_grad = matmul((logit_grad * logit_scale).astype(jnp.bfloat16), block_rows)
    group_log, group_weight, group_targets = (
        lax.all_gather(log_total, "wide", axis=0, tiled=True),
        lax.all_gather(loss_weight, "wide", axis=0, tiled=True),
        lax.all_gather(targets, "wide", axis=0, tiled=True),
    )
    block_rows = lax.all_gather(normed_four, "wide", axis=0, tiled=True)
    logits = right_matmul(block_rows, columns) * logit_scale
    chosen = (vocab_ids[None, :] == group_targets[:, None]).astype(jnp.float32)
    logit_grad = (jnp.exp(logits - group_log[:, None]) - chosen) * group_weight[:, None]
    embed_term = left_matmul((logit_grad * logit_scale).astype(jnp.bfloat16), block_rows)
    embedding_grad = lax.psum_scatter(
        embed_term.astype(jnp.bfloat16), "narrow", scatter_dimension=1, tiled=True
    ).astype(jnp.float32)
    unused, norm_pull = jax.vjp(rms_norm, stream_three, exit_scale)
    stream_grad, exit_gain_grad = norm_pull(normed_grad)
    mlp_back = collect(mlp_gain, mlp_gate, mlp_up, mlp_down, exit_gain)
    branch_grad = stream_grad.astype(jnp.bfloat16)
    down_grad = left_matmul(hidden, branch_grad)
    hidden_grad = right_matmul(branch_grad, mlp_back[3])
    unused, mix_pull = jax.vjp(gelu_mix, gate_pre, up_pre)
    gate_grad, up_grad = mix_pull(hidden_grad)
    gate_low = gate_grad.astype(jnp.bfloat16)
    up_low = up_grad.astype(jnp.bfloat16)
    gate_wgrad = left_matmul(normed_three, gate_low)
    up_wgrad = left_matmul(normed_three, up_low)
    normed_grad = right_matmul(gate_low, mlp_back[1]) + right_matmul(up_low, mlp_back[2])
    unused, norm_pull = jax.vjp(rms_norm, stream_two, mlp_back[0].astype(jnp.float32))
    branch_in, mlp_gain_grad = norm_pull(normed_grad)
    stream_grad = stream_grad + branch_in
    mlp_grads = spread(mlp_gain_grad, gate_wgrad, up_wgrad, down_grad, exit_gain_grad)
    cross_back = collect(cross_gain, cross_query, cross_key, cross_value, cross_out)
    branch_grad = stream_grad.astype(jnp.bfloat16)
    cross_out_grad = left_matmul(attended_two, branch_grad)
    attended_grad = right_matmul(branch_grad, cross_back[4]).astype(jnp.bfloat16)
    query_grad, key_grad, value_grad = attend_back(
        query_two, key_two, value_two, cross_mask, log_two, attended_grad
    )
    query_low = query_grad.astype(jnp.bfloat16)
    key_low = key_grad.astype(jnp.bfloat16)
    value_low = value_grad.astype(jnp.bfloat16)
    cross_query_grad = left_matmul(normed_two, query_low)
    cross_key_grad = left_matmul(memory, key_low)
    cross_value_grad = left_matmul(memory, value_low)
    memory_grad = right_matmul(key_low, cross_back[2]) + right_matmul(value_low, cross_back[3])
    normed_grad = right_matmul(query_low, cross_back[1])
    unused, norm_pull = jax.vjp(rms_norm, stream_one, cross_back[0].astype(jnp.float32))
    branch_in, cross_gain_grad = norm_pull(normed_grad)
    stream_grad = stream_grad + branch_in
    cross_grads = spread(
        cross_gain_grad, cross_query_grad, cross_key_grad, cross_value_grad, cross_out_grad
    )
    self_back = collect(self_gain, self_query, self_key, self_value, self_out)
    branch_grad = stream_grad.astype(jnp.bfloat16)
    self_out_grad = left_matmul(attended_one, branch_grad)
    attended_grad = right_matmul(branch_grad, self_back[4]).astype(jnp.bfloat16)
    query_grad, key_grad, value_grad = attend_back(
        query_one, key_one, value_one, self_mask, log_one, attended_grad
    )
    query_low = query_grad.astype(jnp.bfloat16)
    key_low = key_grad.astype(jnp.bfloat16)
    value_low = value_grad.astype(jnp.bfloat16)
    self_query_grad = left_matmul(normed_one, query_low)
    self_key_grad = left_matmul(normed_one, key_low)
    self_value_grad = left_matmul(normed_one, value_low)
    normed_grad = (
        right_matmul(query_low, self_back[1])
        + right_matmul(key_low, self_back[2])
        + right_matmul(value_low, self_back[3])
    )
    unused, norm_pull = jax.vjp(rms_norm, stream_zero, self_back[0].astype(jnp.float32))
    branch_in, self_gain_grad = norm_pull(normed_grad)
    inputs_grad = stream_grad + branch_in
    self_grads = spread(
        self_gain_grad, self_query_grad, self_key_grad, self_value_grad, self_out_grad
    )
    return (
        stream_three.astype(jnp.bfloat16),
        mean_loss,
        inputs_grad,
        memory_grad,
        self_grads[0],
        self_grads[1],
        self_grads[2],
        self_grads[3],
        self_grads[4],
        cross_grads[0],
        cross_grads[1],
        cross_grads[2],
        cross_grads[3],
        cross_grads[4],
        mlp_grads[0],
        mlp_grads[1],
        mlp_grads[2],
        mlp_grads[3],
        mlp_grads[4],
        embedding_grad,
    )


def solution(mesh):
    placed = (
        P(("wide", "narrow"), None),
        P(("wide", "narrow"), None),
        P(("wide", "narrow")),
        P(("wide", "narrow"), None),
        P(("wide", "narrow"), None),
        P(("wide", "narrow")),
        P(("wide", "narrow"), None),
        P(("wide", "narrow"), None),
        P(("wide", "narrow"), None),
        P(("wide", "narrow"), None),
        P(("wide", "narrow")),
        P(("wide", "narrow"), None),
        P(("wide", "narrow"), None),
        P(("wide", "narrow"), None),
        P(("wide", "narrow"), None),
        P(("wide", "narrow")),
        P(("wide", "narrow"), None),
        P(("wide", "narrow"), None),
        P(("wide", "narrow"), None),
        P(("wide", "narrow")),
        P("wide", "narrow"),
    )
    return jax.shard_map(
        per_device,
        mesh=mesh,
        in_specs=placed,
        out_specs=(
            P(("wide", "narrow"), None),
            P(),
            P(("wide", "narrow"), None),
            P(("wide", "narrow"), None),
            P(("wide", "narrow")),
            P(("wide", "narrow"), None),
            P(("wide", "narrow"), None),
            P(("wide", "narrow"), None),
            P(("wide", "narrow"), None),
            P(("wide", "narrow")),
            P(("wide", "narrow"), None),
            P(("wide", "narrow"), None),
            P(("wide", "narrow"), None),
            P(("wide", "narrow"), None),
            P(("wide", "narrow")),
            P(("wide", "narrow"), None),
            P(("wide", "narrow"), None),
            P(("wide", "narrow"), None),
            P(("wide", "narrow")),
            P("wide", "narrow"),
        ),
        check_vma=False,
    )
```

profile of v0, /device:TPU:0, one launch (start us, length us, event | category | flops | bytes accessed | tf_op | source)
XLA Modules:
  0.0 2613.4 jit_solution(7090359963194495823)
XLA Ops:
  15.3 112.4 %all-gather.37.cloned.1.call-done = bf16[4016,768]{0,1:T(8,128)(2,1)} async-done(((bf16[4016,192]{0,1:T(8,128)(2,1)}), bf16[4016,768]{0,1:T(8,128)(2,1)}) %all-gather.37.cloned.1.call-update) | async-done | bytes 6168592 | tf_op jit(solution)/shard_map/all_gather | solution.py:175
  137.8 38.7 %all-reduce.13 = (bf16[768]{0:T(1024)(128)(2,1)S(1)}, bf16[768]{0:T(1024)(128)(2,1)S(1)}, bf16[768]{0:T(1024)(128)(2,1)S(1)}, bf16[768]{0:T(1024)(128)(2,1)S(1)}) all-reduce(bf16[768]{0:T(1024)(128)(2,1)S(1)} %dynamic-update-slice, bf16[768]{0:T(1024)(128)(2,1)S(1)} %dynamic-update-slice.1, ...), channel_id=1, replica_groups=mesh['wide'=8,'narrow'=4] {'wide','narrow'}, use_global_device_ids=true, to_apply=%add | all-reduce | flops 3072 | bytes 12288
  242.6 52.2 %all-gather.19.cloned.1.call-done = bf16[768,768]{1,0:T(8,128)(2,1)} async-done(((bf16[24,768]{1,0:T(8,128)(2,1)}), bf16[768,768]{1,0:T(8,128)(2,1)}) %all-gather.19.cloned.1.call-update) | async-done | bytes 1179664 | tf_op jit(solution)/shard_map/all_gather | solution.py:139
  352.8 53.5 %all-gather.23.cloned.1.call-done = bf16[768,768]{1,0:T(8,128)(2,1)} async-done(((bf16[24,768]{1,0:T(8,128)(2,1)}), bf16[768,768]{1,0:T(8,128)(2,1)}) %all-gather.23.cloned.1.call-update) | async-done | bytes 1179664 | tf_op jit(solution)/shard_map/all_gather | solution.py:137
  411.7 50.5 %all-gather.25.cloned.1.call-done = bf16[768,768]{1,0:T(8,128)(2,1)} async-done(((bf16[24,768]{1,0:T(8,128)(2,1)}), bf16[768,768]{1,0:T(8,128)(2,1)}) %all-gather.25.cloned.1.call-update) | async-done | bytes 1179664 | tf_op jit(solution)/shard_map/all_gather | solution.py:138
  470.1 47.9 %all-gather.27.cloned.1.call-done = bf16[768,768]{1,0:T(8,128)(2,1)} async-done(((bf16[24,768]{1,0:T(8,128)(2,1)}), bf16[768,768]{1,0:T(8,128)(2,1)}) %all-gather.27.cloned.1.call-update) | async-done | bytes 1179664 | tf_op jit(solution)/shard_map/all_gather | solution.py:139
  526.1 40.5 %while.57 = (s32[]{:T(128)}, bf16[12,320,64]{1,2,0:T(8,128)(2,1)S(1)}, f32[12,320]{1,0:T(8,128)S(1)}, bf16[12,320,64]{2,1,0:T(8,128)(2,1)}, bf16[12,1024,64]{2,1...) while((s32[]{:T(128)}, ...), condition=%wide.region_13.14_spmd.clone, body=%wide.region_10.13_spmd.clone.sunk | while | flops 86507200 | bytes 4659385 | solution.py:66
  578.2 56.5 %all-gather.31.cloned.1.call-done = bf16[768,2048]{1,0:T(8,128)(2,1)} async-done(((bf16[24,2048]{1,0:T(8,128)(2,1)}), bf16[768,2048]{1,0:T(8,128)(2,1)}) %all-gather.31.cloned.1.call-update) | async-done | bytes 3145744 | tf_op jit(solution)/shard_map/all_gather | solution.py:137
  639.4 56.0 %all-gather.33.cloned.1.call-done = bf16[768,2048]{1,0:T(8,128)(2,1)} async-done(((bf16[24,2048]{1,0:T(8,128)(2,1)}), bf16[768,2048]{1,0:T(8,128)(2,1)}) %all-gather.33.cloned.1.call-update) | async-done | bytes 3145744 | tf_op jit(solution)/shard_map/all_gather | solution.py:138
  701.7 54.4 %all-gather.35.cloned.1.call-done = bf16[2048,768]{1,0:T(8,128)(2,1)} async-done(((bf16[64,768]{1,0:T(8,128)(2,1)}), bf16[2048,768]{1,0:T(8,128)(2,1)}) %all-gather.35.cloned.1.call-update) | async-done | bytes 3145744 | tf_op jit(solution)/shard_map/all_gather | solution.py:139
  761.9 223.1 %all-gather.39.cloned.1.call-done = bf16[32128,768]{1,0:T(8,128)(2,1)} async-done(((bf16[4016,768]{1,0:T(8,128)(2,1)}), bf16[32128,768]{1,0:T(8,128)(2,1)}) %all-gather.39.cloned.1.call-update) | async-done | bytes 49348624 | tf_op jit(solution)/shard_map/all_gather | solution.py:178
  1102.9 113.0 %while.58 = (s32[]{:T(128)}, bf16[12,320,64]{1,2,0:T(8,128)(2,1)}, bf16[12,1024,64]{1,2,0:T(8,128)(2,1)}, bf16[12,1024,64]{1,2,0:T(8,128)(2,1)}, bf16[12,320,64]...) while((s32[]{:T(128)}, bf16[12,320,64]{1,2,0:T(8,128)(2,1)}, ...), condition=%wide.region_25.26_spmd.clone, body=%wide.region_23.25_spmd.clone.sunk | while | flops 212991680 | bytes 11519113 | solution.py:84
  1301.9 99.2 %while.59 = (s32[]{:T(128)}, bf16[12,320,64]{1,2,0:T(8,128)(2,1)}, bf16[12,320,64]{1,2,0:T(8,128)(2,1)}, bf16[12,320,64]{1,2,0:T(8,128)(2,1)}, bf16[12,320,64]{2...) while((s32[]{:T(128)}, bf16[12,320,64]{1,2,0:T(8,128)(2,1)}, ...), condition=%wide.region_29.30_spmd.clone, body=%wide.region_27.29_spmd.clone.sunk | while | flops 66662080 | bytes 3973241 | solution.py:84
  1463.1 39.8 %all-reduce.11 = (f32[]{:T(128)}, f32[768]{0:T(1024)S(1)}, f32[768]{0:T(1024)S(1)}, f32[768]{0:T(1024)S(1)}, f32[768]{0:T(1024)S(1)}) all-reduce(f32[]{:T(128)} %select_reduce_fusion.1, f32[768]{0:T(1024)S(1)} %get-tuple-element.566, f32[768]{0:T(1024)S(1)} %copy-done.47, ...), channel_id=1, replica_groups=mesh['wide'=8,'narrow'=4] {'wide','narrow'}, use_global_device_ids=true, to_apply=%region_20.21 | all-reduce | flops 3073 | bytes 24584 | tf_op jit(solution)/shard_map/psum | solution.py:187
  1516.9 103.1 %reduce-scatter.19.cloned.1.call-done = f32[24,768]{1,0:T(8,128)} async-done(((f32[768,768]{1,0:T(8,128)}), f32[24,768]{1,0:T(8,128)}) %reduce-scatter.19.cloned.1.call-update) | async-done | bytes 73744 | tf_op jit(solution)/shard_map/reduce_scatter | solution.py:147
  1620.0 103.7 %reduce-scatter.21.cloned.1.call-done = f32[24,768]{1,0:T(8,128)} async-done(((f32[768,768]{1,0:T(8,128)}), f32[24,768]{1,0:T(8,128)}) %reduce-scatter.21.cloned.1.call-update) | async-done | bytes 73744 | tf_op jit(solution)/shard_map/reduce_scatter | solution.py:148
  1723.7 104.9 %reduce-scatter.23.cloned.1.call-done = f32[24,768]{1,0:T(8,128)} async-done(((f32[768,768]{1,0:T(8,128)}), f32[24,768]{1,0:T(8,128)}) %reduce-scatter.23.cloned.1.call-update) | async-done | bytes 73744 | tf_op jit(solution)/shard_map/reduce_scatter | solution.py:149
  1828.6 103.8 %reduce-scatter.25.cloned.1.call-done = f32[24,768]{1,0:T(8,128)} async-done(((f32[768,768]{1,0:T(8,128)}), f32[24,768]{1,0:T(8,128)}) %reduce-scatter.25.cloned.1.call-update) | async-done | bytes 73744 | tf_op jit(solution)/shard_map/reduce_scatter | solution.py:146
  1932.3 104.8 %reduce-scatter.37.cloned.1.call-done = f32[24,768]{1,0:T(8,128)} async-done(((f32[768,768]{1,0:T(8,128)}), f32[24,768]{1,0:T(8,128)}) %reduce-scatter.37.cloned.1.call-update) | async-done | bytes 73744
  2037.1 103.9 %reduce-scatter.39.cloned.1.call-done = f32[24,768]{1,0:T(8,128)} async-done(((f32[768,768]{1,0:T(8,128)}), f32[24,768]{1,0:T(8,128)}) %reduce-scatter.39.cloned.1.call-update) | async-done | bytes 73744
  2141.0 104.8 %reduce-scatter.27.cloned.1.call-done = f32[24,768]{1,0:T(8,128)} async-done(((f32[768,768]{1,0:T(8,128)}), f32[24,768]{1,0:T(8,128)}) %reduce-scatter.27.cloned.1.call-update) | async-done | bytes 73744 | tf_op jit(solution)/shard_map/reduce_scatter | solution.py:149
  2245.8 119.4 %reduce-scatter.29.cloned.1.call-done = f32[24,2048]{1,0:T(8,128)} async-done(((f32[768,2048]{1,0:T(8,128)}), f32[24,2048]{1,0:T(8,128)}) %reduce-scatter.29.cloned.1.call-update) | async-done | bytes 196624 | tf_op jit(solution)/shard_map/reduce_scatter | solution.py:146
  2365.2 120.7 %reduce-scatter.31.cloned.1.call-done = f32[24,2048]{1,0:T(8,128)} async-done(((f32[768,2048]{1,0:T(8,128)}), f32[24,2048]{1,0:T(8,128)}) %reduce-scatter.31.cloned.1.call-update) | async-done | bytes 196624 | tf_op jit(solution)/shard_map/reduce_scatter | solution.py:147
  2485.9 119.6 %reduce-scatter.33.cloned.1.call-done = f32[64,768]{1,0:T(8,128)} async-done(((f32[2048,768]{1,0:T(8,128)}), f32[64,768]{1,0:T(8,128)}) %reduce-scatter.33.cloned.1.call-update) | async-done | bytes 196624 | tf_op jit(solution)/shard_map/reduce_scatter | solution.py:148
  (631 shorter events, 747.5 us)
Async XLA Ops:
  8.7 230.5 %all-gather.17.cloned.1.call-start = ((), (), s32[]{:S(2)}) async-start(), calls=%async_computation.13 | async-start | bytes 1216512 | tf_op jit(solution)/shard_map/all_gather | solution.py:138
  9.4 285.4 %all-gather.19.cloned.1.call-start = ((), (), s32[]{:S(2)}) async-start(), calls=%async_computation.14 | async-start | bytes 1216512 | tf_op jit(solution)/shard_map/all_gather | solution.py:139
  10.0 340.6 %all-gather.21.cloned.1.call-start = ((), (), s32[]{:S(2)}) async-start(), calls=%async_computation.15 | async-start | bytes 1216512 | tf_op jit(solution)/shard_map/all_gather | solution.py:140
  10.6 395.7 %all-gather.23.cloned.1.call-start = ((), (), s32[]{:S(2)}) async-start(), calls=%async_computation.16 | async-start | bytes 1216512 | tf_op jit(solution)/shard_map/all_gather | solution.py:137
  11.2 451.0 %all-gather.25.cloned.1.call-start = ((), (), s32[]{:S(2)}) async-start(), calls=%async_computation.17 | async-start | bytes 1216512 | tf_op jit(solution)/shard_map/all_gather | solution.py:138
  11.9 506.1 %all-gather.27.cloned.1.call-start = ((), (), s32[]{:S(2)}) async-start(), calls=%async_computation.18 | async-start | bytes 1216512 | tf_op jit(solution)/shard_map/all_gather | solution.py:139
  12.7 561.3 %all-gather.29.cloned.1.call-start = ((), (), s32[]{:S(2)}) async-start(), calls=%async_computation.19 | async-start | bytes 1216512 | tf_op jit(solution)/shard_map/all_gather | solution.py:140
  13.4 621.3 %all-gather.31.cloned.1.call-start = ((), (), s32[]{:S(2)}) async-start(), calls=%async_computation.20 | async-start | bytes 3244032 | tf_op jit(solution)/shard_map/all_gather | solution.py:137
  14.0 681.5 %all-gather.33.cloned.1.call-start = ((), (), s32[]{:S(2)}) async-start(), calls=%async_computation.21 | async-start | bytes 3244032 | tf_op jit(solution)/shard_map/all_gather | solution.py:138
  14.7 741.4 %all-gather.35.cloned.1.call-start = ((), (), s32[]{:S(2)}) async-start(), calls=%async_computation.22 | async-start | bytes 3244032 | tf_op jit(solution)/shard_map/all_gather | solution.py:139
  15.3 969.7 %all-gather.39.cloned.1.call-start = ((), (), s32[]{:S(2)}) async-start(), calls=%async_computation.24 | async-start | bytes 55517184 | tf_op jit(solution)/shard_map/all_gather | solution.py:178
  136.4 1110.0 %all-gather.41.cloned.1.call-start = ((), (), s32[]{:S(2)}) async-start(), calls=%async_computation.34 | async-start | bytes 4423680 | tf_op jit(solution)/shard_map/all_gather | solution.py:200
  761.8 751.6 %reduce-scatter.35.cloned.1.call-start = ((), (), s32[]{:S(2)}) async-start(), calls=%async_computation.35 | async-start | bytes 7864320 | tf_op jit(solution)/shard_map/reduce_scatter | solution.py:205
  1299.1 217.8 %reduce-scatter.17.cloned.1.call-start = ((), (), s32[]{:S(2)}) async-start(), calls=%async_computation.25 | async-start | bytes 2433024 | tf_op jit(solution)/shard_map/reduce_scatter | solution.py:146
  1404.5 215.4 %reduce-scatter.19.cloned.1.call-start = ((), (), s32[]{:S(2)}) async-start(), calls=%async_computation.26 | async-start | bytes 2433024 | tf_op jit(solution)/shard_map/reduce_scatter | solution.py:147
  1408.0 315.8 %reduce-scatter.21.cloned.1.call-start = ((), (), s32[]{:S(2)}) async-start(), calls=%async_computation.27 | async-start | bytes 2433024 | tf_op jit(solution)/shard_map/reduce_scatter | solution.py:148
  1411.4 417.2 %reduce-scatter.23.cloned.1.call-start = ((), (), s32[]{:S(2)}) async-start(), calls=%async_computation.28 | async-start | bytes 2433024 | tf_op jit(solution)/shard_map/reduce_scatter | solution.py:149
  1415.0 517.3 %reduce-scatter.25.cloned.1.call-start = ((), (), s32[]{:S(2)}) async-start(), calls=%async_computation.29 | async-start | bytes 2433024 | tf_op jit(solution)/shard_map/reduce_scatter | solution.py:146
  1418.4 618.7 %reduce-scatter.37.cloned.1.call-start = ((), (), s32[]{:S(2)}) async-start(), calls=%async_computation.36 | async-start | bytes 2433024
  1425.8 715.2 %reduce-scatter.39.cloned.1.call-start = ((), (), s32[]{:S(2)}) async-start(), calls=%async_computation.37 | async-start | bytes 2433024
  1433.2 812.7 %reduce-scatter.27.cloned.1.call-start = ((), (), s32[]{:S(2)}) async-start(), calls=%async_computation.30 | async-start | bytes 2433024 | tf_op jit(solution)/shard_map/reduce_scatter | solution.py:149
  1437.6 927.6 %reduce-scatter.29.cloned.1.call-start = ((), (), s32[]{:S(2)}) async-start(), calls=%async_computation.31 | async-start | bytes 6488064 | tf_op jit(solution)/shard_map/reduce_scatter | solution.py:146
  1443.5 1042.4 %reduce-scatter.31.cloned.1.call-start = ((), (), s32[]{:S(2)}) async-start(), calls=%async_computation.32 | async-start | bytes 6488064 | tf_op jit(solution)/shard_map/reduce_scatter | solution.py:147
  1449.4 1156.1 %reduce-scatter.33.cloned.1.call-start = ((), (), s32[]{:S(2)}) async-start(), calls=%async_computation.33 | async-start | bytes 6488064 | tf_op jit(solution)/shard_map/reduce_scatter | solution.py:148
  (75 other events, 3149.7 us)
Sparse Core Ops, SparseCore 0:
  9.6 118.0 all-gather.36
  185.9 53.2 all-gather.16
  241.8 53.0 all-gather.18
  297.5 53.0 all-gather.20
  353.3 53.0 all-gather.22
  409.1 53.0 all-gather.24
  465.0 53.0 all-gather.26
  520.9 53.0 all-gather.28
  576.7 57.9 all-gather.30
  637.6 57.8 all-gather.32
  698.2 57.8 all-gather.34
  758.0 226.9 all-gather.38
  1299.3 110.3 reduce-scatter.34
  1415.3 99.9 reduce-scatter.16
  1521.9 98.0 reduce-scatter.18
  1625.7 97.9 reduce-scatter.20
  1730.4 98.1 reduce-scatter.22
  1834.3 97.9 reduce-scatter.24
  1939.0 98.0 reduce-scatter.36
  2043.0 97.9 reduce-scatter.38
  2147.7 98.0 reduce-scatter.26
  2251.9 113.2 reduce-scatter.28
  2372.4 113.5 reduce-scatter.30
  2492.0 113.4 reduce-scatter.32
  (2 shorter events, 88.0 us)
where the time goes:
time: 2630 us; the launch traced here: 2610 us
  waiting for transfers between devices  1860 us (71%)
  matrix products  482 us (18%)
  blocking collectives  127 us (5%)
  local copies, waits for them, and re-layouts  71.7 us (3%)
  other arithmetic  48.5 us (2%)
    reduce_scatter x2, waiting for transfers between devices, spread(): lax.psum_scatter(third_part, ('wide', 'narrow'), scatter_dimension=0, til...  224 us
    reduce_scatter x2, waiting for transfers between devices, spread(): lax.psum_scatter(fourth_part, ('wide', 'narrow'), scatter_dimension=0, ti...  223 us
    reduce_scatter x3, waiting for transfers between devices, spread(): lax.psum_scatter(second_part, ('wide', 'narrow'), scatter_dimension=0, ti...  223 us
    all_gather x1, waiting for transfers between devices, per_device(): block_rows = lax.all_gather(columns, 'wide', axis=0, tiled=True)  223 us
    unnamed x28, waiting for transfers between devices  216 us
    reduce_scatter x2, waiting for transfers between devices, spread(): lax.psum_scatter(fifth_part, ('wide', 'narrow'), scatter_dimension=0, til...  210 us
    dot_general x85, matrix products, right_matmul(): lax.dot_general(left_side, right_side, (((1,), (1,)), ((), ())), preferre...  190 us
    all_gather x3, waiting for transfers between devices, collect(): lax.all_gather(fourth_part, ('wide', 'narrow'), axis=0, tiled=True)  155 us
  transfers between devices with their start and end apart: 26, of which 22 were waited for; matrix products, arithmetic and copies ran while one was open for 21% of the time, Pallas kernels for 0%

commit v1 on v0

v1 whole, which is shorter than its diff:
```python
import functools
import math

import jax
import jax.numpy as jnp
from jax import lax
from jax.experimental import pallas as pl
from jax.experimental.pallas import tpu as pltpu
from jax.sharding import PartitionSpec as P

HEADS = 12
EPSILON = 1e-06
NEGATIVE = -1e30
F32 = jnp.float32
BF16 = jnp.bfloat16
LANES = 128
ROW_TILE = 256
VOCAB_TILE = 512
MIX = math.sqrt(2.0 / math.pi)
CUBE = 0.044715

VMEM = pl.BlockSpec(memory_space=pltpu.VMEM)
SMEM = pl.BlockSpec(memory_space=pltpu.SMEM)
ANY = pl.BlockSpec(memory_space=pl.ANY)
PARAMS = pltpu.CompilerParams(vmem_limit_bytes=60 * 2**20)


def nn(left, right):
    return lax.dot_general(left, right, (((1,), (0,)), ((), ())), preferred_element_type=F32)


def nt(left, right):
    return lax.dot_general(left, right, (((1,), (1,)), ((), ())), preferred_element_type=F32)


def tn(left, right):
    return lax.dot_general(left, right, (((0,), (0,)), ((), ())), preferred_element_type=F32)


def like(shape, kind):
    return jax.ShapeDtypeStruct(shape, kind)


def stage_masks(count):
    up = [1 << bit for bit in range(1, count.bit_length() - 1)]
    return up, up[::-1]


def stage_pairs(count):
    even, odd = stage_masks(count)
    return [[(v, v ^ (odd if v % 2 else even)[i]) for v in range(count)] for i in range(len(even))]


def flip_pairs(count):
    return [(v, v ^ 1) for v in range(count)]


def slot_tables(count):
    tables = []
    for masks in stage_masks(count):
        slots = [0]
        for mask in masks:
            slots = slots + [slot ^ mask for slot in slots]
        tables.append(slots)
    even, odd = tables
    return (
        even + [1 ^ slot for slot in odd],
        odd + [1 ^ slot for slot in even],
    )


def slot_places(wide, count):
    even, odd = slot_tables(count)
    table = jnp.where(wide % 2 == 0, jnp.array(even, jnp.int32), jnp.array(odd, jnp.int32))
    return wide ^ table


def gather_wide(block, count):
    held = block[None]
    for pairs in stage_pairs(count):
        held = jnp.concatenate([held, lax.ppermute(held, "wide", pairs)], axis=0)
    return held, lax.ppermute(held, "wide", flip_pairs(count))


def scatter_wide(mine, other, count):
    held = mine.astype(F32) + lax.ppermute(other, "wide", flip_pairs(count)).astype(F32)
    for pairs in stage_pairs(count)[::-1]:
        half = held.shape[0] // 2
        sent = lax.ppermute(held[half:].astype(BF16), "wide", pairs)
        held = held[:half] + sent.astype(F32)
    return held[0]


def narrow_pairs(count, step):
    return [(v, v ^ step) for v in range(count)]


def gather_narrow(block, narrow, count):
    pieces = [block] + [
        lax.ppermute(block, "narrow", narrow_pairs(count, step)) for step in range(1, count)
    ]
    stacked = jnp.stack(pieces)
    return [
        lax.dynamic_index_in_dim(stacked, narrow ^ place, 0, keepdims=False)
        for place in range(count)
    ]


def scatter_narrow(blocks, narrow, count):
    total = lax.dynamic_index_in_dim(blocks, narrow, 0, keepdims=False).astype(F32)
    for step in range(1, count):
        sent = lax.dynamic_index_in_dim(blocks, narrow ^ step, 0, keepdims=False)
        total = total + lax.ppermute(
            sent.astype(BF16), "narrow", narrow_pairs(count, step)
        ).astype(F32)
    return total


def weight_copies(places, mine, other, target, rows, sems):
    half = mine.shape[0]
    matrices = target.shape[0]
    copies = []
    for slot in range(2 * half):
        source = mine if slot < half else other
        start = pl.multiple_of(places[slot] * rows, 8)
        for matrix in range(matrices):
            copies.append(
                pltpu.make_async_copy(
                    source.at[slot % half, pl.ds(matrix * rows, rows), :],
                    target.at[matrix, pl.ds(start, rows), :],
                    sems.at[slot, matrix],
                )
            )
    return copies


def store_blocks(places, value_ref, matrix, rows, mine, other):
    half = mine.shape[0]
    for slot in range(2 * half):
        target = mine if slot < half else other
        start = pl.multiple_of(places[slot] * rows, 8)
        target[slot % half, pl.ds(matrix * rows, rows), :] = value_ref[pl.ds(start, rows), :]


def norm_scale(values):
    return lax.rsqrt(jnp.mean(values * values, axis=-1, keepdims=True) + EPSILON)


def norm_back(values, gain, grad):
    root = norm_scale(values)
    scaled = gain * grad
    gain_grad = jnp.sum(grad * values * root, axis=0, keepdims=True)
    inner = jnp.mean(scaled * values, axis=-1, keepdims=True)
    return root * scaled - values * (root * root * root) * inner, gain_grad


def query_segments(lengths, count):
    places = lax.broadcasted_iota(jnp.int32, (1, count), 1)
    segment = jnp.zeros((1, count), jnp.int32)
    edge = jnp.int32(0)
    for pair in range(lengths.shape[0]):
        edge = edge + lengths[pair]
        segment = segment + (places >= edge).astype(jnp.int32)
    return places, segment


def fill_self_bias(bias, lengths):
    count = bias.shape[1]
    places, segment = query_segments(lengths, count)
    low = jnp.zeros((1, count), jnp.int32)
    edge = jnp.int32(0)
    for pair in range(lengths.shape[0]):
        edge = edge + lengths[pair]
        low = jnp.where(segment == pair + 1, edge, low)
    keys = lax.broadcasted_iota(jnp.int32, bias.shape, 0)
    bias[...] = jnp.where((keys >= low) & (keys <= places), 0.0, NEGATIVE)


def fill_cross_bias(bias, lengths, sources):
    count = bias.shape[1]
    places, segment = query_segments(lengths, count)
    low = jnp.zeros((1, count), jnp.int32)
    high = jnp.full((1, count), bias.shape[0], jnp.int32)
    edge = jnp.int32(0)
    for pair in range(lengths.shape[0]):
        low = jnp.where(segment == pair, edge, low)
        edge = edge + sources[pair]
        high = jnp.where(segment == pair, edge, high)
    keys = lax.broadcasted_iota(jnp.int32, bias.shape, 0)
    bias[...] = jnp.where((keys >= low) & (keys < high), 0.0, NEGATIVE)


def first_half(width):
    return lax.broadcasted_iota(jnp.int32, (1, width), 1) < width // 2


def attend(queries, keys, values, bias, outputs, totals):
    width = 2 * (queries.shape[1] // HEADS)
    chosen = first_half(width)

    def pair_of_heads(pair, carry):
        columns = pl.ds(pl.multiple_of(pair * width, width), width)
        query = queries[:, columns]
        key = keys[:, columns]
        value = values[:, columns].T
        halves = []
        for side in range(2):
            own = jnp.where(chosen if side == 0 else ~chosen, query, 0)
            scores = nt(key, own) + bias[...]
            highest = jnp.max(scores, axis=0, keepdims=True)
            raised = jnp.exp(scores - highest)
            summed = jnp.sum(raised, axis=0, keepdims=True)
            weights = (raised * (1.0 / summed)).astype(BF16)
            totals[2 * pair + side] = highest + jnp.log(summed)
            halves.append(nn(value[side * width // 2 : (side + 1) * width // 2], weights))
        outputs[:, columns] = jnp.concatenate(halves, axis=0).T.astype(BF16)
        return carry

    lax.fori_loop(0, HEADS // 2, pair_of_heads, 0)


def attend_back(queries, keys, values, bias, totals, grads, query_low, key_low, value_low):
    width = 2 * (queries.shape[1] // HEADS)
    chosen = first_half(width)

    def pair_of_heads(pair, carry):
        columns = pl.ds(pl.multiple_of(pair * width, width), width)
        query = queries[:, columns]
        key = keys[:, columns]
        value = values[:, columns]
        grad = grads[:, columns]
        key_across = key.T
        query_parts, key_parts, value_parts = [], [], []
        for side in range(2):
            mine = chosen if side == 0 else ~chosen
            scores = nt(key, jnp.where(mine, query, 0)) + bias[...]
            probs = jnp.exp(scores - totals[2 * pair + side])
            prob_grad = nt(value, jnp.where(mine, grad, 0))
            value_parts.append(nn(probs.astype(BF16), grad))
            weighted = probs * prob_grad
            centre = jnp.sum(weighted, axis=0, keepdims=True)
            score_grad = (weighted - probs * centre).astype(BF16)
            key_parts.append(nn(score_grad, query))
            query_parts.append(
                nn(key_across[side * width // 2 : (side + 1) * width // 2], score_grad)
            )
        query_low[:, columns] = jnp.concatenate(query_parts, axis=0).T.astype(BF16)
        key_low[:, columns] = jnp.where(chosen, key_parts[0], key_parts[1]).astype(BF16)
        value_low[:, columns] = jnp.where(chosen, value_parts[0], value_parts[1]).astype(BF16)
        return carry

    lax.fori_loop(0, HEADS // 2, pair_of_heads, 0)


def self_forward_kernel(
    places, lengths, inputs, gain, mine, other,
    normed, query, key, value, attended, totals, stream,
    weights, bias, sems,
):
    copies = weight_copies(places, mine, other, weights, weights.shape[1] // (2 * mine.shape[0]), sems)
    for copy in copies:
        copy.start()
    values = inputs[...].astype(F32)
    fill_self_bias(bias, lengths)
    low = (values * norm_scale(values) * gain[...]).astype(BF16)
    normed[...] = low
    for copy in copies:
        copy.wait()
    query[...] = nn(low, weights[0]).astype(BF16)
    key[...] = nn(low, weights[1]).astype(BF16)
    value[...] = nn(low, weights[2]).astype(BF16)
    attend(query, key, value, bias, attended, totals)
    stream[...] = values + nn(attended[...], weights[3])


def memory_kernel(places, memory, mine, other, key, value, weights, sems):
    rows = weights.shape[1] // (2 * mine.shape[0])
    copies = weight_copies(
        places, mine.at[:, pl.ds(rows, 2 * rows), :], other.at[:, pl.ds(rows, 2 * rows), :],
        weights, rows, sems,
    )
    for copy in copies:
        copy.start()
    for copy in copies:
        copy.wait()
    key[...] = nn(memory[...], weights[0]).astype(BF16)
    value[...] = nn(memory[...], weights[1]).astype(BF16)


def cross_forward_kernel(
    places, lengths, sources, stream_in, gain, key, value, mine, other,
    normed, query, attended, totals, stream,
    weights, bias, sems,
):
    rows = weights.shape[1] // (2 * mine.shape[0])
    first = weight_copies(places, mine, other, weights.at[pl.ds(0, 1)], rows, sems.at[0])
    last = weight_copies(
        places, mine.at[:, pl.ds(3 * rows, rows), :], other.at[:, pl.ds(3 * rows, rows), :],
        weights.at[pl.ds(1, 1)], rows, sems.at[1],
    )
    for copy in first + last:
        copy.start()
    values = stream_in[...]
    fill_cross_bias(bias, lengths, sources)
    low = (values * norm_scale(values) * gain[...]).astype(BF16)
    normed[...] = low
    for copy in first + last:
        copy.wait()
    query[...] = nn(low, weights[0]).astype(BF16)
    attend(query, key, value, bias, attended, totals)
    stream[...] = values + nn(attended[...], weights[1])


def mlp_forward_kernel(
    places, stream_in, gain, exit_gain, mine, other, down_mine, down_other,
    normed, gate, up, hidden, stream, activations, exit_normed,
    weights, down, sems, down_sems,
):
    rows = weights.shape[1] // (2 * mine.shape[0])
    down_rows = down.shape[1] // (2 * mine.shape[0])
    first = weight_copies(places, mine, other, weights, rows, sems)
    last = weight_copies(places, down_mine, down_other, down, down_rows, down_sems)
    for copy in first + last:
        copy.start()
    values = stream_in[...]
    low = (values * norm_scale(values) * gain[...]).astype(BF16)
    normed[...] = low
    for copy in first:
        copy.wait()
    width = weights.shape[2]
    step = width // 4
    for part in range(4):
        columns = pl.ds(part * step, step)
        gate_pre = nn(low, weights[0, :, columns])
        up_pre = nn(low, weights[1, :, columns])
        gate[:, columns] = gate_pre
        up[:, columns] = up_pre
        bent = jnp.tanh(MIX * (gate_pre + CUBE * (gate_pre * gate_pre * gate_pre)))
        hidden[:, columns] = (0.5 * gate_pre * (1.0 + bent) * up_pre).astype(BF16)
    for copy in last:
        copy.wait()
    out = values + nn(hidden[...], down[0])
    stream[...] = out
    activations[...] = out.astype(BF16)
    exit_normed[...] = (out * norm_scale(out) * exit_gain[...]).astype(BF16)


def exit_scores_kernel(
    places, mine, other, targets, table, raised, across, stats,
    tokens, scores, sems, *, vocab, scale,
):
    half = mine.shape[0]
    rows = mine.shape[1]
    step = pl.program_id(0)
    tile = raised.shape[0]

    @pl.when(step == 0)
    def load():
        copies = []
        for slot in range(2 * half):
            source = mine if slot < half else other
            copies.append(
                pltpu.make_async_copy(
                    source.at[slot % half],
                    tokens.at[pl.ds(pl.multiple_of(places[slot] * rows, 8), rows), :],
                    sems.at[slot],
                )
            )
        for copy in copies:
            copy.start()
        for copy in copies:
            copy.wait()

    own = tokens[pl.ds(pl.multiple_of(step * tile, tile), tile), :]
    across[...] = own.T
    width = scores.shape[1]
    lanes = lax.broadcasted_iota(jnp.int32, (tile, VOCAB_TILE), 1)
    wanted = targets[...]
    highest = jnp.full((tile, 1), NEGATIVE, F32)
    picked = jnp.zeros((tile, 1), F32)
    for first in range(0, width, VOCAB_TILE):
        part = nn(own, table[:, first : first + VOCAB_TILE]) * scale
        if first + VOCAB_TILE > vocab:
            part = jnp.where(lanes < vocab - first, part, NEGATIVE)
        scores[:, first : first + VOCAB_TILE] = part
        highest = jnp.maximum(highest, jnp.max(part, axis=1, keepdims=True))
        picked = picked + jnp.sum(
            jnp.where(lanes == wanted - first, part, 0.0), axis=1, keepdims=True
        )
    summed = jnp.zeros((tile, 1), F32)
    for first in range(0, width, VOCAB_TILE):
        part = jnp.exp(scores[:, first : first + VOCAB_TILE] - highest)
        raised[:, first : first + VOCAB_TILE] = part.astype(BF16)
        summed = summed + jnp.sum(part, axis=1, keepdims=True)
    spot = lax.broadcasted_iota(jnp.int32, (tile, LANES), 1)
    packed = jnp.where(spot == 0, highest, jnp.where(spot == 1, summed, picked))
    stats[...] = packed.T[:8]


def exit_grads_kernel(
    table, raised, across, columns, targets, token_grad, table_grad, total, *, vocab,
):
    step = pl.program_id(0)
    tile = raised.shape[0]
    width = raised.shape[1]
    factors = jnp.concatenate(
        [columns[...], jnp.zeros((LANES - columns.shape[0], tile), F32)], axis=0
    ).T
    factor, at_target = factors[:, 0:1], factors[:, 1:2]
    wanted = targets[...]
    lanes = lax.broadcasted_iota(jnp.int32, (tile, VOCAB_TILE), 1)
    grad = jnp.zeros((tile, token_grad.shape[1]), F32)

    @pl.when(step == 0)
    def clear():
        total[...] = jnp.zeros_like(total)

    for first in range(0, width, VOCAB_TILE):
        chunk = slice(first, first + VOCAB_TILE)
        part = raised[:, chunk].astype(F32) * factor
        part = jnp.where(lanes == wanted - first, at_target, part).astype(BF16)
        grad = grad + nt(part, table[:, chunk])
        total[:, chunk] += nn(across[...], part)
    token_grad[...] = grad.astype(BF16)

    @pl.when(step == pl.num_programs(0) - 1)
    def finish():
        table_grad[...] = total[...].astype(BF16)


def mlp_backward_kernel(
    places, grad_in, stream_three, stream_two, gain, exit_gain, normed, gate, up, hidden,
    mine, other, down_mine, down_other,
    stream_grad, gains, grad_mine, grad_other, down_grad_mine, down_grad_other,
    weights, down, total, gate_low, up_low, result, down_result, sems, down_sems,
):
    rows = weights.shape[1] // (2 * mine.shape[0])
    down_rows = down.shape[1] // (2 * mine.shape[0])
    first = weight_copies(places, down_mine, down_other, down, down_rows, down_sems)
    last = weight_copies(places, mine, other, weights, rows, sems)
    for copy in first + last:
        copy.start()
    stream_back, exit_gain_grad = norm_back(stream_three[...], exit_gain[...], grad_in[...].astype(F32))
    branch = stream_back.astype(BF16)
    for copy in first + last:
        copy.wait()
    width = weights.shape[2]
    step = width // 4
    for part in range(4):
        columns = pl.ds(part * step, step)
        gate_pre = gate[:, columns]
        up_pre = up[:, columns]
        hidden_grad = nt(branch, down[0, columns, :])
        bent = jnp.tanh(MIX * (gate_pre + CUBE * (gate_pre * gate_pre * gate_pre)))
        slope = 0.5 * (1.0 + bent) + 0.5 * gate_pre * (1.0 - bent * bent) * (
            MIX * (1.0 + 3.0 * CUBE * gate_pre * gate_pre)
        )
        gate_low[:, columns] = (hidden_grad * up_pre * slope).astype(BF16)
        up_low[:, columns] = (hidden_grad * (0.5 * gate_pre * (1.0 + bent))).astype(BF16)
    normed_grad = nt(gate_low[...], weights[0]) + nt(up_low[...], weights[1])
    branch_in, gain_grad = norm_back(stream_two[...], gain[...], normed_grad)
    stream_grad[...] = stream_back + branch_in
    gains[...] = jnp.concatenate(
        [gain_grad, exit_gain_grad, jnp.zeros((6, gain_grad.shape[1]), F32)], axis=0
    )
    for matrix, low in enumerate((gate_low, up_low)):
        for part in range(4):
            columns = pl.ds(part * step, step)
            result[:, columns] = tn(normed[...], low[:, columns]).astype(BF16)
        store_blocks(places, result, matrix, rows, grad_mine, grad_other)
    for part in range(4):
        columns = pl.ds(part * step, step)
        down_result[columns, :] = tn(hidden[:, columns], branch).astype(BF16)
    store_blocks(places, down_result, 0, down_rows, down_grad_mine, down_grad_other)


def cross_backward_kernel(
    places, lengths, sources, grad_in, stream_in, gain, normed, memory,
    query, key, value, totals, attended, mine, other,
    stream_grad, gains, memory_grad, grad_mine, grad_other,
    weights, bias, result, branch, attended_grad, query_low, key_low, value_low, sems,
):
    rows = weights.shape[1] // (2 * mine.shape[0])
    copies = weight_copies(places, mine, other, weights, rows, sems)
    for copy in copies:
        copy.start()
    fill_cross_bias(bias, lengths, sources)
    branch[...] = grad_in[...].astype(BF16)
    for copy in copies:
        copy.wait()
    attended_grad[...] = nt(branch[...], weights[3]).astype(BF16)
    attend_back(
        query, key, value, bias, totals, attended_grad, query_low, key_low, value_low
    )
    normed_grad = nt(query_low[...], weights[0])
    branch_in, gain_grad = norm_back(stream_in[...], gain[...], normed_grad)
    stream_grad[...] = grad_in[...] + branch_in
    gains[...] = jnp.broadcast_to(gain_grad, gains.shape)
    memory_grad[...] = nt(key_low[...], weights[1]) + nt(value_low[...], weights[2])
    pairs = ((normed, query_low), (memory, key_low), (memory, value_low), (attended, branch))
    for matrix, (left, right) in enumerate(pairs):
        result[...] = tn(left[...], right[...]).astype(BF16)
        store_blocks(places, result, matrix, rows, grad_mine, grad_other)


def self_backward_kernel(
    places, lengths, grad_in, inputs, gain, normed,
    query, key, value, totals, attended, mine, other,
    stream_grad, gains, grad_mine, grad_other,
    weights, bias, result, branch, attended_grad, query_low, key_low, value_low, sems,
):
    rows = weights.shape[1] // (2 * mine.shape[0])
    copies = weight_copies(places, mine, other, weights, rows, sems)
    for copy in copies:
        copy.start()
    fill_self_bias(bias, lengths)
    branch[...] = grad_in[...].astype(BF16)
    for copy in copies:
        copy.wait()
    attended_grad[...] = nt(branch[...], weights[3]).astype(BF16)
    attend_back(
        query, key, value, bias, totals, attended_grad, query_low, key_low, value_low
    )
    normed_grad = (
        nt(query_low[...], weights[0])
        + nt(key_low[...], weights[1])
        + nt(value_low[...], weights[2])
    )
    branch_in, gain_grad = norm_back(inputs[...].astype(F32), gain[...], normed_grad)
    stream_grad[...] = grad_in[...] + branch_in
    gains[...] = jnp.broadcast_to(gain_grad, gains.shape)
    pairs = ((normed, query_low), (normed, key_low), (normed, value_low), (attended, branch))
    for matrix, (left, right) in enumerate(pairs):
        result[...] = tn(left[...], right[...]).astype(BF16)
        store_blocks(places, result, matrix, rows, grad_mine, grad_other)


def per_device(
    inputs,
    memory,
    targets,
    tgt_lengths,
    src_lengths,
    self_gain,
    self_query,
    self_key,
    self_value,
    self_out,
    cross_gain,
    cross_query,
    cross_key,
    cross_value,
    cross_out,
    mlp_gain,
    mlp_gate,
    mlp_up,
    mlp_down,
    exit_gain,
    embedding,
):
    tokens, model = inputs.shape
    slots = memory.shape[0]
    hidden_width = mlp_gate.shape[1]
    pair_slots = tgt_lengths.shape[1]
    wide_count = lax.axis_size("wide")
    narrow_count = lax.axis_size("narrow")
    wide = lax.axis_index("wide")
    narrow = lax.axis_index("narrow")
    half = wide_count // 2
    slot_total = tokens * wide_count * narrow_count
    scale = 1.0 / math.sqrt(model)
    places = slot_places(wide, wide_count)
    lengths, sources = tgt_lengths[0], src_lengths[0]
    shard = self_query.shape[0]
    rows = shard * narrow_count
    down_rows = mlp_down.shape[0] * narrow_count

    aligned = rows % 8 == 0
    kernel_places = places if aligned else jnp.arange(2, dtype=jnp.int32)
    kernel_count = wide_count if aligned else 2

    ids = jnp.arange(wide_count, dtype=jnp.int32)
    into_order = (places[None, :] == ids[:, None]).astype(BF16)

    def reorder(matrix, blocks):
        flat = blocks.reshape(wide_count, -1)
        return nn(matrix, flat).astype(BF16).reshape(blocks.shape)

    def collect(parts):
        across = [gather_narrow(part, narrow, narrow_count) for part in parts]
        block = jnp.concatenate([piece for pieces in across for piece in pieces], axis=0)
        mine, other = gather_wide(block, wide_count)
        if aligned:
            return mine, other
        ordered = reorder(into_order, jnp.concatenate([mine, other], axis=0))
        ordered = ordered.reshape(wide_count, len(parts), -1, block.shape[-1]).transpose(1, 0, 2, 3)
        ordered = ordered.reshape(len(parts), 2, -1, block.shape[-1]).transpose(1, 0, 2, 3)
        ordered = ordered.reshape(2, -1, block.shape[-1])
        return ordered[:1], ordered[1:]

    def spread(grad_mine, grad_other, matrices, part):
        if not aligned:
            ordered = jnp.concatenate([grad_mine, grad_other], axis=0)
            width = ordered.shape[-1]
            ordered = ordered.reshape(2, matrices, -1, width).transpose(1, 0, 2, 3)
            ordered = ordered.reshape(matrices, wide_count, -1, width).transpose(1, 0, 2, 3)
            ordered = reorder(into_order.T, ordered.reshape(wide_count, -1, width))
            grad_mine, grad_other = ordered[:half], ordered[half:]
        summed = scatter_wide(grad_mine, grad_other, wide_count)
        summed = summed.reshape(matrices, narrow_count, part, summed.shape[-1])
        return scatter_narrow(summed.transpose(1, 0, 2, 3), narrow, narrow_count)

    gain_rows = jnp.zeros((8, LANES), F32)
    for place, member in enumerate((self_gain, cross_gain, mlp_gain, exit_gain)):
        gain_rows = gain_rows.at[place, :shard].set(member.astype(F32))
    gain_across = jnp.stack(gather_narrow(gain_rows, narrow, narrow_count))
    gain_mine, gain_other = gather_wide(gain_across, wide_count)
    gain_all = jnp.concatenate([gain_mine, gain_other], axis=0)[:, :, :4, :shard]
    order = (places[None, :] == jnp.arange(wide_count)[:, None]).astype(F32)
    gain_all = jnp.sum(order[:, :, None, None, None] * gain_all[None], axis=1)
    gain_all = gain_all.transpose(2, 0, 1, 3).reshape(4, 1, model)

    self_mine, self_other = collect([self_query, self_key, self_value, self_out])
    cross_mine, cross_other = collect([cross_query, cross_key, cross_value, cross_out])
    gate_mine, gate_other = collect([mlp_gate, mlp_up])
    down_mine, down_other = collect([mlp_down])

    vocab = embedding.shape[0]
    padded = -(-vocab // VOCAB_TILE) * VOCAB_TILE
    turned = jnp.pad(embedding.T, ((0, 0), (0, padded - vocab)))
    table = lax.all_gather(turned, "narrow", axis=0, tiled=True)

    head_rows = like((HEADS, 1, tokens), F32)
    activation = like((tokens, model), BF16)
    stream_like = like((tokens, model), F32)
    matrix_sems = pltpu.SemaphoreType.DMA((kernel_count, 4))

    normed_one, query_one, key_one, value_one, attended_one, totals_one, stream_one = pl.pallas_call(
        self_forward_kernel,
        in_specs=[SMEM, SMEM, VMEM, VMEM, ANY, ANY],
        out_specs=[VMEM] * 7,
        out_shape=[activation] * 5 + [head_rows, stream_like],
        scratch_shapes=[
            pltpu.VMEM((4, model, model), BF16),
            pltpu.VMEM((tokens, tokens), F32),
            matrix_sems,
        ],
        compiler_params=PARAMS,
        name="self_forward",
    )(kernel_places, lengths, inputs, gain_all[0], self_mine, self_other)

    key_two, value_two = pl.pallas_call(
        memory_kernel,
        in_specs=[SMEM, VMEM, ANY, ANY],
        out_specs=[VMEM] * 2,
        out_shape=[like((slots, model), BF16)] * 2,
        scratch_shapes=[
            pltpu.VMEM((2, model, model), BF16),
            pltpu.SemaphoreType.DMA((kernel_count, 2)),
        ],
        compiler_params=PARAMS,
        name="memory_projection",
    )(kernel_places, memory, cross_mine, cross_other)

    normed_two, query_two, attended_two, totals_two, stream_two = pl.pallas_call(
        cross_forward_kernel,
        in_specs=[SMEM, SMEM, SMEM, VMEM, VMEM, VMEM, VMEM, ANY, ANY],
        out_specs=[VMEM] * 5,
        out_shape=[activation] * 3 + [head_rows, stream_like],
        scratch_shapes=[
            pltpu.VMEM((2, model, model), BF16),
            pltpu.VMEM((slots, tokens), F32),
            pltpu.SemaphoreType.DMA((2, kernel_count, 1)),
        ],
        compiler_params=PARAMS,
        name="cross_forward",
    )(kernel_places, lengths, sources, stream_one, gain_all[1], key_two, value_two, cross_mine, cross_other)

    wide_f32 = like((tokens, hidden_width), F32)
    wide_low = like((tokens, hidden_width), BF16)
    normed_three, gate_pre, up_pre, hidden, stream_three, activations, normed_four = pl.pallas_call(
        mlp_forward_kernel,
        in_specs=[SMEM, VMEM, VMEM, VMEM, ANY, ANY, ANY, ANY],
        out_specs=[VMEM] * 7,
        out_shape=[activation, wide_f32, wide_f32, wide_low, stream_like, activation, activation],
        scratch_shapes=[
            pltpu.VMEM((2, model, hidden_width), BF16),
            pltpu.VMEM((1, hidden_width, model), BF16),
            pltpu.SemaphoreType.DMA((kernel_count, 2)),
            pltpu.SemaphoreType.DMA((kernel_count, 1)),
        ],
        compiler_params=PARAMS,
        name="mlp_forward",
    )(kernel_places, stream_two, gain_all[2], gain_all[3], gate_mine, gate_other, down_mine, down_other)

    exit_mine, exit_other = gather_wide(normed_four, wide_count)
    group = tokens * wide_count
    tiles = group // ROW_TILE
    segment = jnp.sum(
        (jnp.arange(tokens, dtype=jnp.int32)[None, :]
         >= jnp.sum(jnp.where(jnp.arange(pair_slots)[None, :] <= jnp.arange(pair_slots)[:, None], lengths[None, :], 0), axis=1)[:, None]
         ).astype(jnp.int32),
        axis=0,
    )
    loss_weight = (segment < pair_slots).astype(F32)
    packed = jnp.concatenate(
        [loss_weight[None], targets.astype(F32)[None], jnp.zeros((6, tokens), F32)], axis=0
    )
    packed_mine, packed_other = gather_wide(packed, wide_count)
    packed_all = jnp.concatenate([packed_mine, packed_other], axis=0)[:, :2]
    packed_all = jnp.sum(order[:, :, None, None] * packed_all[None], axis=1)
    group_weight = packed_all[:, 0].reshape(group)
    group_targets = packed_all[:, 1].reshape(group).astype(jnp.int32) - wide * vocab
    group_targets = jnp.where(group_targets < vocab, group_targets, -1)
    target_column = group_targets[:, None]

    raised, tokens_across, stats = pl.pallas_call(
        functools.partial(exit_scores_kernel, vocab=vocab, scale=scale),
        grid=(tiles,),
        in_specs=[
            SMEM, ANY, ANY,
            pl.BlockSpec((ROW_TILE, 1), lambda i: (i, 0)),
            pl.BlockSpec((model, padded), lambda i: (0, 0)),
        ],
        out_specs=[
            pl.BlockSpec((ROW_TILE, padded), lambda i: (i, 0)),
            pl.BlockSpec((model, ROW_TILE), lambda i: (0, i)),
            pl.BlockSpec((8, ROW_TILE), lambda i: (0, i)),
        ],
        out_shape=[
            like((group, padded), BF16),
            like((model, group), BF16),
            like((8, group), F32),
        ],
        scratch_shapes=[
            pltpu.VMEM((group, model), BF16),
            pltpu.VMEM((ROW_TILE, padded), F32),
            pltpu.SemaphoreType.DMA((wide_count,)),
        ],
        compiler_params=PARAMS,
        name="exit_scores",
    )(places, exit_mine, exit_other, target_column, table)

    own_peak = stats[0]
    joint = stats
    for pairs in stage_pairs(wide_count) + [flip_pairs(wide_count)]:
        came = lax.ppermute(joint, "wide", pairs)
        peak = jnp.maximum(joint[0], came[0])
        summed = joint[1] * jnp.exp(joint[0] - peak) + came[1] * jnp.exp(came[0] - peak)
        joint = jnp.concatenate(
            [peak[None], summed[None], joint[2:3] + came[2:3], jnp.zeros((5, group), F32)], axis=0
        )
    log_total = joint[0] + jnp.log(joint[1])
    picked = joint[2]
    loss_part = jnp.sum(group_weight * (log_total - picked))
    loss_tile = jnp.full((8, LANES), loss_part, F32)
    loss_all = loss_tile
    for step in range(1, narrow_count):
        loss_all = loss_all + lax.ppermute(loss_tile, "narrow", narrow_pairs(narrow_count, step))
    mean_loss = loss_all[0, 0] / slot_total

    factor = jnp.exp(own_peak - log_total) * (group_weight * scale)
    at_target = (jnp.exp(picked - log_total) - 1.0) * (group_weight * scale)
    columns = jnp.concatenate(
        [factor[None], at_target[None], jnp.zeros((6, group), F32)], axis=0
    )
    token_grad, table_grad = pl.pallas_call(
        functools.partial(exit_grads_kernel, vocab=vocab),
        grid=(tiles,),
        in_specs=[
            pl.BlockSpec((model, padded), lambda i: (0, 0)),
            pl.BlockSpec((ROW_TILE, padded), lambda i: (i, 0)),
            pl.BlockSpec((model, ROW_TILE), lambda i: (0, i)),
            pl.BlockSpec((8, ROW_TILE), lambda i: (0, i)),
            pl.BlockSpec((ROW_TILE, 1), lambda i: (i, 0)),
        ],
        out_specs=[
            pl.BlockSpec((ROW_TILE, model), lambda i: (i, 0)),
            pl.BlockSpec((model, padded), lambda i: (0, 0)),
        ],
        out_shape=[like((group, model), BF16), like((model, padded), BF16)],
        scratch_shapes=[pltpu.VMEM((model, padded), F32)],
        compiler_params=PARAMS,
        name="exit_grads",
    )(table, raised, tokens_across, columns, target_column)

    table_sum = lax.psum_scatter(table_grad, "narrow", scatter_dimension=0, tiled=True)
    embedding_grad = table_sum.astype(F32).T[:vocab]

    blocks = token_grad.reshape(wide_count, tokens, model)
    relative = jnp.concatenate(
        [lax.dynamic_index_in_dim(blocks, places[slot], 0) for slot in range(wide_count)], axis=0
    )
    exit_grad = scatter_wide(relative[:half], relative[half:], wide_count)

    two_gains = like((8, model), F32)
    stream_two_grad, mlp_gains, gate_g_mine, gate_g_other, down_g_mine, down_g_other = pl.pallas_call(
        mlp_backward_kernel,
        in_specs=[SMEM] + [VMEM] * 9 + [ANY] * 4,
        out_specs=[VMEM] * 6,
        out_shape=[
            stream_like,
            two_gains,
            like(gate_mine.shape, BF16),
            like(gate_mine.shape, BF16),
            like(down_mine.shape, BF16),
            like(down_mine.shape, BF16),
        ],
        scratch_shapes=[
            pltpu.VMEM((2, model, hidden_width), BF16),
            pltpu.VMEM((1, hidden_width, model), BF16),
            pltpu.VMEM((8, LANES), F32),
            pltpu.VMEM((tokens, hidden_width), BF16),
            pltpu.VMEM((tokens, hidden_width), BF16),
            pltpu.VMEM((model, hidden_width), BF16),
            pltpu.VMEM((hidden_width, model), BF16),
            pltpu.SemaphoreType.DMA((kernel_count, 2)),
            pltpu.SemaphoreType.DMA((kernel_count, 1)),
        ],
        compiler_params=PARAMS,
        name="mlp_backward",
    )(
        kernel_places, exit_grad, stream_three, stream_two, gain_all[2], gain_all[3], normed_three,
        gate_pre, up_pre, hidden, gate_mine, gate_other, down_mine, down_other,
    )
    gate_sum = spread(gate_g_mine, gate_g_other, 2, shard)
    down_sum = spread(down_g_mine, down_g_other, 1, mlp_down.shape[0])

    low_rows = pltpu.VMEM((tokens, model), BF16)
    stream_one_grad, cross_gains, memory_grad, cross_g_mine, cross_g_other = pl.pallas_call(
        cross_backward_kernel,
        in_specs=[SMEM] * 3 + [VMEM] * 10 + [ANY] * 2,
        out_specs=[VMEM] * 5,
        out_shape=[
            stream_like,
            two_gains,
            like((slots, model), F32),
            like(cross_mine.shape, BF16),
            like(cross_mine.shape, BF16),
        ],
        scratch_shapes=[
            pltpu.VMEM((4, model, model), BF16),
            pltpu.VMEM((slots, tokens), F32),
            pltpu.VMEM((model, model), BF16),
            low_rows,
            low_rows,
            low_rows,
            pltpu.VMEM((slots, model), BF16),
            pltpu.VMEM((slots, model), BF16),
            matrix_sems,
        ],
        compiler_params=PARAMS,
        name="cross_backward",
    )(
        kernel_places, lengths, sources, stream_two_grad, stream_one, gain_all[1], normed_two, memory,
        query_two, key_two, value_two, totals_two, attended_two, cross_mine, cross_other,
    )
    cross_sum = spread(cross_g_mine, cross_g_other, 4, shard)

    inputs_grad, self_gains, self_g_mine, self_g_other = pl.pallas_call(
        self_backward_kernel,
        in_specs=[SMEM] * 2 + [VMEM] * 9 + [ANY] * 2,
        out_specs=[VMEM] * 4,
        out_shape=[
            stream_like,
            two_gains,
            like(self_mine.shape, BF16),
            like(self_mine.shape, BF16),
        ],
        scratch_shapes=[
            pltpu.VMEM((4, model, model), BF16),
            pltpu.VMEM((tokens, tokens), F32),
            pltpu.VMEM((model, model), BF16),
            low_rows,
            low_rows,
            low_rows,
            low_rows,
            low_rows,
            matrix_sems,
        ],
        compiler_params=PARAMS,
        name="self_backward",
    )(
        kernel_places, lengths, stream_one_grad, inputs, gain_all[0], normed_one,
        query_one, key_one, value_one, totals_one, attended_one, self_mine, self_other,
    )
    self_sum = spread(self_g_mine, self_g_other, 4, shard)

    gains = jnp.stack([self_gains[0], cross_gains[0], mlp_gains[0], mlp_gains[1]])
    gains = lax.psum(gains, ("wide", "narrow")).reshape(4, wide_count * narrow_count, shard)
    gains = lax.dynamic_index_in_dim(gains, wide * narrow_count + narrow, 1, keepdims=False)

    return (
        activations,
        mean_loss,
        inputs_grad,
        memory_grad,
        gains[0],
        self_sum[0],
        self_sum[1],
        self_sum[2],
        self_sum[3],
        gains[1],
        cross_sum[0],
        cross_sum[1],
        cross_sum[2],
        cross_sum[3],
        gains[2],
        gate_sum[0],
        gate_sum[1],
        down_sum[0],
        gains[3],
        embedding_grad,
    )


def solution(mesh):
    both = ("wide", "narrow")
    rows, flat = P(both, None), P(both)
    placed = (
        rows, rows, flat, rows, rows,
        flat, rows, rows, rows, rows,
        flat, rows, rows, rows, rows,
        flat, rows, rows, rows, flat,
        P("wide", "narrow"),
    )
    given = (
        rows, P(), rows, rows,
        flat, rows, rows, rows, rows,
        flat, rows, rows, rows, rows,
        flat, rows, rows, rows, flat,
        P("wide", "narrow"),
    )
    return jax.shard_map(
        per_device, mesh=mesh, in_specs=placed, out_specs=given, check_vma=False
    )
```

time: 2630 us -> 707 us (0.27)
  waiting for transfers between devices: 1860 us -> 277 us
  matrix products: 482 us -> 0 us
  Pallas kernels: 0 us -> 204 us
  starting transfers between devices: 1.25 us -> 92.5 us
  blocking collectives: 127 us -> 38.3 us
  local copies, waits for them, and re-layouts: 71.7 us -> 21.7 us
    reduce_scatter x10 -> x1, waiting for transfers between devices: 880 us -> 0.01 us  [per_device(): lax.psum_scatter(table_grad, 'narrow', scatter_dimension=0, tiled=True)]
    all_gather x14 -> x1, waiting for transfers between devices: 768 us -> 0.02 us  [per_device(): table = lax.all_gather(turned, 'narrow', axis=0, tiled=True)]
    dot_general x205 -> x0, matrix products: 482 us -> none  [the longest x85 190 us: right_matmul(): lax.dot_general(left_side, right_side, (((1,), (1,)), ((), ())), preferre...]
    ppermute x0 -> x90, waiting for transfers between devices: none -> 277 us  [the longest x14 108 us: gather_wide(): held = jnp.concatenate([held, lax.ppermute(held, 'wide', pairs)], axis=0)]
    unnamed x28 -> x2, waiting for transfers between devices: 216 us -> 0.03 us
    pallas_call x0 -> x9, Pallas kernels: none -> 204 us  [the longest x1 48 us: per_device(): pl.pallas_call(functools.partial(exit_grads_kernel, vocab=vocab), grid=(t...]
    ppermute x0 -> x90, starting transfers between devices: none -> 92.5 us  [the longest x36 53.6 us: gather_narrow(): lax.ppermute(block, 'narrow', narrow_pairs(count, step))]
    unnamed x3 -> x0, blocking collectives: 86.9 us -> none
  transfers between devices with their start and end apart: 26 -> 92, of which waited for: 22 -> 44; matrix products, arithmetic and copies ran while one was open for 21% -> 6% of each run, Pallas kernels for 0% -> 17%
where the time goes in v1:
time: 707 us; the launch traced here: 701 us
  waiting for transfers between devices  277 us (39%)
  Pallas kernels  204 us (29%)
  starting transfers between devices  92.5 us (13%)
  blocking collectives  38.3 us (5%)
  other arithmetic  34.6 us (5%)
  between operations  33.4 us (5%)
  local copies, waits for them, and re-layouts  21.7 us (3%)
    ppermute x14, waiting for transfers between devices, gather_wide(): held = jnp.concatenate([held, lax.ppermute(held, 'wide', pairs)], axis=0)  108 us
    ppermute x10, waiting for transfers between devices, scatter_wide(): sent = lax.ppermute(held[half:].astype(BF16), 'wide', pairs)  66.5 us
    ppermute x36, waiting for transfers between devices, gather_narrow(): lax.ppermute(block, 'narrow', narrow_pairs(count, step))  54.1 us
    ppermute x36, starting transfers between devices, gather_narrow(): lax.ppermute(block, 'narrow', narrow_pairs(count, step))  53.6 us
    pallas_call x1, Pallas kernels, per_device(): pl.pallas_call(functools.partial(exit_grads_kernel, vocab=vocab), grid=(t...  48 us
    pallas_call x1, Pallas kernels, per_device(): pl.pallas_call(functools.partial(exit_scores_kernel, vocab=vocab, scale=s...  38.9 us
    psum x1, blocking collectives, per_device(): lax.psum(gains, ('wide', 'narrow'))  38.3 us
    pallas_call x1, Pallas kernels, per_device(): pl.pallas_call(cross_backward_kernel, in_specs=[SMEM] * 3 + [VMEM] * 10 +...  30.7 us
  transfers between devices with their start and end apart: 92, of which 44 were waited for; matrix products, arithmetic and copies ran while one was open for 6% of the time, Pallas kernels for 17%

profile of v1, /device:TPU:0, one launch (start us, length us, event | category | flops | bytes accessed | tf_op | source)
XLA Modules:
  0.0 701.3 jit_solution(4260390560458858783)
XLA Ops:
  56.7 8.3 %collective-permute-done.31 = bf16[24,768]{1,0:T(8,128)(2,1)S(1)} collective-permute-done((bf16[24,768]{1,0:T(8,128)(2,1)S(1)}, bf16[24,768]{1,0:T(8,128)(2,1)S(1)}, u32[]{:S(2)}, u32[]{:S(2)}) %collective-permute-start.31) | collective-permute-done | bytes 36896 | tf_op jit(solution)/shard_map/ppermute | solution.py:100
  69.6 12.3 %collective-permute-done.37 = bf16[24,2048]{1,0:T(8,128)(2,1)S(1)} collective-permute-done((bf16[24,2048]{1,0:T(8,128)(2,1)S(1)}, bf16[24,2048]{1,0:T(8,128)(2,1)S(1)}, u32[]{:S(2)}, u32[]{:S(2)}) %collective-permute-start.37) | collective-permute-done | bytes 98336 | tf_op jit(solution)/shard_map/ppermute | solution.py:100
  91.7 8.4 %collective-permute-done.40 = bf16[24,2048]{1,0:T(8,128)(2,1)S(1)} collective-permute-done((bf16[24,2048]{1,0:T(8,128)(2,1)S(1)}, bf16[24,2048]{1,0:T(8,128)(2,1)S(1)}, u32[]{:S(2)}, u32[]{:S(2)}) %collective-permute-start.40) | collective-permute-done | bytes 98336 | tf_op jit(solution)/shard_map/ppermute | solution.py:100
  106.9 16.2 %collective-permute-done.42 = bf16[1,192,2048]{2,1,0:T(8,128)(2,1)S(1)} collective-permute-done((bf16[1,192,2048]{2,1,0:T(8,128)(2,1)S(1)}, bf16[1,192,2048]{2,1,0:T(8,128)(2,1)S(1)}, u32[]{:S(2)}, u32[]{:S(2)}) %collective-permute-start.42) | collective-permute-done | bytes 786464 | tf_op jit(solution)/shard_map/ppermute | solution.py:81
  124.1 11.7 %collective-permute-done.33 = bf16[1,384,768]{2,1,0:T(8,128)(2,1)S(1)} collective-permute-done((bf16[1,384,768]{2,1,0:T(8,128)(2,1)S(1)}, bf16[1,384,768]{2,1,0:T(8,128)(2,1)S(1)}, u32[]{:S(2)}, u32[]{:S(2)}) %collective-permute-start.33) | collective-permute-done | bytes 589856 | tf_op jit(solution)/shard_map/ppermute | solution.py:81
  135.9 12.5 %collective-permute-done.18 = bf16[1,384,768]{2,1,0:T(8,128)(2,1)S(1)} collective-permute-done((bf16[1,384,768]{2,1,0:T(8,128)(2,1)S(1)}, bf16[1,384,768]{2,1,0:T(8,128)(2,1)S(1)}, u32[]{:S(2)}, u32[]{:S(2)}) %collective-permute-start.18) | collective-permute-done | bytes 589856 | tf_op jit(solution)/shard_map/ppermute | solution.py:81
  152.9 10.1 %collective-permute-done.48 = bf16[1,256,768]{2,1,0:T(8,128)(2,1)S(1)} collective-permute-done((bf16[1,256,768]{2,1,0:T(8,128)(2,1)S(1)}, bf16[1,256,768]{2,1,0:T(8,128)(2,1)S(1)}, u32[]{:S(2)}, u32[]{:S(2)}) %collective-permute-start.48) | collective-permute-done | bytes 393248 | tf_op jit(solution)/shard_map/ppermute | solution.py:81
  165.0 12.3 %collective-permute-done.19 = bf16[2,384,768]{2,1,0:T(8,128)(2,1)S(1)} collective-permute-done((bf16[2,384,768]{2,1,0:T(8,128)(2,1)S(1)}, bf16[2,384,768]{2,1,0:T(8,128)(2,1)S(1)}, u32[]{:S(2)}, u32[]{:S(2)}) %collective-permute-start.19) | collective-permute-done | bytes 1179680 | tf_op jit(solution)/shard_map/ppermute | solution.py:81
  221.3 11.8 %self_forward.1 = (bf16[320,768]{1,0:T(8,128)(2,1)}, bf16[320,768]{1,0:T(8,128)(2,1)}, bf16[320,768]{1,0:T(8,128)(2,1)}, bf16[320,768]{1,0:T(8,128)(2,1)}, bf16[...) custom-call(s32[8]{0:T(128)} %copy-done.6, s32[2]{0:T(128)} %bitcast.364, bf16[320,768]{1,0:T(8,128)(2,1)} %inputs.3, ...), custom_call_target="tpu_custom_call" | custom-call | tf_op jit(solution)/shard_map/self_forward/pallas_call | solution.py:638
  233.1 16.9 %cross_forward.1 = (bf16[320,768]{1,0:T(8,128)(2,1)}, bf16[320,768]{1,0:T(8,128)(2,1)}, bf16[320,768]{1,0:T(8,128)(2,1)}, f32[12,1,320]{2,1,0:T(1,128)}, f32[320,768]{1,0:T(8,128)}) custom-call(s32[8]{0:T(128)} %copy-done.6, s32[2]{0:T(128)} %bitcast.365, s32[2]{0:T(128)} %bitcast.372, f32[320,768]{1,0:T(8,128)} %get-tuple-element.109.stream_in, ...), custom_call_target="tpu_custom_call" | custom-call | tf_op jit(solution)/shard_map/cross_forward/pallas_call | solution.py:665
  250.1 11.2 %mlp_forward.1 = (bf16[320,768]{1,0:T(8,128)(2,1)}, f32[320,2048]{1,0:T(8,128)}, f32[320,2048]{1,0:T(8,128)}, bf16[320,2048]{1,0:T(8,128)(2,1)}, f32[320,768]{1,...) custom-call(s32[8]{0:T(128)} %copy-done.6, f32[320,768]{1,0:T(8,128)} %get-tuple-element.112.stream_in.stream_two, ...), custom_call_target="tpu_custom_call" | custom-call | tf_op jit(solution)/shard_map/mlp_forward/pallas_call | solution.py:681
  261.3 9.0 %collective-permute-done.54 = bf16[1,320,768]{2,1,0:T(8,128)(2,1)S(1)} collective-permute-done((bf16[1,320,768]{2,1,0:T(8,128)(2,1)}, bf16[1,320,768]{2,1,0:T(8,128)(2,1)S(1)}, u32[]{:S(2)}, u32[]{:S(2)}) %collective-permute-start.54) | collective-permute-done | bytes 491552 | tf_op jit(solution)/shard_map/ppermute | solution.py:81
  271.6 14.1 %collective-permute-done.55 = bf16[2,320,768]{2,1,0:T(8,128)(2,1)S(1)} collective-permute-done((bf16[2,320,768]{2,1,0:T(8,128)(2,1)S(1)}, bf16[2,320,768]{2,1,0:T(8,128)(2,1)S(1)}, u32[]{:S(2)}, u32[]{:S(2)}) %collective-permute-start.55) | collective-permute-done | bytes 983072 | tf_op jit(solution)/shard_map/ppermute | solution.py:81
  298.0 38.9 %exit_scores.1 = (bf16[2560,4096]{1,0:T(8,128)(2,1)}, bf16[768,2560]{1,0:T(8,128)(2,1)}, f32[8,2560]{1,0:T(8,128)}) custom-call(s32[8]{0:T(128)} %copy-done.6, bf16[4,320,768]{2,1,0:T(8,128)(2,1)} %copy-done.1, bf16[4,320,768]{2,1,0:T(8,128)(2,1)} %collective-permute-done.56.other, s32[2560,1]{1,0:T(8,128)} %compare_select_fusion.targets, ...), custom_call_target="tpu_custom_call" | custom-call | tf_op jit(solution)/shard_map/exit_scores/pallas_call | solution.py:717
  363.0 48.0 %exit_grads.1 = (bf16[2560,768]{1,0:T(8,128)(2,1)}, bf16[768,4096]{1,0:T(8,128)(2,1)}) custom-call(bf16[768,4096]{1,0:T(8,128)(2,1)} %all-gather.2.cloned.1.call-done.table, bf16[2560,4096]{1,0:T(8,128)(2,1)} %get-tuple-element.116.raised, bf16[768,2560]{1,0:T(8,128)(2,1)} %get-tuple-element.117.across, f32[8,2560]{1,0:T(8,128)} %maximum_maximum_fusion.2.columns, ...), custom_call_target="tpu_custom_call" | custom-call | tf_op jit(solution)/shard_map/exit_grads/pallas_call | solution.py:767
  423.4 12.2 %collective-permute-done.64 = bf16[2,320,768]{2,1,0:T(8,128)(2,1)S(1)} collective-permute-done((bf16[2,320,768]{2,1,0:T(8,128)(2,1)S(1)}, bf16[2,320,768]{2,1,0:T(8,128)(2,1)S(1)}, u32[]{:S(2)}, u32[]{:S(2)}) %collective-permute-start.64) | collective-permute-done | bytes 983072 | tf_op jit(solution)/shard_map/ppermute | solution.py:89
  436.0 8.8 %collective-permute-done.65 = bf16[1,320,768]{2,1,0:T(8,128)(2,1)S(1)} collective-permute-done((bf16[1,320,768]{2,1,0:T(8,128)(2,1)S(1)}, bf16[1,320,768]{2,1,0:T(8,128)(2,1)S(1)}, u32[]{:S(2)}, u32[]{:S(2)}) %collective-permute-start.65) | collective-permute-done | bytes 491552 | tf_op jit(solution)/shard_map/ppermute | solution.py:89
  445.9 21.3 %mlp_backward.1 = (f32[320,768]{1,0:T(8,128)}, f32[8,768]{1,0:T(8,128)}, bf16[4,192,2048]{2,1,0:T(8,128)(2,1)}, bf16[4,192,2048]{2,1,0:T(8,128)(2,1)}, bf16[4,25...) custom-call(s32[8]{0:T(128)} %copy-done.6, f32[320,768]{1,0:T(8,128)} %fusion.grad_in, ...), custom_call_target="tpu_custom_call" | custom-call | tf_op jit(solution)/shard_map/mlp_backward/pallas_call | solution.py:797
  467.2 30.7 %cross_backward.1 = (f32[320,768]{1,0:T(8,128)}, f32[8,768]{1,0:T(8,128)}, f32[1024,768]{1,0:T(8,128)}, bf16[4,384,768]{2,1,0:T(8,128)(2,1)}, bf16[4,384,768]{2,1,0:T(8,128)(2,1)}) custom-call(s32[8]{0:T(128)} %copy-done.6, s32[2]{0:T(128)} %bitcast.366, s32[2]{0:T(128)} %bitcast.373, f32[320,768]{1,0:T(8,128)} %get-tuple-element.124.grad_in, ...), custom_call_target="tpu_custom_call" | custom-call | tf_op jit(solution)/shard_map/cross_backward/pallas_call | solution.py:830
  498.4 18.2 %self_backward.1 = (f32[320,768]{1,0:T(8,128)}, f32[8,768]{1,0:T(8,128)}, bf16[4,384,768]{2,1,0:T(8,128)(2,1)}, bf16[4,384,768]{2,1,0:T(8,128)(2,1)}) custom-call(s32[8]{0:T(128)} %copy-done.6, s32[2]{0:T(128)} %bitcast.367, f32[320,768]{1,0:T(8,128)} %get-tuple-element.129.grad_in, bf16[320,768]{1,0:T(8,128)(2,1)} %inputs.3, f32[1,768]{1,0:T(1,128)} %squeeze.298.gain, ...), custom_call_target="tpu_custom_call" | custom-call | tf_op jit(solution)/shard_map/self_backward/pallas_call | solution.py:860
  537.0 38.3 %psum.7 = f32[4,32,24]{2,1,0:T(8,128)S(1)} all-reduce(f32[4,32,24]{2,1,0:T(8,128)S(1)} %reshape.519), channel_id=1, replica_groups=mesh['wide'=8,'narrow'=4] {'wide','narrow'}, use_global_device_ids=true, to_apply=%region_5.6 | all-reduce | flops 3072 | bytes 24576 | tf_op jit(solution)/shard_map/psum | solution.py:890
  596.1 11.3 %collective-permute-done.73 = bf16[2,384,768]{2,1,0:T(8,128)(2,1)S(1)} collective-permute-done((bf16[2,384,768]{2,1,0:T(8,128)(2,1)S(1)}, bf16[2,384,768]{2,1,0:T(8,128)(2,1)S(1)}, u32[]{:S(2)}, u32[]{:S(2)}) %collective-permute-start.73) | collective-permute-done | bytes 1179680 | tf_op jit(solution)/shard_map/ppermute | solution.py:89
  609.8 16.6 %collective-permute-done.67 = bf16[2,384,768]{2,1,0:T(8,128)(2,1)S(1)} collective-permute-done((bf16[2,384,768]{2,1,0:T(8,128)(2,1)S(1)}, bf16[2,384,768]{2,1,0:T(8,128)(2,1)S(1)}, u32[]{:S(2)}, u32[]{:S(2)}) %collective-permute-start.67) | collective-permute-done | bytes 1179680 | tf_op jit(solution)/shard_map/ppermute | solution.py:89
  633.5 9.5 %collective-permute-done.68 = bf16[1,384,768]{2,1,0:T(8,128)(2,1)S(1)} collective-permute-done((bf16[1,384,768]{2,1,0:T(8,128)(2,1)S(1)}, bf16[1,384,768]{2,1,0:T(8,128)(2,1)S(1)}, u32[]{:S(2)}, u32[]{:S(2)}) %collective-permute-start.68) | collective-permute-done | bytes 589856 | tf_op jit(solution)/shard_map/ppermute | solution.py:89
  (401 shorter events, 259.4 us)
Async XLA Ops:
  7.2 290.8 %all-gather.2.cloned.1.call-start = ((), (), s32[]{:S(2)}) async-start(), calls=%async_computation.1 | async-start | bytes 7864320 | tf_op jit(solution)/shard_map/all_gather | solution.py:631
  19.6 669.9 %reduce-scatter.2.cloned.1.call-start = ((), (), s32[]{:S(2)}) async-start(), calls=%async_computation.2 | async-start | bytes 7864320 | tf_op jit(solution)/shard_map/reduce_scatter | solution.py:787
  20.3 83.5 %collective-permute-start.14 = (bf16[24,768]{1,0:T(8,128)(2,1)S(1)}, bf16[24,768]{1,0:T(8,128)(2,1)S(1)}, u32[]{:S(2)}, u32[]{:S(2)}) collective-permute-start(bf16[24,768]{1,0:T(8,128)(2,1)S(1)} %copy-done.18), channel_id=1, source_target_pairs={{0,3},{1,2},{2,1},{3,0},{4,7},{5,6},{6,5},{7,4},{8,11},{9,10},{10,... | collective-permute-start | bytes 110600 | tf_op jit(solution)/shard_map/ppermute | solution.py:100
  24.1 79.8 %collective-permute-start.13 = (bf16[24,768]{1,0:T(8,128)(2,1)S(1)}, bf16[24,768]{1,0:T(8,128)(2,1)S(1)}, u32[]{:S(2)}, u32[]{:S(2)}) collective-permute-start(bf16[24,768]{1,0:T(8,128)(2,1)S(1)} %copy-done.18), channel_id=1, source_target_pairs={{0,2},{1,3},{2,0},{3,1},{4,6},{5,7},{6,4},{7,5},{8,10},{9,11},{10,... | collective-permute-start | bytes 110600 | tf_op jit(solution)/shard_map/ppermute | solution.py:100
  104.8 31.0 %collective-permute-start.33 = (bf16[1,384,768]{2,1,0:T(8,128)(2,1)S(1)}, bf16[1,384,768]{2,1,0:T(8,128)(2,1)S(1)}, u32[]{:S(2)}, u32[]{:S(2)}) collective-permute-start(bf16[1,384,768]{2,1,0:T(8,128)(2,1)S(1)} %bitcast.308), channel_id=1, source_target_pairs={{0,8},{4,20},{8,0},{12,28},{16,24},{20,4},{24,16},{28,12},{1,9},{5... | collective-permute-start | bytes 1769480 | tf_op jit(solution)/shard_map/ppermute | solution.py:81
  123.3 27.6 %collective-permute-start.43 = (bf16[2,192,2048]{2,1,0:T(8,128)(2,1)S(1)}, bf16[2,192,2048]{2,1,0:T(8,128)(2,1)S(1)}, u32[]{:S(2)}, u32[]{:S(2)}) collective-permute-start(bf16[2,192,2048]{2,1,0:T(8,128)(2,1)S(1)} %pad_maximum_fusion.5), channel_id=1, source_target_pairs={{0,16},{4,12},{8,24},{12,4},{16,0},{20,28},{24,8},{28,20},{1,17},{... | collective-permute-start | bytes 4718600 | tf_op jit(solution)/shard_map/ppermute | solution.py:81
  123.5 24.9 %collective-permute-start.18 = (bf16[1,384,768]{2,1,0:T(8,128)(2,1)S(1)}, bf16[1,384,768]{2,1,0:T(8,128)(2,1)S(1)}, u32[]{:S(2)}, u32[]{:S(2)}) collective-permute-start(bf16[1,384,768]{2,1,0:T(8,128)(2,1)S(1)} %bitcast.305), channel_id=1, source_target_pairs={{0,8},{4,20},{8,0},{12,28},{16,24},{20,4},{24,16},{28,12},{1,9},{5... | collective-permute-start | bytes 1769480 | tf_op jit(solution)/shard_map/ppermute | solution.py:81
  123.6 24.9 %collective-permute-start.47 = (bf16[64,768]{1,0:T(8,128)(2,1)S(1)}, bf16[64,768]{1,0:T(8,128)(2,1)S(1)}, u32[]{:S(2)}, u32[]{:S(2)}) collective-permute-start(bf16[64,768]{1,0:T(8,128)(2,1)S(1)} %copy-done.10), channel_id=1, source_target_pairs={{0,3},{1,2},{2,1},{3,0},{4,7},{5,6},{6,5},{7,4},{8,11},{9,10},{10,... | collective-permute-start | bytes 294920 | tf_op jit(solution)/shard_map/ppermute | solution.py:100
  124.1 26.5 %collective-permute-start.46 = (bf16[64,768]{1,0:T(8,128)(2,1)S(1)}, bf16[64,768]{1,0:T(8,128)(2,1)S(1)}, u32[]{:S(2)}, u32[]{:S(2)}) collective-permute-start(bf16[64,768]{1,0:T(8,128)(2,1)S(1)} %copy-done.10), channel_id=1, source_target_pairs={{0,2},{1,3},{2,0},{3,1},{4,6},{5,7},{6,4},{7,5},{8,10},{9,11},{10,... | collective-permute-start | bytes 294920 | tf_op jit(solution)/shard_map/ppermute | solution.py:100
  148.6 28.7 %collective-permute-start.19 = (bf16[2,384,768]{2,1,0:T(8,128)(2,1)S(1)}, bf16[2,384,768]{2,1,0:T(8,128)(2,1)S(1)}, u32[]{:S(2)}, u32[]{:S(2)}) collective-permute-start(bf16[2,384,768]{2,1,0:T(8,128)(2,1)S(1)} %pad_maximum_fusion.7), channel_id=1, source_target_pairs={{0,16},{4,12},{8,24},{12,4},{16,0},{20,28},{24,8},{28,20},{1,17},{... | collective-permute-start | bytes 3538952 | tf_op jit(solution)/shard_map/ppermute | solution.py:81
  152.9 97.2 %collective-permute-start.44 = (bf16[4,192,2048]{2,1,0:T(8,128)(2,1)}, bf16[4,192,2048]{2,1,0:T(8,128)(2,1)}, u32[]{:S(2)}, u32[]{:S(2)}) collective-permute-start(bf16[4,192,2048]{2,1,0:T(8,128)(2,1)} %pad_maximum_fusion.mine), channel_id=1, source_target_pairs={{0,4},{4,0},{8,12},{12,8},{16,20},{20,16},{24,28},{28,24},{1,5},{5... | collective-permute-start | bytes 9437192 | tf_op jit(solution)/shard_map/ppermute | solution.py:82
  164.9 49.3 %collective-permute-start.35 = (bf16[4,384,768]{2,1,0:T(8,128)(2,1)S(1)}, bf16[4,384,768]{2,1,0:T(8,128)(2,1)}, u32[]{:S(2)}, u32[]{:S(2)}) collective-permute-start(bf16[4,384,768]{2,1,0:T(8,128)(2,1)S(1)} %pad_maximum_fusion.2.mine), channel_id=1, source_target_pairs={{0,4},{4,0},{8,12},{12,8},{16,20},{20,16},{24,28},{28,24},{1,5},{5... | collective-permute-start | bytes 7077896 | tf_op jit(solution)/shard_map/ppermute | solution.py:82
  178.9 42.4 %collective-permute-start.20 = (bf16[4,384,768]{2,1,0:T(8,128)(2,1)}, bf16[4,384,768]{2,1,0:T(8,128)(2,1)}, u32[]{:S(2)}, u32[]{:S(2)}) collective-permute-start(bf16[4,384,768]{2,1,0:T(8,128)(2,1)} %pad_maximum_fusion.1.mine), channel_id=1, source_target_pairs={{0,4},{4,0},{8,12},{12,8},{16,20},{20,16},{24,28},{28,24},{1,5},{5... | collective-permute-start | bytes 7077896 | tf_op jit(solution)/shard_map/ppermute | solution.py:82
  188.2 61.8 %collective-permute-start.50 = (bf16[4,256,768]{2,1,0:T(8,128)(2,1)}, bf16[4,256,768]{2,1,0:T(8,128)(2,1)}, u32[]{:S(2)}, u32[]{:S(2)}) collective-permute-start(bf16[4,256,768]{2,1,0:T(8,128)(2,1)} %pad_maximum_fusion.6.down_mine), channel_id=1, source_target_pairs={{0,4},{4,0},{8,12},{12,8},{16,20},{20,16},{24,28},{28,24},{1,5},{5... | collective-permute-start | bytes 4718600 | tf_op jit(solution)/shard_map/ppermute | solution.py:82
  497.8 82.8 %collective-permute-start.72 = (bf16[4,384,768]{2,1,0:T(8,128)(2,1)}, bf16[4,384,768]{2,1,0:T(8,128)(2,1)}, u32[]{:S(2)}, u32[]{:S(2)}) collective-permute-start(bf16[4,384,768]{2,1,0:T(8,128)(2,1)} %get-tuple-element.144), channel_id=1, source_target_pairs={{0,4},{4,0},{8,12},{12,8},{16,20},{20,16},{24,28},{28,24},{1,5},{5... | collective-permute-start | bytes 7077896 | tf_op jit(solution)/shard_map/ppermute | solution.py:86
  497.9 77.9 %collective-permute-start.84 = (bf16[4,256,768]{2,1,0:T(8,128)(2,1)}, bf16[4,256,768]{2,1,0:T(8,128)(2,1)}, u32[]{:S(2)}, u32[]{:S(2)}) collective-permute-start(bf16[4,256,768]{2,1,0:T(8,128)(2,1)} %get-tuple-element.148), channel_id=1, source_target_pairs={{0,4},{4,0},{8,12},{12,8},{16,20},{20,16},{24,28},{28,24},{1,5},{5... | collective-permute-start | bytes 4718600 | tf_op jit(solution)/shard_map/ppermute | solution.py:86
  516.7 66.4 %collective-permute-start.66 = (bf16[4,384,768]{2,1,0:T(8,128)(2,1)}, bf16[4,384,768]{2,1,0:T(8,128)(2,1)}, u32[]{:S(2)}, u32[]{:S(2)}) collective-permute-start(bf16[4,384,768]{2,1,0:T(8,128)(2,1)} %get-tuple-element.142), channel_id=1, source_target_pairs={{0,4},{4,0},{8,12},{12,8},{16,20},{20,16},{24,28},{28,24},{1,5},{5... | collective-permute-start | bytes 7077896 | tf_op jit(solution)/shard_map/ppermute | solution.py:86
  516.8 76.1 %collective-permute-start.78 = (bf16[4,192,2048]{2,1,0:T(8,128)(2,1)}, bf16[4,192,2048]{2,1,0:T(8,128)(2,1)S(1)}, u32[]{:S(2)}, u32[]{:S(2)}) collective-permute-start(bf16[4,192,2048]{2,1,0:T(8,128)(2,1)} %get-tuple-element.146), channel_id=1, source_target_pairs={{0,4},{4,0},{8,12},{12,8},{16,20},{20,16},{24,28},{28,24},{1,5},{5... | collective-permute-start | bytes 9437192 | tf_op jit(solution)/shard_map/ppermute | solution.py:86
  582.9 24.5 %collective-permute-start.73 = (bf16[2,384,768]{2,1,0:T(8,128)(2,1)S(1)}, bf16[2,384,768]{2,1,0:T(8,128)(2,1)S(1)}, u32[]{:S(2)}, u32[]{:S(2)}) collective-permute-start(bf16[2,384,768]{2,1,0:T(8,128)(2,1)S(1)} %slice.496), channel_id=1, source_target_pairs={{0,16},{4,12},{8,24},{12,4},{16,0},{20,28},{24,8},{28,20},{1,17},{... | collective-permute-start | bytes 3538952 | tf_op jit(solution)/shard_map/ppermute | solution.py:89
  586.7 39.7 %collective-permute-start.67 = (bf16[2,384,768]{2,1,0:T(8,128)(2,1)S(1)}, bf16[2,384,768]{2,1,0:T(8,128)(2,1)S(1)}, u32[]{:S(2)}, u32[]{:S(2)}) collective-permute-start(bf16[2,384,768]{2,1,0:T(8,128)(2,1)S(1)} %slice.497), channel_id=1, source_target_pairs={{0,16},{4,12},{8,24},{12,4},{16,0},{20,28},{24,8},{28,20},{1,17},{... | collective-permute-start | bytes 3538952 | tf_op jit(solution)/shard_map/ppermute | solution.py:89
  590.9 37.9 %collective-permute-start.86 = (bf16[1,256,768]{2,1,0:T(8,128)(2,1)S(1)}, bf16[1,256,768]{2,1,0:T(8,128)(2,1)S(1)}, u32[]{:S(2)}, u32[]{:S(2)}) collective-permute-start(bf16[1,256,768]{2,1,0:T(8,128)(2,1)S(1)} %slice.504), channel_id=1, source_target_pairs={{0,8},{4,20},{8,0},{12,28},{16,24},{20,4},{24,16},{28,12},{1,9},{5... | collective-permute-start | bytes 1179656 | tf_op jit(solution)/shard_map/ppermute | solution.py:89
  594.4 55.2 %collective-permute-start.79 = (bf16[2,192,2048]{2,1,0:T(8,128)(2,1)S(1)}, bf16[2,192,2048]{2,1,0:T(8,128)(2,1)S(1)}, u32[]{:S(2)}, u32[]{:S(2)}) collective-permute-start(bf16[2,192,2048]{2,1,0:T(8,128)(2,1)S(1)} %slice.495), channel_id=1, source_target_pairs={{0,16},{4,12},{8,24},{12,4},{16,0},{20,28},{24,8},{28,20},{1,17},{... | collective-permute-start | bytes 4718600 | tf_op jit(solution)/shard_map/ppermute | solution.py:89
  607.7 24.7 %collective-permute-start.74 = (bf16[1,384,768]{2,1,0:T(8,128)(2,1)S(1)}, bf16[1,384,768]{2,1,0:T(8,128)(2,1)S(1)}, u32[]{:S(2)}, u32[]{:S(2)}) collective-permute-start(bf16[1,384,768]{2,1,0:T(8,128)(2,1)S(1)} %slice.501), channel_id=1, source_target_pairs={{0,8},{4,20},{8,0},{12,28},{16,24},{20,4},{24,16},{28,12},{1,9},{5... | collective-permute-start | bytes 1769480 | tf_op jit(solution)/shard_map/ppermute | solution.py:89
  630.6 23.9 %collective-permute-start.88 = (bf16[1,64,768]{2,1,0:T(8,128)(2,1)S(1)}, bf16[1,64,768]{2,1,0:T(8,128)(2,1)S(1)}, u32[]{:S(2)}, u32[]{:S(2)}) collective-permute-start(bf16[1,64,768]{2,1,0:T(8,128)(2,1)S(1)} %get-tuple-element.188), channel_id=1, source_target_pairs={{0,2},{1,3},{2,0},{3,1},{4,6},{5,7},{6,4},{7,5},{8,10},{9,11},{10,... | collective-permute-start | bytes 294920 | tf_op jit(solution)/shard_map/ppermute | solution.py:113
  (96 other events, 1285.2 us)
Sparse Core Ops, SparseCore 0:
  19.7 151.1 all-gather.1
  414.8 108.5 reduce-scatter.1

commit v2 on v1

v2 whole, which is shorter than its diff:
```python
import functools
import math

import jax
import jax.numpy as jnp
from jax import lax
from jax.experimental import pallas as pl
from jax.experimental.pallas import tpu as pltpu
from jax.sharding import PartitionSpec as P

HEADS = 12
EPSILON = 1e-06
NEGATIVE = -1e30
F32 = jnp.float32
BF16 = jnp.bfloat16
LANES = 128
ROW_TILE = 256
GRAD_TILE = 256
VOCAB_TILE = 512
MIX = math.sqrt(2.0 / math.pi)
CUBE = 0.044715
LOG2E = math.log2(math.e)
META_WIDE, META_TILES, META_LISTS = 0, 1, 2

VMEM = pl.BlockSpec(memory_space=pltpu.VMEM)
SMEM = pl.BlockSpec(memory_space=pltpu.SMEM)
ANY = pl.BlockSpec(memory_space=pl.ANY)
PARAMS = pltpu.CompilerParams(vmem_limit_bytes=60 * 2**20)


def work(gigaflops):
    return pl.CostEstimate(flops=gigaflops * 10**9, bytes_accessed=10**6, transcendentals=0)


def nn(left, right):
    return lax.dot_general(left, right, (((1,), (0,)), ((), ())), preferred_element_type=F32)


def nt(left, right):
    return lax.dot_general(left, right, (((1,), (1,)), ((), ())), preferred_element_type=F32)


def tn(left, right):
    return lax.dot_general(left, right, (((0,), (0,)), ((), ())), preferred_element_type=F32)


def like(shape, kind):
    return jax.ShapeDtypeStruct(shape, kind)


def stage_masks(count):
    up = [1 << bit for bit in range(1, count.bit_length() - 1)]
    return up, up[::-1]


def stage_pairs(count):
    even, odd = stage_masks(count)
    return [[(v, v ^ (odd if v % 2 else even)[i]) for v in range(count)] for i in range(len(even))]


def flip_pairs(count):
    return [(v, v ^ 1) for v in range(count)]


def slot_tables(count):
    tables = []
    for masks in stage_masks(count):
        slots = [0]
        for mask in masks:
            slots = slots + [slot ^ mask for slot in slots]
        tables.append(slots)
    even, odd = tables
    return (
        even + [1 ^ slot for slot in odd],
        odd + [1 ^ slot for slot in even],
    )


def slot_places(wide, count):
    even, odd = slot_tables(count)
    table = jnp.where(wide % 2 == 0, jnp.array(even, jnp.int32), jnp.array(odd, jnp.int32))
    return wide ^ table


def tie(value, *others):
    return lax.optimization_barrier((value, *others))[0]


def cross_core(value, count):
    return lax.ppermute(value, "wide", flip_pairs(count))


def gather_wide(block, count):
    held = block[None]
    *early, last = stage_pairs(count)
    for pairs in early:
        held = jnp.concatenate([held, lax.ppermute(held, "wide", pairs)], axis=0)
    came = lax.ppermute(held, "wide", last)
    return held, came, cross_core(held, count), cross_core(came, count)


def scatter_core(parts, count):
    sent, kept = cross_core(parts[3], count), cross_core(parts[2], count)
    return (parts[1], sent), (parts[0], kept)


def scatter_far(sent, kept, count):
    far = (sent[0].astype(F32) + sent[1].astype(F32)).astype(BF16)
    came = lax.ppermute(far, "wide", stage_pairs(count)[-1])
    return far, came, kept


def scatter_near(came, kept, count):
    held = kept[0].astype(F32) + kept[1].astype(F32) + came.astype(F32)
    *rest, last = stage_pairs(count)[-2::-1]
    for pairs in rest:
        half = held.shape[0] // 2
        sent = lax.ppermute(held[half:].astype(BF16), "wide", pairs)
        held = held[:half] + sent.astype(F32)
    far = held[1].astype(BF16)
    return far, lax.ppermute(far, "wide", last), held[0]


def scatter_wide(parts, count):
    far, came, kept = scatter_far(*scatter_core(parts, count), count)
    far, came, held = scatter_near(came, kept, count)
    return held + came.astype(F32)


def narrow_pairs(count, step):
    return [(v, v ^ step) for v in range(count)]


def gather_narrow(block, count):
    return [block] + [
        lax.ppermute(block, "narrow", narrow_pairs(count, step)) for step in range(1, count)
    ]


def pick(values, place, axis=0):
    return lax.dynamic_index_in_dim(values, place.astype(jnp.uint32), axis, keepdims=False)


def in_line_order(pieces, narrow):
    stacked = jnp.stack(pieces)
    return [pick(stacked, narrow ^ place) for place in range(stacked.shape[0])]


def scatter_narrow(blocks, narrow, count):
    total = pick(blocks, narrow)
    for step in range(1, count):
        sent = pick(blocks, narrow ^ step).astype(BF16)
        total = total + lax.ppermute(sent, "narrow", narrow_pairs(count, step)).astype(F32)
    return total


def weight_copies(places, parts, start, target, rows, sems):
    size = parts[0].shape[0]
    copies = []
    for slot in range(len(parts) * size):
        place = pl.multiple_of(places[slot] * rows, 8)
        for matrix in range(target.shape[0]):
            copies.append(
                pltpu.make_async_copy(
                    parts[slot // size].at[slot % size, pl.ds(start + matrix * rows, rows), :],
                    target.at[matrix, pl.ds(place, rows), :],
                    sems.at[slot, matrix],
                )
            )
    return copies


def store_blocks(places, value_ref, start, rows, parts):
    size = parts[0].shape[0]
    for slot in range(len(parts) * size):
        place = pl.multiple_of(places[slot] * rows, 8)
        parts[slot // size][slot % size, pl.ds(start, rows), :] = value_ref[pl.ds(place, rows), :]


def norm_scale(values):
    return lax.rsqrt(jnp.mean(values * values, axis=-1, keepdims=True) + EPSILON)


def norm_back(values, gain, grad):
    root = norm_scale(values)
    scaled = gain * grad
    gain_grad = jnp.sum(grad * values * root, axis=0, keepdims=True)
    inner = jnp.mean(scaled * values, axis=-1, keepdims=True)
    return root * scaled - values * (root * root * root) * inner, gain_grad


def query_segments(lengths, count):
    places = lax.broadcasted_iota(jnp.int32, (1, count), 1)
    segment = jnp.zeros((1, count), jnp.int32)
    edge = jnp.int32(0)
    for pair in range(lengths.shape[0]):
        edge = edge + lengths[pair]
        segment = segment + (places >= edge).astype(jnp.int32)
    return places, segment


def fill_self_bias(bias, lengths):
    count = bias.shape[1]
    places, segment = query_segments(lengths, count)
    low = jnp.zeros((1, count), jnp.int32)
    edge = jnp.int32(0)
    for pair in range(lengths.shape[0]):
        edge = edge + lengths[pair]
        low = jnp.where(segment == pair + 1, edge, low)
    keys = lax.broadcasted_iota(jnp.int32, bias.shape, 0)
    bias[...] = jnp.where((keys >= low) & (keys <= places), 0.0, NEGATIVE)


def fill_cross_bias(bias, lengths, sources):
    count = bias.shape[1]
    places, segment = query_segments(lengths, count)
    low = jnp.zeros((1, count), jnp.int32)
    high = jnp.full((1, count), bias.shape[0], jnp.int32)
    edge = jnp.int32(0)
    for pair in range(lengths.shape[0]):
        low = jnp.where(segment == pair, edge, low)
        edge = edge + sources[pair]
        high = jnp.where(segment == pair, edge, high)
    keys = lax.broadcasted_iota(jnp.int32, bias.shape, 0)
    bias[...] = jnp.where((keys >= low) & (keys < high), 0.0, NEGATIVE)


def first_half(width):
    return lax.broadcasted_iota(jnp.int32, (1, width), 1) < width // 2


def attend(queries, keys, values, bias, outputs, totals):
    width = 2 * (queries.shape[1] // HEADS)
    chosen = first_half(width)

    def pair_of_heads(pair, carry):
        columns = pl.ds(pl.multiple_of(pair * width, width), width)
        query = queries[:, columns]
        key = keys[:, columns]
        value = values[:, columns].T
        halves = []
        for side in range(2):
            own = jnp.where(chosen if side == 0 else ~chosen, query, 0)
            scores = nt(key, own) + bias[...]
            highest = jnp.max(scores, axis=0, keepdims=True)
            raised = jnp.exp(scores - highest)
            summed = jnp.sum(raised, axis=0, keepdims=True)
            weights = (raised * (1.0 / summed)).astype(BF16)
            totals[2 * pair + side] = highest + jnp.log(summed)
            halves.append(nn(value[side * width // 2 : (side + 1) * width // 2], weights))
        outputs[:, columns] = jnp.concatenate(halves, axis=0).T.astype(BF16)
        return carry

    lax.fori_loop(0, HEADS // 2, pair_of_heads, 0)


def attend_back(queries, keys, values, bias, totals, grads, query_low, key_low, value_low):
    width = 2 * (queries.shape[1] // HEADS)
    chosen = first_half(width)

    def pair_of_heads(pair, carry):
        columns = pl.ds(pl.multiple_of(pair * width, width), width)
        query = queries[:, columns]
        key = keys[:, columns]
        value = values[:, columns]
        grad = grads[:, columns]
        key_across = key.T
        query_parts, key_parts, value_parts = [], [], []
        for side in range(2):
            mine = chosen if side == 0 else ~chosen
            scores = nt(key, jnp.where(mine, query, 0)) + bias[...]
            probs = jnp.exp(scores - totals[2 * pair + side])
            prob_grad = nt(value, jnp.where(mine, grad, 0))
            value_parts.append(nn(probs.astype(BF16), grad))
            weighted = probs * prob_grad
            centre = jnp.sum(weighted, axis=0, keepdims=True)
            score_grad = (weighted - probs * centre).astype(BF16)
            key_parts.append(nn(score_grad, query))
            query_parts.append(
                nn(key_across[side * width // 2 : (side + 1) * width // 2], score_grad)
            )
        query_low[:, columns] = jnp.concatenate(query_parts, axis=0).T.astype(BF16)
        key_low[:, columns] = jnp.where(chosen, key_parts[0], key_parts[1]).astype(BF16)
        value_low[:, columns] = jnp.where(chosen, value_parts[0], value_parts[1]).astype(BF16)
        return carry

    lax.fori_loop(0, HEADS // 2, pair_of_heads, 0)


def block_rows(weights, parts):
    return weights.shape[1] // (len(parts) * parts[0].shape[0])


def join_kernel(*refs):
    start = 0
    for ref in refs[:-1]:
        refs[-1][start : start + ref.shape[0], :] = ref[...]
        start += ref.shape[0]


def join_rows(*members):
    if any(member.shape[0] % 8 for member in members):
        return jnp.concatenate(members, axis=0)
    rows = sum(member.shape[0] for member in members)
    return pl.pallas_call(
        join_kernel,
        in_specs=[VMEM] * len(members),
        out_specs=VMEM,
        out_shape=like((rows, members[0].shape[1]), members[0].dtype),
        cost_estimate=work(1),
        name="join_rows",
    )(*members)


def line_kernel(narrow, *refs, sizes):
    pieces, block = refs[:-1], refs[-1]
    start = 0
    for size in sizes:
        for step, piece in enumerate(pieces):
            place = pl.multiple_of(start * len(pieces) + (narrow[0] ^ step) * size, 8)
            block[pl.ds(place, size), :] = piece[start : start + size]
        start += size


def join_wide_kernel(*refs):
    block = refs[-1]
    width = block.shape[1]
    start, spot = 0, 0
    for ref in refs[:-1]:
        if ref.shape[1] == width:
            block[start : start + ref.shape[0], :] = ref[...]
            start += ref.shape[0]
    for ref in refs[:-1]:
        if ref.shape[1] != width:
            for first in range(0, ref.shape[1], LANES):
                top = start + spot // (width // LANES) * ref.shape[0]
                left = spot % (width // LANES) * LANES
                block[top : top + ref.shape[0], left : left + LANES] = ref[:, first : first + LANES]
                spot += 1
            size = ref.shape[0]
    while spot % (width // LANES):
        top = start + spot // (width // LANES) * size
        left = spot % (width // LANES) * LANES
        block[top : top + size, left : left + LANES] = jnp.zeros((size, LANES), BF16)
        spot += 1


def line_wide_kernel(narrow, *refs, sizes, wide_size):
    pieces, block, wide_block = refs[:-2], refs[-2], refs[-1]
    count, width = len(pieces), block.shape[1]
    start = 0
    for size in sizes:
        for step, piece in enumerate(pieces):
            place = pl.multiple_of(start * count + (narrow[0] ^ step) * size, 8)
            block[pl.ds(place, size), :] = piece[start : start + size]
        start += size
    matrices = wide_block.shape[0] // (count * wide_size)
    spot = 0
    for matrix in range(matrices):
        for first in range(0, wide_block.shape[1], LANES):
            top = start + spot // (width // LANES) * wide_size
            left = spot % (width // LANES) * LANES
            for step, piece in enumerate(pieces):
                place = pl.multiple_of((matrix * count + (narrow[0] ^ step)) * wide_size, 8)
                wide_block[pl.ds(place, wide_size), first : first + LANES] = piece[
                    top : top + wide_size, left : left + LANES
                ]
            spot += 1


def self_forward_kernel(
    places, lengths, inputs, *refs,
):
    parts = refs[:4]
    normed, query, key, value, attended, totals, stream, gains = refs[4:12]
    weights, gain_parts, bias, sems, gain_sems = refs[12:]
    size = parts[0].shape[0]
    rows = block_rows(weights, parts)
    gain_copies = [
        pltpu.make_async_copy(
            parts[slot // size].at[slot % size, pl.ds(4 * rows, gain_parts.shape[1]), :],
            gain_parts.at[slot],
            gain_sems.at[slot],
        )
        for slot in range(4 * size)
    ]
    copies = weight_copies(places, parts, 0, weights, rows, sems)
    for copy in gain_copies + copies:
        copy.start()
    values = inputs[...].astype(F32)
    fill_self_bias(bias, lengths)
    scaled = values * norm_scale(values)
    for copy in gain_copies:
        copy.wait()
    members = gain_parts[...].astype(F32).reshape(-1, 8, gains.shape[1])
    summed = members[0]
    for member in range(1, members.shape[0]):
        summed = summed + members[member]
    gains[...] = summed
    low = (scaled * summed[0:1]).astype(BF16)
    normed[...] = low
    for copy in copies:
        copy.wait()
    query[...] = nn(low, weights[0]).astype(BF16)
    key[...] = nn(low, weights[1]).astype(BF16)
    value[...] = nn(low, weights[2]).astype(BF16)
    attend(query, key, value, bias, attended, totals)
    stream[...] = values + nn(attended[...], weights[3])


def memory_kernel(places, memory, *refs):
    parts = refs[:4]
    key, value, weights, sems = refs[4:]
    rows = block_rows(weights, parts)
    copies = weight_copies(places, parts, rows, weights, rows, sems)
    for copy in copies:
        copy.start()
    for copy in copies:
        copy.wait()
    key[...] = nn(memory[...], weights[0]).astype(BF16)
    value[...] = nn(memory[...], weights[1]).astype(BF16)


def cross_forward_kernel(
    places, lengths, sources, stream_in, gains, key, value, *refs,
):
    parts = refs[:4]
    normed, query, attended, totals, stream, weights, bias, sems = refs[4:]
    rows = block_rows(weights, parts)
    copies = weight_copies(places, parts, 0, weights.at[pl.ds(0, 1)], rows, sems.at[0])
    copies += weight_copies(places, parts, 3 * rows, weights.at[pl.ds(1, 1)], rows, sems.at[1])
    for copy in copies:
        copy.start()
    values = stream_in[...]
    fill_cross_bias(bias, lengths, sources)
    low = (values * norm_scale(values) * gains[1:2]).astype(BF16)
    normed[...] = low
    for copy in copies:
        copy.wait()
    query[...] = nn(low, weights[0]).astype(BF16)
    attend(query, key, value, bias, attended, totals)
    stream[...] = values + nn(attended[...], weights[1])


def mlp_forward_kernel(
    places, stream_in, gains, side, *refs,
):
    parts, down_parts = refs[:4], refs[4:8]
    normed, gate, up, hidden, stream, activations, exit_normed = refs[8:15]
    weights, down, sems, down_sems = refs[15:]
    rows, down_rows = block_rows(weights, parts), block_rows(down, down_parts)
    first = weight_copies(places, parts, 0, weights, rows, sems)
    last = weight_copies(
        places, down_parts, down_parts[0].shape[1] - down_rows, down, down_rows, down_sems
    )
    for copy in first + last:
        copy.start()
    values = stream_in[...]
    low = (values * norm_scale(values) * gains[2:3]).astype(BF16)
    normed[...] = low
    for copy in first:
        copy.wait()
    width = weights.shape[2]
    step = width // 4
    for part in range(4):
        columns = pl.ds(part * step, step)
        gate_pre = nn(low, weights[0, :, columns])
        up_pre = nn(low, weights[1, :, columns])
        gate[:, columns] = gate_pre
        up[:, columns] = up_pre
        bent = jnp.tanh(MIX * (gate_pre + CUBE * (gate_pre * gate_pre * gate_pre)))
        hidden[:, columns] = (0.5 * gate_pre * (1.0 + bent) * up_pre).astype(BF16)
    for copy in last:
        copy.wait()
    out = values + nn(hidden[...], down[0])
    stream[...] = out
    activations[...] = out.astype(BF16)
    count = out.shape[0]
    exit_normed[:count] = (out * norm_scale(out) * gains[3:4]).astype(BF16)
    exit_normed[count:] = side[...]


def exit_scores_kernel(meta, slot_of, *refs, vocab, scale):
    parts = refs[:4]
    source, raised, across, stats = refs[4:8]
    table, tokens, columns, landed, scores, table_sem, sems = refs[8:]
    size = parts[0].shape[0]
    members = 4 * size
    ring = landed.shape[0]
    count = parts[0].shape[1] - 8
    step = pl.program_id(0)
    tile = raised.shape[0]
    starts, counts = META_LISTS, META_LISTS + members

    def fetch(member):
        slot = slot_of[member]
        for part in range(4):

            @pl.when(slot // size == part)
            def start():
                pltpu.make_async_copy(
                    parts[part].at[slot % size], landed.at[member % ring], sems.at[member % ring]
                ).start()

    @pl.when(step == 0)
    def load():
        whole = pltpu.make_async_copy(source, table, table_sem)
        for member in range(min(ring, members)):
            fetch(member)
        whole.start()
        tokens[...] = jnp.zeros_like(tokens)
        columns[...] = jnp.zeros_like(columns)
        lanes = -(-count // LANES) * LANES
        spots = lax.broadcasted_iota(jnp.int32, (1, lanes), 1)
        for member in range(members):
            pltpu.make_async_copy(
                parts[0].at[0], landed.at[member % ring], sems.at[member % ring]
            ).wait()
            begin = pl.multiple_of(meta[starts + member], 16)
            block = landed[member % ring]
            tokens[pl.ds(begin, count), :] = block[:count]
            side = block[count:, :lanes].astype(F32)
            wanted = side[0:1] * 256.0 + side[1:2]
            weight = jnp.where(spots < meta[counts + member], 1.0, 0.0)
            packed = jnp.concatenate(
                [weight, wanted, jnp.zeros((LANES - 2, lanes), F32)], axis=0
            )
            columns[pl.ds(begin, count), :] = packed.T[:count]
            if member + ring < members:
                fetch(member + ring)
        whole.wait()

    spot = lax.broadcasted_iota(jnp.int32, (tile, LANES), 1)

    @pl.when(step < meta[META_TILES])
    def compute():
        here = pl.ds(pl.multiple_of(step * tile, tile), tile)
        own = tokens[here, :]
        column = columns[here, :]
        across[...] = own.T
        width = scores.shape[1]
        lanes = lax.broadcasted_iota(jnp.int32, (tile, LANES), 1)
        wanted = column[:, 1:2].astype(jnp.int32) - meta[META_WIDE] * vocab
        wanted = jnp.where(wanted < vocab, wanted, -1)
        peaks = jnp.full((tile, LANES), NEGATIVE, F32)
        found = jnp.zeros((tile, LANES), F32)
        for first in range(0, width, VOCAB_TILE):
            part = nn(own, table[:, first : first + VOCAB_TILE])
            for inner in range(0, VOCAB_TILE, LANES):
                piece = part[:, inner : inner + LANES]
                offset = first + inner
                if offset + LANES > vocab:
                    piece = jnp.where(lanes < vocab - offset, piece, NEGATIVE)
                scores[:, offset : offset + LANES] = piece
                peaks = jnp.maximum(peaks, piece)
                found = found + jnp.where(lanes == wanted - offset, piece, 0.0)
        highest = jnp.max(peaks, axis=1, keepdims=True)
        sums = jnp.zeros((tile, LANES), F32)
        for offset in range(0, width, LANES):
            piece = jnp.exp2((scores[:, offset : offset + LANES] - highest) * (scale * LOG2E))
            raised[:, offset : offset + LANES] = piece.astype(BF16)
            sums = sums + piece
        summed = jnp.sum(sums, axis=1, keepdims=True)
        picked = jnp.sum(found, axis=1, keepdims=True)
        values = (highest * scale, summed, picked * scale, column[:, 0:1], column[:, 1:2])
        packed = jnp.zeros((tile, LANES), F32)
        for place, value in enumerate(values):
            packed = jnp.where(spot == place, value, packed)
        stats[...] = packed.T[:8]

    @pl.when(step >= meta[META_TILES])
    def skip():
        rows = lax.broadcasted_iota(jnp.int32, stats.shape, 0)
        stats[...] = jnp.where(rows == 1, 1.0, 0.0)


def exit_grads_kernel(meta, places, *refs, vocab):
    source, raised, across, factors = refs[:4]
    parts = refs[4:8]
    table_grad = refs[8]
    table, total, token_grad, landed, table_sem, sems = refs[9:]
    size = parts[0].shape[0]
    members = 4 * size
    count = parts[0].shape[1]
    starts, counts = META_LISTS, META_LISTS + members
    step = pl.program_id(0)
    tile = raised.shape[0]
    width = raised.shape[1]

    @pl.when(step == 0)
    def load():
        whole = pltpu.make_async_copy(source, table, table_sem)
        whole.start()
        total[...] = jnp.zeros_like(total)
        whole.wait()

    @pl.when(step < meta[META_TILES] // (tile // ROW_TILE))
    def compute():
        columns = jnp.concatenate(
            [factors[...], jnp.zeros((LANES - factors.shape[0], tile), F32)], axis=0
        ).T
        factor, at_target = columns[:, 0:1], columns[:, 1:2]
        wanted = columns[:, 2:3].astype(jnp.int32) - meta[META_WIDE] * vocab
        wanted = jnp.where(wanted < vocab, wanted, -1)
        lanes = lax.broadcasted_iota(jnp.int32, (tile, VOCAB_TILE), 1)
        grad = jnp.zeros((tile, token_grad.shape[1]), F32)
        for first in range(0, width, VOCAB_TILE):
            chunk = slice(first, first + VOCAB_TILE)
            part = raised[:, chunk].astype(F32) * factor
            part = jnp.where(lanes == wanted - first, at_target, part).astype(BF16)
            grad = grad + nt(part, table[:, chunk])
            total[:, chunk] += nn(across[...], part)
        token_grad[pl.ds(pl.multiple_of(step * tile, tile), tile), :] = grad.astype(BF16)

    @pl.when(step == pl.num_programs(0) - 1)
    def finish():
        copies = []
        spots = lax.broadcasted_iota(jnp.int32, (count, 1), 0)
        for slot in range(members):
            if slot >= 2:
                copies[slot - 2].wait()
            member = places[slot]
            begin = pl.multiple_of(meta[starts + member], 16)
            block = token_grad[pl.ds(begin, count), :].astype(F32)
            landed[slot % 2] = jnp.where(spots < meta[counts + member], block, 0.0).astype(BF16)
            copy = pltpu.make_async_copy(
                landed.at[slot % 2], parts[slot // size].at[slot % size], sems.at[slot % 2]
            )
            copy.start()
            copies.append(copy)
        table_grad[...] = total[...].astype(BF16)
        for copy in copies[-2:]:
            copy.wait()


def mlp_backward_kernel(
    places, grad_in, stream_three, stream_two, gain, normed, gate, up, hidden, *refs,
):
    parts, down_parts = refs[:4], refs[4:8]
    stream_grad, gains = refs[8:10]
    grad_parts, down_grad_parts = refs[10:14], refs[14:18]
    weights, down, gate_low, up_low, result, down_result, sems, down_sems = refs[18:]
    rows, down_rows = block_rows(weights, parts), block_rows(down, down_parts)
    copies = weight_copies(
        places, down_parts, down_parts[0].shape[1] - down_rows, down, down_rows, down_sems
    )
    copies += weight_copies(places, parts, 0, weights, rows, sems)
    for copy in copies:
        copy.start()
    stream_back, exit_gain_grad = norm_back(stream_three[...], gain[3:4], grad_in[...])
    branch = stream_back.astype(BF16)
    for copy in copies:
        copy.wait()
    width = weights.shape[2]
    step = width // 4
    for part in range(4):
        columns = pl.ds(part * step, step)
        gate_pre = gate[:, columns]
        up_pre = up[:, columns]
        hidden_grad = nt(branch, down[0, columns, :])
        bent = jnp.tanh(MIX * (gate_pre + CUBE * (gate_pre * gate_pre * gate_pre)))
        slope = 0.5 * (1.0 + bent) + 0.5 * gate_pre * (1.0 - bent * bent) * (
            MIX * (1.0 + 3.0 * CUBE * gate_pre * gate_pre)
        )
        gate_low[:, columns] = (hidden_grad * up_pre * slope).astype(BF16)
        up_low[:, columns] = (hidden_grad * (0.5 * gate_pre * (1.0 + bent))).astype(BF16)
    normed_grad = nt(gate_low[...], weights[0]) + nt(up_low[...], weights[1])
    branch_in, gain_grad = norm_back(stream_two[...], gain[2:3], normed_grad)
    stream_grad[...] = stream_back + branch_in
    gains[...] = jnp.concatenate(
        [gain_grad, exit_gain_grad, jnp.zeros((6, gain_grad.shape[1]), F32)], axis=0
    )
    for matrix, low in enumerate((gate_low, up_low)):
        for part in range(4):
            columns = pl.ds(part * step, step)
            result[:, columns] = tn(normed[...], low[:, columns]).astype(BF16)
        store_blocks(places, result, matrix * rows, rows, grad_parts)
    for part in range(4):
        columns = pl.ds(part * step, step)
        down_result[columns, :] = tn(hidden[:, columns], branch).astype(BF16)
    store_blocks(places, down_result, 0, down_rows, down_grad_parts)


def cross_attention_backward_kernel(
    places, lengths, sources, grad_in, query, key, value, totals, *refs,
):
    parts = refs[:4]
    branch, query_low, key_low, value_low, weights, bias, attended_grad, sems = refs[4:]
    rows = block_rows(weights, parts)
    copies = weight_copies(places, parts, 3 * rows, weights, rows, sems)
    for copy in copies:
        copy.start()
    fill_cross_bias(bias, lengths, sources)
    branch[...] = grad_in[...].astype(BF16)
    for copy in copies:
        copy.wait()
    attended_grad[...] = nt(branch[...], weights[0]).astype(BF16)
    attend_back(
        query, key, value, bias, totals, attended_grad, query_low, key_low, value_low
    )


def cross_backward_kernel(
    places, grad_in, stream_in, gain, normed, memory, attended,
    branch, query_low, key_low, value_low, *refs,
):
    parts = refs[:4]
    stream_grad, gains, memory_grad = refs[4:7]
    grad_parts = refs[7:11]
    weights, result, sems = refs[11:]
    rows = block_rows(weights, parts)
    copies = weight_copies(places, parts, 0, weights, rows, sems)
    for copy in copies:
        copy.start()
    pairs = ((normed, query_low), (memory, key_low), (memory, value_low), (attended, branch))
    for matrix, (left, right) in enumerate(pairs):
        result[...] = tn(left[...], right[...]).astype(BF16)
        store_blocks(places, result, matrix * rows, rows, grad_parts)
    for copy in copies:
        copy.wait()
    normed_grad = nt(query_low[...], weights[0])
    branch_in, gain_grad = norm_back(stream_in[...], gain[1:2], normed_grad)
    stream_grad[...] = grad_in[...] + branch_in
    gains[...] = jnp.broadcast_to(gain_grad, gains.shape)
    memory_grad[...] = nt(key_low[...], weights[1]) + nt(value_low[...], weights[2])


def self_attention_backward_kernel(
    places, lengths, grad_in, query, key, value, totals, *refs,
):
    parts = refs[:4]
    branch, query_low, key_low, value_low, weights, bias, attended_grad, sems = refs[4:]
    rows = block_rows(weights, parts)
    copies = weight_copies(places, parts, 3 * rows, weights, rows, sems)
    for copy in copies:
        copy.start()
    fill_self_bias(bias, lengths)
    branch[...] = grad_in[...].astype(BF16)
    for copy in copies:
        copy.wait()
    attended_grad[...] = nt(branch[...], weights[0]).astype(BF16)
    attend_back(
        query, key, value, bias, totals, attended_grad, query_low, key_low, value_low
    )


def self_backward_kernel(
    places, grad_in, inputs, gain, normed, attended, cross_gains, mlp_gains,
    branch, query_low, key_low, value_low, *refs,
):
    parts = refs[:4]
    stream_grad = refs[4]
    grad_parts = refs[5:9]
    weights, result, sems = refs[9:]
    rows = block_rows(weights, parts)
    copies = weight_copies(places, parts, 0, weights, rows, sems)
    for copy in copies:
        copy.start()
    pairs = ((normed, query_low), (normed, key_low), (normed, value_low), (attended, branch))
    for matrix, (left, right) in enumerate(pairs):
        result[...] = tn(left[...], right[...]).astype(BF16)
        store_blocks(places, result, matrix * rows, rows, grad_parts)
    for copy in copies:
        copy.wait()
    normed_grad = (
        nt(query_low[...], weights[0])
        + nt(key_low[...], weights[1])
        + nt(value_low[...], weights[2])
    )
    branch_in, gain_grad = norm_back(inputs[...].astype(F32), gain[0:1], normed_grad)
    stream_grad[...] = grad_in[...] + branch_in
    spot = lax.broadcasted_iota(jnp.int32, (8, gain_grad.shape[1]), 0)
    terms = jnp.where(spot == 0, gain_grad, 0.0)
    terms = jnp.where(spot == 1, cross_gains[0:1], terms)
    terms = jnp.where(spot == 2, mlp_gains[0:1], terms)
    terms = jnp.where(spot == 3, mlp_gains[1:2], terms).astype(BF16)
    for part in grad_parts:
        for slot in range(part.shape[0]):
            for start in range(4 * rows, part.shape[1], 8):
                part[slot, start : start + 8, :] = terms


def per_device(
    inputs,
    memory,
    targets,
    tgt_lengths,
    src_lengths,
    self_gain,
    self_query,
    self_key,
    self_value,
    self_out,
    cross_gain,
    cross_query,
    cross_key,
    cross_value,
    cross_out,
    mlp_gain,
    mlp_gate,
    mlp_up,
    mlp_down,
    exit_gain,
    embedding,
):
    tokens, model = inputs.shape
    slots = memory.shape[0]
    hidden_width = mlp_gate.shape[1]
    pair_slots = tgt_lengths.shape[1]
    wide_count = lax.axis_size("wide")
    narrow_count = lax.axis_size("narrow")
    wide = lax.axis_index("wide")
    narrow = lax.axis_index("narrow")
    slot_total = tokens * wide_count * narrow_count
    scale = 1.0 / math.sqrt(model)
    places = slot_places(wide, wide_count)
    lengths, sources = tgt_lengths[0], src_lengths[0]
    shard = self_query.shape[0]
    rows = shard * narrow_count
    down_rows = mlp_down.shape[0] * narrow_count

    aligned = rows % 8 == 0
    kernel_places = places if aligned else jnp.arange(4, dtype=jnp.int32)
    kernel_count = wide_count if aligned else 4
    ids = jnp.arange(wide_count, dtype=jnp.int32)
    order = places[None, :] == ids[:, None]

    def reorder(matrix, blocks):
        flat = blocks.reshape(wide_count, -1)
        return nn(matrix.astype(BF16), flat).astype(BF16).reshape(blocks.shape)

    def for_kernels(parts, sizes):
        if aligned:
            return parts
        whole, start, members = jnp.concatenate(parts, axis=0), 0, []
        for size in sizes:
            ordered = reorder(order, whole[:, start : start + size])
            members.append(ordered.reshape(4, -1, whole.shape[-1]))
            start += size
        return jnp.split(jnp.concatenate(members, axis=1), 4)

    def from_kernels(parts, sizes):
        if aligned:
            return parts
        whole, start, members = jnp.concatenate(parts, axis=0), 0, []
        for size in sizes:
            extent = size * wide_count // 4
            member = whole[:, start : start + extent].reshape(wide_count, size, -1)
            members.append(reorder(order.T, member))
            start += extent
        return jnp.split(jnp.concatenate(members, axis=1), 4)

    def line_block(pieces, sizes, *others):
        pieces = lax.optimization_barrier((*pieces, *others))[: len(pieces)]
        if all(size % 8 == 0 for size in sizes):
            return pl.pallas_call(
                functools.partial(line_kernel, sizes=sizes),
                in_specs=[SMEM] + [VMEM] * len(pieces),
                out_specs=VMEM,
                out_shape=like((pieces[0].shape[0] * len(pieces), pieces[0].shape[1]), BF16),
                compiler_params=PARAMS,
                cost_estimate=work(1),
                name="line_block",
            )(narrow[None], *pieces)
        ordered, start, members = in_line_order(pieces, narrow), 0, []
        for size in sizes:
            members += [piece[start : start + size] for piece in ordered]
            start += size
        return jnp.concatenate(members, axis=0)

    self_sizes, cross_sizes = [shard] * 4 + [8], [shard] * 4 + [mlp_down.shape[0]]
    gate_sizes = [shard] * 2
    count = jnp.sum(lengths)
    owner = wide * narrow_count + narrow
    gain_shards = jnp.stack([self_gain, cross_gain, mlp_gain, exit_gain])
    numbers = jnp.broadcast_to(
        jnp.stack([count // 16, count % 16])[:, None], (2, shard)
    ).astype(BF16)
    own_rows = jnp.concatenate([gain_shards, numbers, jnp.zeros((2, shard), BF16)], axis=0)
    own_rows = jnp.tile(own_rows, (1, model // shard))
    own_columns = jnp.arange(model, dtype=jnp.int32)[None, :] // shard == owner
    own_rows = jnp.where(own_columns, own_rows, 0)
    self_pack = join_rows(self_query, self_key, self_value, self_out, own_rows)
    members = (cross_query, cross_key, cross_value, cross_out, mlp_down)
    if aligned:
        wide_rows = -(-2 * hidden_width // model) * shard
        joined_pack = pl.pallas_call(
            join_wide_kernel,
            in_specs=[VMEM] * 7,
            out_specs=VMEM,
            out_shape=like((sum(cross_sizes) + wide_rows, model), BF16),
            compiler_params=PARAMS,
            cost_estimate=work(1),
            name="join_wide",
        )(*members, mlp_gate, mlp_up)
    side = jnp.stack([targets // 256, targets % 256]).astype(BF16)
    side = jnp.pad(side, ((0, 6), (0, model - tokens)))

    self_line = gather_narrow(self_pack, narrow_count)
    self_block = line_block(self_line, self_sizes)

    vocab = embedding.shape[0]
    padded = -(-vocab // VOCAB_TILE) * VOCAB_TILE
    turned = jnp.pad(embedding.T, ((0, 0), (0, padded - vocab)))
    table = lax.all_gather(tie(turned, *self_line), "narrow", axis=0, tiled=True)

    *early, last = stage_pairs(wide_count)

    def gather_early(block):
        held = block[None]
        for pairs in early:
            held = jnp.concatenate([held, lax.ppermute(held, "wide", pairs)], axis=0)
        return held

    if aligned:
        joined_line = gather_narrow(tie(joined_pack, *self_line), narrow_count)
    else:
        cross_line = gather_narrow(join_rows(*members), narrow_count)
        gate_line = gather_narrow(join_rows(mlp_gate, mlp_up), narrow_count)
    self_held = gather_early(self_block)
    self_came = lax.ppermute(self_held, "wide", last)
    if aligned:
        joined_line = lax.optimization_barrier((*joined_line, self_held))[:narrow_count]
        cross_block, gate_block = pl.pallas_call(
            functools.partial(line_wide_kernel, sizes=cross_sizes, wide_size=shard),
            in_specs=[SMEM] + [VMEM] * narrow_count,
            out_specs=[VMEM] * 2,
            out_shape=[
                like((sum(cross_sizes) * narrow_count, model), BF16),
                like((2 * rows, hidden_width), BF16),
            ],
            compiler_params=PARAMS,
            cost_estimate=work(1),
            name="line_wide",
        )(narrow[None], *joined_line)
    else:
        cross_block = line_block(cross_line, cross_sizes)
        gate_block = line_block(gate_line, gate_sizes)
    self_parts = (
        self_held, self_came, cross_core(self_held, wide_count), cross_core(self_came, wide_count)
    )
    cross_held = gather_early(tie(cross_block, self_came))
    cross_came = lax.ppermute(cross_held, "wide", last)

    head_rows = like((HEADS, 1, tokens), F32)
    activation = like((tokens, model), BF16)
    stream_like = like((tokens, model), F32)
    matrix_sems = pltpu.SemaphoreType.DMA((kernel_count, 4))
    one_matrix_sems = pltpu.SemaphoreType.DMA((kernel_count, 1))

    self_gathered = for_kernels(self_parts, [size * narrow_count for size in self_sizes])
    (
        normed_one, query_one, key_one, value_one, attended_one, totals_one, stream_one, gain_all,
    ) = pl.pallas_call(
        self_forward_kernel,
        in_specs=[SMEM, SMEM, VMEM] + [ANY] * 4,
        out_specs=[VMEM] * 8,
        out_shape=[activation] * 5 + [head_rows, stream_like, like((8, model), F32)],
        scratch_shapes=[
            pltpu.VMEM((4, model, model), BF16),
            pltpu.VMEM((kernel_count, 8 * narrow_count * wide_count // kernel_count, model), BF16),
            pltpu.VMEM((tokens, tokens), F32),
            matrix_sems,
            pltpu.SemaphoreType.DMA((kernel_count,)),
        ],
        compiler_params=PARAMS,
        cost_estimate=work(1),
        name="self_forward",
    )(kernel_places, lengths, tie(inputs, cross_held), *self_gathered)

    numbers = (gain_all[4] * 16.0 + gain_all[5]).reshape(wide_count, narrow_count, shard)[:, :, 0]
    numbers = jnp.sum(
        jnp.where(jnp.arange(narrow_count)[None, :] == narrow, numbers, 0.0), axis=1
    ).astype(jnp.int32)
    extents = (numbers + 15) // 16 * 16
    starts = jnp.sum(jnp.where(ids[None, :] < ids[:, None], extents[None, :], 0), axis=1)
    needed = (jnp.sum(extents) + GRAD_TILE - 1) // GRAD_TILE * (GRAD_TILE // ROW_TILE)
    meta = jnp.concatenate([jnp.stack([wide, needed]), starts, numbers])
    slot_of = jnp.sum(jnp.where(order, ids[None, :], 0), axis=1)

    cross_came = tie(cross_came, stream_one)
    cross_parts = (
        cross_held, cross_came, cross_core(cross_held, wide_count), cross_core(cross_came, wide_count)
    )
    gate_held = gather_early(tie(gate_block, cross_came))
    gate_came = lax.ppermute(gate_held, "wide", last)
    cross_gathered = for_kernels(cross_parts, [size * narrow_count for size in cross_sizes])

    key_two, value_two = pl.pallas_call(
        memory_kernel,
        in_specs=[SMEM, VMEM] + [ANY] * 4,
        out_specs=[VMEM] * 2,
        out_shape=[like((slots, model), BF16)] * 2,
        scratch_shapes=[
            pltpu.VMEM((2, model, model), BF16),
            pltpu.SemaphoreType.DMA((kernel_count, 2)),
        ],
        compiler_params=PARAMS,
        cost_estimate=work(1),
        name="memory_projection",
    )(kernel_places, memory, *cross_gathered)

    normed_two, query_two, attended_two, totals_two, stream_two = pl.pallas_call(
        cross_forward_kernel,
        in_specs=[SMEM, SMEM, SMEM, VMEM, VMEM, VMEM, VMEM] + [ANY] * 4,
        out_specs=[VMEM] * 5,
        out_shape=[activation] * 3 + [head_rows, stream_like],
        scratch_shapes=[
            pltpu.VMEM((2, model, model), BF16),
            pltpu.VMEM((slots, tokens), F32),
            pltpu.SemaphoreType.DMA((2, kernel_count, 1)),
        ],
        compiler_params=PARAMS,
        cost_estimate=work(1),
        name="cross_forward",
    )(
        kernel_places, lengths, sources, tie(stream_one, gate_held), gain_all, key_two, value_two,
        *cross_gathered,
    )

    gate_came = tie(gate_came, stream_two)
    gate_parts = (
        gate_held, gate_came, cross_core(gate_held, wide_count), cross_core(gate_came, wide_count)
    )
    gate_gathered = for_kernels(gate_parts, [size * narrow_count for size in gate_sizes])

    wide_f32 = like((tokens, hidden_width), F32)
    wide_low = like((tokens, hidden_width), BF16)
    normed_three, gate_pre, up_pre, hidden, stream_three, activations, normed_four = pl.pallas_call(
        mlp_forward_kernel,
        in_specs=[SMEM, VMEM, VMEM, VMEM] + [ANY] * 8,
        out_specs=[VMEM] * 7,
        out_shape=[
            activation, wide_f32, wide_f32, wide_low, stream_like, activation,
            like((tokens + 8, model), BF16),
        ],
        scratch_shapes=[
            pltpu.VMEM((2, model, hidden_width), BF16),
            pltpu.VMEM((1, hidden_width, model), BF16),
            pltpu.SemaphoreType.DMA((kernel_count, 2)),
            one_matrix_sems,
        ],
        compiler_params=PARAMS,
        cost_estimate=work(1),
        name="mlp_forward",
    )(kernel_places, stream_two, gain_all, side, *gate_gathered, *cross_gathered)

    exit_parts = gather_wide(normed_four, wide_count)
    group = tokens * wide_count
    tiles = -(-group // GRAD_TILE) * (GRAD_TILE // ROW_TILE)
    kept = lambda i, meta: jnp.minimum(i, meta[META_TILES] - 1)
    kept_grad = lambda i, meta: jnp.minimum(i, meta[META_TILES] * ROW_TILE // GRAD_TILE - 1)

    raised, tokens_across, stats = pl.pallas_call(
        functools.partial(exit_scores_kernel, vocab=vocab, scale=scale),
        grid_spec=pltpu.PrefetchScalarGridSpec(
            num_scalar_prefetch=2,
            grid=(tiles,),
            in_specs=[ANY] * 5,
            out_specs=[
                pl.BlockSpec((ROW_TILE, padded), lambda i, meta, slots: (kept(i, meta), 0)),
                pl.BlockSpec((model, ROW_TILE), lambda i, meta, slots: (0, kept(i, meta))),
                pl.BlockSpec((8, ROW_TILE), lambda i, meta, slots: (0, i)),
            ],
            scratch_shapes=[
                pltpu.VMEM((model, padded), BF16),
                pltpu.VMEM((tiles * ROW_TILE, model), BF16),
                pltpu.VMEM((tiles * ROW_TILE, LANES), F32),
                pltpu.VMEM((min(wide_count, 8), tokens + 8, model), BF16),
                pltpu.VMEM((ROW_TILE, padded), F32),
                pltpu.SemaphoreType.DMA,
                pltpu.SemaphoreType.DMA((min(wide_count, 8),)),
            ],
        ),
        out_shape=[
            like((tiles * ROW_TILE, padded), BF16),
            like((model, tiles * ROW_TILE), BF16),
            like((8, tiles * ROW_TILE), F32),
        ],
        compiler_params=PARAMS,
        cost_estimate=work(1),
        name="exit_scores",
    )(meta, slot_of, *exit_parts, table)

    own_peak = stats[0]
    joint = stats
    for pairs in stage_pairs(wide_count) + [flip_pairs(wide_count)]:
        came = lax.ppermute(joint, "wide", pairs)
        peak = jnp.maximum(joint[0], came[0])
        summed = joint[1] * jnp.exp(joint[0] - peak) + came[1] * jnp.exp(came[0] - peak)
        joint = jnp.concatenate([peak[None], summed[None], joint[2:3] + came[2:3], stats[3:]], axis=0)
    log_total = joint[0] + jnp.log(joint[1])
    picked, group_weight = joint[2], stats[3]
    loss_part = jnp.full((8, LANES), jnp.sum(group_weight * (log_total - picked)), F32)
    loss_all = loss_part
    for step in range(1, narrow_count):
        loss_all = loss_all + lax.ppermute(loss_part, "narrow", narrow_pairs(narrow_count, step))
    mean_loss = loss_all[0, 0] / slot_total

    factor = jnp.exp(own_peak - log_total) * (group_weight * scale)
    at_target = (jnp.exp(picked - log_total) - 1.0) * (group_weight * scale)
    factors = jnp.concatenate([factor[None], at_target[None], stats[4:5], stats[3:]], axis=0)
    token_part = like((wide_count // 4, tokens, model), BF16)
    *exit_grads, table_grad = pl.pallas_call(
        functools.partial(exit_grads_kernel, vocab=vocab),
        grid_spec=pltpu.PrefetchScalarGridSpec(
            num_scalar_prefetch=2,
            grid=(tiles * ROW_TILE // GRAD_TILE,),
            in_specs=[
                ANY,
                pl.BlockSpec((GRAD_TILE, padded), lambda i, meta, slots: (kept_grad(i, meta), 0)),
                pl.BlockSpec((model, GRAD_TILE), lambda i, meta, slots: (0, kept_grad(i, meta))),
                pl.BlockSpec((8, GRAD_TILE), lambda i, meta, slots: (0, i)),
            ],
            out_specs=[ANY] * 4 + [pl.BlockSpec((model, padded), lambda i, meta, slots: (0, 0))],
            scratch_shapes=[
                pltpu.VMEM((model, padded), BF16),
                pltpu.VMEM((model, padded), F32),
                pltpu.VMEM((tiles * ROW_TILE, model), BF16),
                pltpu.VMEM((2, tokens, model), BF16),
                pltpu.SemaphoreType.DMA,
                pltpu.SemaphoreType.DMA((2,)),
            ],
        ),
        out_shape=[token_part] * 4 + [like((model, padded), BF16)],
        compiler_params=PARAMS,
        cost_estimate=work(1),
        name="exit_grads",
    )(meta, places, table, raised, tokens_across, factors)

    table_sum = lax.psum_scatter(table_grad, "narrow", scatter_dimension=0, tiled=True)
    embedding_grad = table_sum.astype(F32).T[:vocab]
    exit_grad = scatter_wide(exit_grads, wide_count)

    gain_like = like((8, model), F32)
    stream_two_grad, mlp_gains, *mlp_grads = pl.pallas_call(
        mlp_backward_kernel,
        in_specs=[SMEM] + [VMEM] * 8 + [ANY] * 8,
        out_specs=[VMEM] * 10,
        out_shape=[stream_like, gain_like]
        + [like(part.shape, BF16) for part in gate_gathered]
        + [
            like((part.shape[0], hidden_width // kernel_count, model), BF16)
            for part in cross_gathered
        ],
        scratch_shapes=[
            pltpu.VMEM((2, model, hidden_width), BF16),
            pltpu.VMEM((1, hidden_width, model), BF16),
            pltpu.VMEM((tokens, hidden_width), BF16),
            pltpu.VMEM((tokens, hidden_width), BF16),
            pltpu.VMEM((model, hidden_width), BF16),
            pltpu.VMEM((hidden_width, model), BF16),
            pltpu.SemaphoreType.DMA((kernel_count, 2)),
            one_matrix_sems,
        ],
        compiler_params=PARAMS,
        cost_estimate=work(1),
        name="mlp_backward",
    )(
        kernel_places, exit_grad, stream_three, stream_two, gain_all, normed_three,
        gate_pre, up_pre, hidden, *gate_gathered, *cross_gathered,
    )
    gate_scatter = scatter_core(from_kernels(mlp_grads[:4], [rows, rows]), wide_count)
    down_scatter = scatter_core(from_kernels(mlp_grads[4:], [down_rows]), wide_count)

    low_like = like((slots, model), BF16)
    branch_two, query_two_low, key_two_low, value_two_low = pl.pallas_call(
        cross_attention_backward_kernel,
        in_specs=[SMEM] * 3 + [VMEM] * 5 + [ANY] * 4,
        out_specs=[VMEM] * 4,
        out_shape=[activation, activation, low_like, low_like],
        scratch_shapes=[
            pltpu.VMEM((1, model, model), BF16),
            pltpu.VMEM((slots, tokens), F32),
            pltpu.VMEM((tokens, model), BF16),
            one_matrix_sems,
        ],
        compiler_params=PARAMS,
        cost_estimate=work(1),
        name="cross_attention_backward",
    )(
        kernel_places, lengths, sources, stream_two_grad, query_two, key_two, value_two, totals_two,
        *cross_gathered,
    )

    def go_far(scatter, *others):
        (own, came), kept = scatter
        return scatter_far((own, tie(came, *others)), kept, wide_count)

    def go_near(state, *others):
        _, came, kept = state
        return scatter_near(tie(came, *others), kept, wide_count)

    gate_far = go_far(gate_scatter, query_two_low)
    down_far = go_far(down_scatter, query_two_low)

    cross_matrices = like((cross_gathered[0].shape[0], 4 * model // kernel_count, model), BF16)
    stream_one_grad, cross_gains, memory_grad, *cross_grads = pl.pallas_call(
        cross_backward_kernel,
        in_specs=[SMEM] + [VMEM] * 10 + [ANY] * 4,
        out_specs=[VMEM] * 7,
        out_shape=[stream_like, gain_like, like((slots, model), F32)] + [cross_matrices] * 4,
        scratch_shapes=[
            pltpu.VMEM((3, model, model), BF16),
            pltpu.VMEM((model, model), BF16),
            pltpu.SemaphoreType.DMA((kernel_count, 3)),
        ],
        compiler_params=PARAMS,
        cost_estimate=work(1),
        name="cross_backward",
    )(
        kernel_places, tie(stream_two_grad, gate_far[0], down_far[0]), stream_one, gain_all,
        normed_two, memory, attended_two, branch_two, query_two_low, key_two_low, value_two_low,
        *cross_gathered,
    )
    cross_scatter = scatter_core(from_kernels(cross_grads, [rows] * 4), wide_count)

    branch_one, query_one_low, key_one_low, value_one_low = pl.pallas_call(
        self_attention_backward_kernel,
        in_specs=[SMEM] * 2 + [VMEM] * 5 + [ANY] * 4,
        out_specs=[VMEM] * 4,
        out_shape=[activation] * 4,
        scratch_shapes=[
            pltpu.VMEM((1, model, model), BF16),
            pltpu.VMEM((tokens, tokens), F32),
            pltpu.VMEM((tokens, model), BF16),
            one_matrix_sems,
        ],
        compiler_params=PARAMS,
        cost_estimate=work(1),
        name="self_attention_backward",
    )(
        kernel_places, lengths, tie(stream_one_grad, loss_all), query_one, key_one, value_one, totals_one,
        *self_gathered,
    )
    gate_near = go_near(gate_far, query_one_low)
    down_near = go_near(down_far, query_one_low)
    cross_far = go_far(cross_scatter, query_one_low)

    inputs_grad, *self_grads = pl.pallas_call(
        self_backward_kernel,
        in_specs=[SMEM] + [VMEM] * 11 + [ANY] * 4,
        out_specs=[VMEM] * 5,
        out_shape=[stream_like] + [like(part.shape, BF16) for part in self_gathered],
        scratch_shapes=[
            pltpu.VMEM((3, model, model), BF16),
            pltpu.VMEM((model, model), BF16),
            pltpu.SemaphoreType.DMA((kernel_count, 3)),
        ],
        compiler_params=PARAMS,
        cost_estimate=work(1),
        name="self_backward",
    )(
        kernel_places, tie(stream_one_grad, gate_near[0], down_near[0], cross_far[0]), inputs,
        gain_all, normed_one, attended_one, cross_gains, mlp_gains, branch_one, query_one_low,
        key_one_low, value_one_low, *self_gathered,
    )
    extra = narrow_count * 8
    self_scatter = scatter_core(from_kernels(self_grads, [rows] * 4 + [extra]), wide_count)

    def finish(near, matrices, *others):
        _, came, held = near
        summed = held + tie(came, *others).astype(F32)
        width = summed.shape[-1]
        size = matrices * (summed.shape[0] // (matrices * 8 * narrow_count)) * 8 * narrow_count
        members = [
            summed[:size].reshape(matrices, narrow_count, -1, width).transpose(1, 0, 2, 3)
            .reshape(narrow_count, -1, width)
        ]
        if size < summed.shape[0]:
            members.append(summed[size:].reshape(narrow_count, -1, width))
        return scatter_narrow(jnp.concatenate(members, axis=1), narrow, narrow_count)

    gate_sum = finish(gate_near, 2, inputs_grad).reshape(2, shard, hidden_width)
    down_sum = finish(down_near, 1, inputs_grad)
    cross_near = go_near(cross_far, inputs_grad)
    self_far = go_far(self_scatter)
    cross_sum = finish(cross_near, 4).reshape(4, shard, model)
    self_sum = finish(go_near(self_far), 4)
    gains = pick(self_sum[4 * shard :].reshape(8, model // shard, shard), owner, 1)
    self_sum = self_sum[: 4 * shard].reshape(4, shard, model)

    return (
        activations,
        mean_loss,
        inputs_grad,
        memory_grad,
        gains[0],
        self_sum[0],
        self_sum[1],
        self_sum[2],
        self_sum[3],
        gains[1],
        cross_sum[0],
        cross_sum[1],
        cross_sum[2],
        cross_sum[3],
        gains[2],
        gate_sum[0],
        gate_sum[1],
        down_sum,
        gains[3],
        embedding_grad,
    )


def solution(mesh):
    both = ("wide", "narrow")
    rows, flat = P(both, None), P(both)
    placed = (
        rows, rows, flat, rows, rows,
        flat, rows, rows, rows, rows,
        flat, rows, rows, rows, rows,
        flat, rows, rows, rows, flat,
        P("wide", "narrow"),
    )
    given = (
        rows, P(), rows, rows,
        flat, rows, rows, rows, rows,
        flat, rows, rows, rows, rows,
        flat, rows, rows, rows, flat,
        P("wide", "narrow"),
    )
    return jax.shard_map(
        per_device, mesh=mesh, in_specs=placed, out_specs=given, check_vma=False
    )
```

time: 707 us -> 532 us (0.75)
  waiting for transfers between devices: 277 us -> 175 us
  blocking collectives: 38.3 us -> 0 us
  between operations: 33.4 us -> 20.4 us
  starting transfers between devices: 92.5 us -> 79.6 us
  Pallas kernels: 204 us -> 196 us
    ppermute x14 -> x1, waiting for transfers between devices: 108 us -> 7.15 us  [gather_wide(): held = jnp.concatenate([held, lax.ppermute(held, 'wide', pairs)], axis=0)]
    ppermute x36 -> x6, starting transfers between devices: 53.6 us -> 10.6 us  [gather_narrow(): lax.ppermute(block, 'narrow', narrow_pairs(count, step))]
    psum x1 -> x0, blocking collectives: 38.3 us -> none  [per_device(): lax.psum(gains, ('wide', 'narrow'))]
    ppermute x37 -> x50, starting transfers between devices: 34 us -> 62.4 us  [the longest x12 25.1 us: scatter_narrow(): lax.ppermute(sent, 'narrow', narrow_pairs(count, step)).astype(F32)]
    pallas_call x1, Pallas kernels: 38.9 us -> 24.5 us  [per_device(): pl.pallas_call(functools.partial(exit_scores_kernel, vocab=vocab, scale=s...]
    ppermute x36 -> x6, waiting for transfers between devices: 54.1 us -> 44.7 us  [gather_narrow(): lax.ppermute(block, 'narrow', narrow_pairs(count, step))]
    ppermute x37 -> x50, waiting for transfers between devices: 109 us -> 118 us  [the longest x3 36.7 us: gather_early(): held = jnp.concatenate([held, lax.ppermute(held, 'wide', pairs)], axis=0)]
    concatenate x14 -> x1, other arithmetic: 8.99 us -> 1.13 us  [gather_wide(): held = jnp.concatenate([held, lax.ppermute(held, 'wide', pairs)], axis=0)]
  transfers between devices with their start and end apart: 92 -> 62, of which waited for: 44 -> 28; matrix products, arithmetic and copies ran while one was open for 6% -> 7% of each run, Pallas kernels for 17% -> 25%
where the time goes in v2:
time: 532 us; the launch traced here: 527 us
  Pallas kernels  196 us (37%)
  waiting for transfers between devices  175 us (33%)
  starting transfers between devices  79.6 us (15%)
  other arithmetic  39.4 us (7%)
  between operations  20.4 us (4%)
  local copies, waits for them, and re-layouts  16.6 us (3%)
    ppermute x6, waiting for transfers between devices, gather_narrow(): lax.ppermute(block, 'narrow', narrow_pairs(count, step))  44.7 us
    pallas_call x1, Pallas kernels, per_device(): pl.pallas_call(functools.partial(exit_grads_kernel, vocab=vocab), grid_sp...  37.2 us
    ppermute x3, waiting for transfers between devices, gather_early(): held = jnp.concatenate([held, lax.ppermute(held, 'wide', pairs)], axis=0)  36.7 us
    ppermute x12, waiting for transfers between devices, scatter_narrow(): lax.ppermute(sent, 'narrow', narrow_pairs(count, step)).astype(F32)  25.3 us
    ppermute x12, starting transfers between devices, scatter_narrow(): lax.ppermute(sent, 'narrow', narrow_pairs(count, step)).astype(F32)  25.1 us
    pallas_call x1, Pallas kernels, per_device(): pl.pallas_call(functools.partial(exit_scores_kernel, vocab=vocab, scale=s...  24.5 us
    pallas_call x1, Pallas kernels, per_device(): pl.pallas_call(mlp_backward_kernel, in_specs=[SMEM] + [VMEM] * 8 + [ANY]...  21.4 us
    pallas_call x1, Pallas kernels, per_device(): pl.pallas_call(cross_attention_backward_kernel, in_specs=[SMEM] * 3 + [VM...  20.6 us
  transfers between devices with their start and end apart: 62, of which 28 were waited for; matrix products, arithmetic and copies ran while one was open for 7% of the time, Pallas kernels for 25%

profile of v2, /device:TPU:0, one launch (start us, length us, event | category | flops | bytes accessed | tf_op | source)
XLA Modules:
  0.0 527.2 jit_solution(14915646687739469405)
XLA Ops:
  24.0 8.3 %collective-permute-done.1.refs_2_ = bf16[104,768]{1,0:T(8,128)(2,1)S(1)} collective-permute-done((bf16[104,768]{1,0:T(8,128)(2,1)}, bf16[104,768]{1,0:T(8,128)(2,1)S(1)}, u32[]{:S(2)}, u32[]{:S(2)}) %collective-permute-start.1) | collective-permute-done | bytes 159776 | tf_op jit(solution)/shard_map/ppermute | solution.py:136
  36.6 9.1 %collective-permute-done.6 = bf16[1,416,768]{2,1,0:T(8,128)(2,1)S(1)} collective-permute-done((bf16[1,416,768]{2,1,0:T(8,128)(2,1)}, bf16[1,416,768]{2,1,0:T(8,128)(2,1)S(1)}, u32[]{:S(2)}, u32[]{:S(2)}) %collective-permute-start.6) | collective-permute-done | bytes 639008 | tf_op jit(solution)/shard_map/ppermute | solution.py:912
  55.4 14.3 %collective-permute-done.3.refs_1_ = bf16[304,768]{1,0:T(8,128)(2,1)S(1)} collective-permute-done((bf16[304,768]{1,0:T(8,128)(2,1)}, bf16[304,768]{1,0:T(8,128)(2,1)S(1)}, u32[]{:S(2)}, u32[]{:S(2)}) %collective-permute-start.3) | collective-permute-done | bytes 466976 | tf_op jit(solution)/shard_map/ppermute | solution.py:136
  69.7 18.0 %collective-permute-done.4.refs_2_ = bf16[304,768]{1,0:T(8,128)(2,1)S(1)} collective-permute-done((bf16[304,768]{1,0:T(8,128)(2,1)}, bf16[304,768]{1,0:T(8,128)(2,1)S(1)}, u32[]{:S(2)}, u32[]{:S(2)}) %collective-permute-start.4) | collective-permute-done | bytes 466976 | tf_op jit(solution)/shard_map/ppermute | solution.py:136
  94.2 14.9 %collective-permute-done.8 = bf16[1,640,768]{2,1,0:T(8,128)(2,1)} collective-permute-done((bf16[1,640,768]{2,1,0:T(8,128)(2,1)}, bf16[1,640,768]{2,1,0:T(8,128)(2,1)}, u32[]{:S(2)}, u32[]{:S(2)}) %collective-permute-start.8) | collective-permute-done | bytes 983072 | tf_op jit(solution)/shard_map/ppermute | solution.py:912
  116.3 12.3 %self_forward.1 = (bf16[320,768]{1,0:T(8,128)(2,1)}, bf16[320,768]{1,0:T(8,128)(2,1)}, bf16[320,768]{1,0:T(8,128)(2,1)}, bf16[320,768]{1,0:T(8,128)(2,1)}, bf16[...) custom-call(s32[8]{0:T(128)} %fusion.61.places, s32[2]{0:T(128)} %bitcast.148, ...), custom_call_target="tpu_custom_call" | custom-call | flops 1000000000 | bytes 1000000 | tf_op jit(solution)/shard_map/self_forward/pallas_call | solution.py:954
  128.6 11.2 %collective-permute-done.11.refs_1_.refs_5_ = bf16[2,640,768]{2,1,0:T(8,128)(2,1)} collective-permute-done((bf16[2,640,768]{2,1,0:T(8,128)(2,1)S(1)}, bf16[2,640,768]{2,1,0:T(8,128)(2,1)}, u32[]{:S(2)}, u32[]{:S(2)}) %collective-permute-start.11) | collective-permute-done | bytes 1966112 | tf_op jit(solution)/shard_map/ppermute | solution.py:943
  142.7 12.6 %collective-permute-done.12 = bf16[1,192,2048]{2,1,0:T(8,128)(2,1)S(1)} collective-permute-done((bf16[1,192,2048]{2,1,0:T(8,128)(2,1)S(1)}, bf16[1,192,2048]{2,1,0:T(8,128)(2,1)S(1)}, u32[]{:S(2)}, u32[]{:S(2)}) %collective-permute-start.12) | collective-permute-done | bytes 786464 | tf_op jit(solution)/shard_map/ppermute | solution.py:912
  158.2 7.0 %memory_projection.1 = (bf16[1024,768]{1,0:T(8,128)(2,1)}, bf16[1024,768]{1,0:T(8,128)(2,1)}) custom-call(s32[8]{0:T(128)} %fusion.61.places, bf16[1024,768]{1,0:T(8,128)(2,1)} %memory.3, bf16[2,640,768]{2,1,0:T(8,128)(2,1)} %copy-done, bf16[2,640,768]{2,1,0:T(8,128)(2,1)} %collective-permute-done.11.refs_1_.refs_5_, bf16[2,640,768]{2,1,0:T(8,128)(2,1)} %copy-done.1, ...), custom_call_target="tpu_custom_call" | custom-call | flops 1000000000 | bytes 1000000 | tf_op jit(solution)/shard_map/memory_projection/pallas_call | solution.py:989
  165.2 16.5 %cross_forward.1 = (bf16[320,768]{1,0:T(8,128)(2,1)}, bf16[320,768]{1,0:T(8,128)(2,1)}, bf16[320,768]{1,0:T(8,128)(2,1)}, f32[12,1,320]{2,1,0:T(1,128)}, f32[320,768]{1,0:T(8,128)}) custom-call(s32[8]{0:T(128)} %fusion.61.places, s32[2]{0:T(128)} %bitcast.149, s32[2]{0:T(128)} %bitcast.152, f32[320,768]{1,0:T(8,128)} %get-tuple-element.125.stream_in, ...), custom_call_target="tpu_custom_call" | custom-call | flops 1000000000 | bytes 1000000 | tf_op jit(solution)/shard_map/cross_forward/pallas_call | solution.py:1003
  186.5 11.1 %mlp_forward.1 = (bf16[320,768]{1,0:T(8,128)(2,1)}, f32[320,2048]{1,0:T(8,128)}, f32[320,2048]{1,0:T(8,128)}, bf16[320,2048]{1,0:T(8,128)(2,1)}, f32[320,768]{1,...) custom-call(s32[8]{0:T(128)} %fusion.61.places, f32[320,768]{1,0:T(8,128)} %get-tuple-element.129.stream_in.stream_two, ...), custom_call_target="tpu_custom_call" | custom-call | flops 1000000000 | bytes 1000000 | tf_op jit(solution)/shard_map/mlp_forward/pallas_call | solution.py:1029
  200.0 7.2 %collective-permute-done.18 = bf16[1,328,768]{2,1,0:T(8,128)(2,1)S(1)} collective-permute-done((bf16[1,328,768]{2,1,0:T(8,128)(2,1)}, bf16[1,328,768]{2,1,0:T(8,128)(2,1)S(1)}, u32[]{:S(2)}, u32[]{:S(2)}) %collective-permute-start.18) | collective-permute-done | bytes 503840 | tf_op jit(solution)/shard_map/ppermute | solution.py:97
  210.3 12.4 %collective-permute-done.19.refs_1_ = bf16[2,328,768]{2,1,0:T(8,128)(2,1)S(1)} collective-permute-done((bf16[2,328,768]{2,1,0:T(8,128)(2,1)S(1)}, bf16[2,328,768]{2,1,0:T(8,128)(2,1)S(1)}, u32[]{:S(2)}, u32[]{:S(2)}) %collective-permute-start.19) | collective-permute-done | bytes 1007648 | tf_op jit(solution)/shard_map/ppermute | solution.py:98
  227.7 24.5 %exit_scores.1 = (bf16[2560,4096]{1,0:T(8,128)(2,1)}, bf16[768,2560]{1,0:T(8,128)(2,1)}, f32[8,2560]{1,0:T(8,128)}) custom-call(s32[18]{0:T(128)} %pad_add_fusion.meta, s32[8]{0:T(128)} %select_reduce_fusion.slot_of, bf16[2,328,768]{2,1,0:T(8,128)(2,1)} %copy-done.6, bf16[2,328,768]{2,1,0:T(8,128)(2,1)} %copy-done.15, bf16[2,328,768]{2,1,0:T(8,128)(2,1)} %copy-done.16, ...), custom_call_target="tpu_custom_call" | custom-call | flops 1000000000 | bytes 1000000 | tf_op jit(solution)/shard_map/exit_scores/pallas_call | solution.py:1054
  267.1 37.2 %exit_grads.1 = (bf16[2,320,768]{2,1,0:T(8,128)(2,1)}, bf16[2,320,768]{2,1,0:T(8,128)(2,1)}, bf16[2,320,768]{2,1,0:T(8,128)(2,1)}, bf16[2,320,768]{2,1,0:T(8,128)(2,1)}, bf16[768,4096]{1,0:T(8,128)(2,1)}) custom-call(s32[18]{0:T(128)} %pad_add_fusion.meta, s32[8]{0:T(128)} %fusion.61.places, bf16[768,4096]{1,0:T(8,128)(2,1)} %all-gather.2.cloned.1.call-done.refs_4_.refs_0_, ...), custom_call_target="tpu_custom_call" | custom-call | flops 1000000000 | bytes 1000000 | tf_op jit(solution)/shard_map/exit_grads/pallas_call | solution.py:1104
  311.5 12.3 %collective-permute-done.30 = bf16[2,320,768]{2,1,0:T(8,128)(2,1)S(1)} collective-permute-done((bf16[2,320,768]{2,1,0:T(8,128)(2,1)}, bf16[2,320,768]{2,1,0:T(8,128)(2,1)S(1)}, u32[]{:S(2)}, u32[]{:S(2)}) %collective-permute-start.30) | collective-permute-done | bytes 983072 | tf_op jit(solution)/shard_map/ppermute | solution.py:109
  326.3 6.8 %collective-permute-done.31 = bf16[320,768]{1,0:T(8,128)(2,1)S(1)} collective-permute-done((bf16[320,768]{1,0:T(8,128)(2,1)S(1)}, bf16[320,768]{1,0:T(8,128)(2,1)S(1)}, u32[]{:S(2)}, u32[]{:S(2)}) %collective-permute-start.31) | collective-permute-done | bytes 491552 | tf_op jit(solution)/shard_map/ppermute | solution.py:121
  334.1 21.4 %mlp_backward.1 = (f32[320,768]{1,0:T(8,128)}, f32[8,768]{1,0:T(8,128)}, bf16[2,192,2048]{2,1,0:T(8,128)(2,1)}, bf16[2,192,2048]{2,1,0:T(8,128)(2,1)}, bf16[2,19...) custom-call(s32[8]{0:T(128)} %fusion.61.places, ...), custom_call_target="tpu_custom_call" | custom-call | flops 1000000000 | bytes 1000000 | tf_op jit(solution)/shard_map/mlp_backward/pallas_call | solution.py:1136
  357.3 8.9 %collective-permute-start.27 = (f32[8,128]{1,0:T(8,128)S(1)}, f32[8,128]{1,0:T(8,128)S(1)}, u32[]{:S(2)}, u32[]{:S(2)}) collective-permute-start(f32[8,128]{1,0:T(8,128)S(1)} %broadcast_in_dim.95), channel_id=1, source_target_pairs={{0,3},{1,2},{2,1},{3,0},{4,7},{5,6},{6,5},{7,4},{8,11},{9,10},{10,... | collective-permute-start | bytes 12296 | tf_op jit(solution)/shard_map/ppermute | solution.py:1097
  366.9 20.6 %cross_attention_backward.1 = (bf16[320,768]{1,0:T(8,128)(2,1)}, bf16[320,768]{1,0:T(8,128)(2,1)}, bf16[1024,768]{1,0:T(8,128)(2,1)}, bf16[1024,768]{1,0:T(8,128)(2,1)}) custom-call(s32[8]{0:T(128)} %fusion.61.places, s32[2]{0:T(128)} %bitcast.150, s32[2]{0:T(128)} %bitcast.153, f32[320,768]{1,0:T(8,128)} %get-tuple-element.156.grad_in, ...), custom_call_target="tpu_custom_call" | custom-call | flops 1000000000 | bytes 1000000 | tf_op jit(solution)/shard_map/cross_attention_backward/pallas_call | solution.py:1167
  392.9 14.5 %cross_backward.1 = (f32[320,768]{1,0:T(8,128)}, f32[8,768]{1,0:T(8,128)}, f32[1024,768]{1,0:T(8,128)}, bf16[2,384,768]{2,1,0:T(8,128)(2,1)}, bf16[2,384,768]{2,...) custom-call(s32[8]{0:T(128)} %fusion.61.places, f32[320,768]{1,0:T(8,128)} %get-tuple-element.156.grad_in, ...), custom_call_target="tpu_custom_call" | custom-call | flops 1000000000 | bytes 1000000 | tf_op jit(solution)/shard_map/cross_backward/pallas_call | solution.py:1198
  408.2 11.2 %self_attention_backward.1 = (bf16[320,768]{1,0:T(8,128)(2,1)}, bf16[320,768]{1,0:T(8,128)(2,1)}, bf16[320,768]{1,0:T(8,128)(2,1)}, bf16[320,768]{1,0:T(8,128)(2,1)}) custom-call(s32[8]{0:T(128)} %fusion.61.places, s32[2]{0:T(128)} %bitcast.151, f32[320,768]{1,0:T(8,128)} %get-tuple-element.178.grad_in, bf16[320,768]{1,0:T(8,128)(2,1)} %get-tuple-element.166.query, ...), custom_call_target="tpu_custom_call" | custom-call | flops 1000000000 | bytes 1000000 | tf_op jit(solution)/shard_map/self_attention_backward/pallas_call | solution.py:1218
  434.6 11.3 %self_backward.1 = (f32[320,768]{1,0:T(8,128)}, bf16[2,416,768]{2,1,0:T(8,128)(2,1)}, bf16[2,416,768]{2,1,0:T(8,128)(2,1)}, bf16[2,416,768]{2,1,0:T(8,128)(2,1)}, bf16[2,416,768]{2,1,0:T(8,128)(2,1)}) custom-call(s32[8]{0:T(128)} %fusion.61.places, f32[320,768]{1,0:T(8,128)} %get-tuple-element.178.grad_in, bf16[320,768]{1,0:T(8,128)(2,1)} %inputs.2, ...), custom_call_target="tpu_custom_call" | custom-call | flops 1000000000 | bytes 1000000 | tf_op jit(solution)/shard_map/self_backward/pallas_call | solution.py:1240
  469.1 7.8 %collective-permute-start.53 = (bf16[48,2048]{1,0:T(8,128)(2,1)S(1)}, bf16[48,2048]{1,0:T(8,128)(2,1)S(1)}, u32[]{:S(2)}, u32[]{:S(2)}) collective-permute-start(bf16[48,2048]{1,0:T(8,128)(2,1)S(1)} %get-tuple-element.216), channel_id=1, source_target_pairs={{0,1},{1,0},{2,3},{3,2},{4,5},{5,4},{6,7},{7,6},{8,9},{9,8},{10,11... | collective-permute-start | bytes 589832 | tf_op jit(solution)/shard_map/ppermute | solution.py:153
  (256 shorter events, 175.4 us)
Async XLA Ops:
  7.2 219.5 %all-gather.2.cloned.1.call-start = ((), (), s32[]{:S(2)}) async-start(), calls=%async_computation.1 | async-start | bytes 7864320 | tf_op jit(solution)/shard_map/all_gather | solution.py:905
  46.9 44.4 %collective-permute-start.7 = (bf16[2,416,768]{2,1,0:T(8,128)(2,1)S(1)}, bf16[2,416,768]{2,1,0:T(8,128)(2,1)}, u32[]{:S(2)}, u32[]{:S(2)}) collective-permute-start(bf16[2,416,768]{2,1,0:T(8,128)(2,1)S(1)} %pad_maximum_fusion.2.refs_0_), channel_id=1, source_target_pairs={{0,16},{4,12},{8,24},{12,4},{16,0},{20,28},{24,8},{28,20},{1,17},{... | collective-permute-start | bytes 3833864 | tf_op jit(solution)/shard_map/ppermute | solution.py:921
  50.4 19.3 %collective-permute-start.3 = (bf16[304,768]{1,0:T(8,128)(2,1)}, bf16[304,768]{1,0:T(8,128)(2,1)S(1)}, u32[]{:S(2)}, u32[]{:S(2)}) collective-permute-start(bf16[304,768]{1,0:T(8,128)(2,1)} %join_wide.1.refs_0_), channel_id=1, source_target_pairs={{0,1},{1,0},{2,3},{3,2},{4,5},{5,4},{6,7},{7,6},{8,9},{9,8},{10,11... | collective-permute-start | bytes 1400840 | tf_op jit(solution)/shard_map/ppermute | solution.py:136
  52.9 34.8 %collective-permute-start.4 = (bf16[304,768]{1,0:T(8,128)(2,1)}, bf16[304,768]{1,0:T(8,128)(2,1)S(1)}, u32[]{:S(2)}, u32[]{:S(2)}) collective-permute-start(bf16[304,768]{1,0:T(8,128)(2,1)} %join_wide.1.refs_0_), channel_id=1, source_target_pairs={{0,2},{1,3},{2,0},{3,1},{4,6},{5,7},{6,4},{7,5},{8,10},{9,11},{10,... | collective-permute-start | bytes 1400840 | tf_op jit(solution)/shard_map/ppermute | solution.py:136
  53.9 33.8 %collective-permute-start.5 = (bf16[304,768]{1,0:T(8,128)(2,1)}, bf16[304,768]{1,0:T(8,128)(2,1)}, u32[]{:S(2)}, u32[]{:S(2)}) collective-permute-start(bf16[304,768]{1,0:T(8,128)(2,1)} %join_wide.1.refs_0_), channel_id=1, source_target_pairs={{0,3},{1,2},{2,1},{3,0},{4,7},{5,6},{6,5},{7,4},{8,11},{9,10},{10,... | collective-permute-start | bytes 1400840 | tf_op jit(solution)/shard_map/ppermute | solution.py:136
  94.2 421.2 %reduce-scatter.2.cloned.1.call-start = ((), (), s32[]{:S(2)}) async-start(), calls=%async_computation.2 | async-start | bytes 7864320 | tf_op jit(solution)/shard_map/reduce_scatter | solution.py:1131
  111.0 28.8 %collective-permute-start.11 = (bf16[2,640,768]{2,1,0:T(8,128)(2,1)S(1)}, bf16[2,640,768]{2,1,0:T(8,128)(2,1)}, u32[]{:S(2)}, u32[]{:S(2)}) collective-permute-start(bf16[2,640,768]{2,1,0:T(8,128)(2,1)S(1)} %pad_maximum_fusion.refs_0_.refs_4_), channel_id=1, source_target_pairs={{0,16},{4,12},{8,24},{12,4},{16,0},{20,28},{24,8},{28,20},{1,17},{... | collective-permute-start | bytes 5898248 | tf_op jit(solution)/shard_map/ppermute | solution.py:943
  156.6 25.1 %collective-permute-start.15 = (bf16[2,192,2048]{2,1,0:T(8,128)(2,1)S(1)}, bf16[2,192,2048]{2,1,0:T(8,128)(2,1)}, u32[]{:S(2)}, u32[]{:S(2)}) collective-permute-start(bf16[2,192,2048]{2,1,0:T(8,128)(2,1)S(1)} %pad_maximum_fusion.1.refs_0_), channel_id=1, source_target_pairs={{0,16},{4,12},{8,24},{12,4},{16,0},{20,28},{24,8},{28,20},{1,17},{... | collective-permute-start | bytes 4718600 | tf_op jit(solution)/shard_map/ppermute | solution.py:986
  156.7 26.1 %collective-permute-start.16 = (bf16[2,192,2048]{2,1,0:T(8,128)(2,1)S(1)}, bf16[2,192,2048]{2,1,0:T(8,128)(2,1)}, u32[]{:S(2)}, u32[]{:S(2)}) collective-permute-start(bf16[2,192,2048]{2,1,0:T(8,128)(2,1)S(1)} %pad_maximum_fusion.1.refs_0_), channel_id=1, source_target_pairs={{0,4},{4,0},{8,12},{12,8},{16,20},{20,16},{24,28},{28,24},{1,5},{5... | collective-permute-start | bytes 4718600 | tf_op jit(solution)/shard_map/ppermute | solution.py:90
  355.5 32.3 %collective-permute-start.32 = (bf16[2,192,2048]{2,1,0:T(8,128)(2,1)}, bf16[2,192,2048]{2,1,0:T(8,128)(2,1)S(1)}, u32[]{:S(2)}, u32[]{:S(2)}) collective-permute-start(bf16[2,192,2048]{2,1,0:T(8,128)(2,1)} %get-tuple-element.148), channel_id=1, source_target_pairs={{0,4},{4,0},{8,12},{12,8},{16,20},{20,16},{24,28},{28,24},{1,5},{5... | collective-permute-start | bytes 4718600 | tf_op jit(solution)/shard_map/ppermute | solution.py:90
  355.6 32.0 %collective-permute-start.33 = (bf16[2,256,768]{2,1,0:T(8,128)(2,1)}, bf16[2,256,768]{2,1,0:T(8,128)(2,1)S(1)}, u32[]{:S(2)}, u32[]{:S(2)}) collective-permute-start(bf16[2,256,768]{2,1,0:T(8,128)(2,1)} %get-tuple-element.154), channel_id=1, source_target_pairs={{0,4},{4,0},{8,12},{12,8},{16,20},{20,16},{24,28},{28,24},{1,5},{5... | collective-permute-start | bytes 2359304 | tf_op jit(solution)/shard_map/ppermute | solution.py:90
  357.3 33.2 %collective-permute-start.27 = (f32[8,128]{1,0:T(8,128)S(1)}, f32[8,128]{1,0:T(8,128)S(1)}, u32[]{:S(2)}, u32[]{:S(2)}) collective-permute-start(f32[8,128]{1,0:T(8,128)S(1)} %broadcast_in_dim.95), channel_id=1, source_target_pairs={{0,3},{1,2},{2,1},{3,0},{4,7},{5,6},{6,5},{7,4},{8,11},{9,10},{10,... | collective-permute-start | bytes 12296 | tf_op jit(solution)/shard_map/ppermute | solution.py:1097
  366.3 24.6 %collective-permute-start.26 = (f32[8,128]{1,0:T(8,128)S(1)}, f32[8,128]{1,0:T(8,128)S(1)}, u32[]{:S(2)}, u32[]{:S(2)}) collective-permute-start(f32[8,128]{1,0:T(8,128)S(1)} %broadcast_in_dim.95), channel_id=1, source_target_pairs={{0,2},{1,3},{2,0},{3,1},{4,6},{5,7},{6,4},{7,5},{8,10},{9,11},{10,... | collective-permute-start | bytes 12296 | tf_op jit(solution)/shard_map/ppermute | solution.py:1097
  366.3 41.2 %collective-permute-start.25 = (f32[8,128]{1,0:T(8,128)S(1)}, f32[8,128]{1,0:T(8,128)S(1)}, u32[]{:S(2)}, u32[]{:S(2)}) collective-permute-start(f32[8,128]{1,0:T(8,128)S(1)} %broadcast_in_dim.95), channel_id=1, source_target_pairs={{0,1},{1,0},{2,3},{3,2},{4,5},{5,4},{6,7},{7,6},{8,9},{9,8},{10,11... | collective-permute-start | bytes 12296 | tf_op jit(solution)/shard_map/ppermute | solution.py:1097
  387.5 31.8 %collective-permute-start.36 = (bf16[2,256,768]{2,1,0:T(8,128)(2,1)}, bf16[2,256,768]{2,1,0:T(8,128)(2,1)}, u32[]{:S(2)}, u32[]{:S(2)}) collective-permute-start(bf16[2,256,768]{2,1,0:T(8,128)(2,1)} %get-tuple-element.173), channel_id=1, source_target_pairs={{0,4},{4,0},{8,12},{12,8},{16,20},{20,16},{24,28},{28,24},{1,5},{5... | collective-permute-start | bytes 2359304 | tf_op jit(solution)/shard_map/ppermute | solution.py:90
  387.8 31.5 %collective-permute-start.37 = (bf16[2,256,768]{2,1,0:T(8,128)(2,1)S(1)}, bf16[2,256,768]{2,1,0:T(8,128)(2,1)}, u32[]{:S(2)}, u32[]{:S(2)}) collective-permute-start(bf16[2,256,768]{2,1,0:T(8,128)(2,1)S(1)} %add_convert_fusion.4), channel_id=1, source_target_pairs={{0,16},{4,12},{8,24},{12,4},{16,0},{20,28},{24,8},{28,20},{1,17},{... | collective-permute-start | bytes 2359304 | tf_op jit(solution)/shard_map/ppermute | solution.py:109
  390.5 36.8 %collective-permute-start.34 = (bf16[2,192,2048]{2,1,0:T(8,128)(2,1)}, bf16[2,192,2048]{2,1,0:T(8,128)(2,1)S(1)}, u32[]{:S(2)}, u32[]{:S(2)}) collective-permute-start(bf16[2,192,2048]{2,1,0:T(8,128)(2,1)} %get-tuple-element.164), channel_id=1, source_target_pairs={{0,4},{4,0},{8,12},{12,8},{16,20},{20,16},{24,28},{28,24},{1,5},{5... | collective-permute-start | bytes 4718600 | tf_op jit(solution)/shard_map/ppermute | solution.py:90
  390.8 36.5 %collective-permute-start.35 = (bf16[2,192,2048]{2,1,0:T(8,128)(2,1)S(1)}, bf16[2,192,2048]{2,1,0:T(8,128)(2,1)}, u32[]{:S(2)}, u32[]{:S(2)}) collective-permute-start(bf16[2,192,2048]{2,1,0:T(8,128)(2,1)S(1)} %add_convert_fusion), channel_id=1, source_target_pairs={{0,16},{4,12},{8,24},{12,4},{16,0},{20,28},{24,8},{28,20},{1,17},{... | collective-permute-start | bytes 4718600 | tf_op jit(solution)/shard_map/ppermute | solution.py:109
  422.7 23.8 %collective-permute-start.56 = (bf16[256,768]{1,0:T(8,128)(2,1)S(1)}, bf16[256,768]{1,0:T(8,128)(2,1)}, u32[]{:S(2)}, u32[]{:S(2)}) collective-permute-start(bf16[256,768]{1,0:T(8,128)(2,1)S(1)} %fusion.9), channel_id=1, source_target_pairs={{0,8},{4,20},{8,0},{12,28},{16,24},{20,4},{24,16},{28,12},{1,9},{5... | collective-permute-start | bytes 1179656 | tf_op jit(solution)/shard_map/ppermute | solution.py:121
  426.3 24.2 %collective-permute-start.47 = (bf16[2,384,768]{2,1,0:T(8,128)(2,1)}, bf16[2,384,768]{2,1,0:T(8,128)(2,1)}, u32[]{:S(2)}, u32[]{:S(2)}) collective-permute-start(bf16[2,384,768]{2,1,0:T(8,128)(2,1)} %add_convert_fusion.2), channel_id=1, source_target_pairs={{0,16},{4,12},{8,24},{12,4},{16,0},{20,28},{24,8},{28,20},{1,17},{... | collective-permute-start | bytes 3538952 | tf_op jit(solution)/shard_map/ppermute | solution.py:109
  432.2 22.3 %collective-permute-start.52 = (bf16[192,2048]{1,0:T(8,128)(2,1)}, bf16[192,2048]{1,0:T(8,128)(2,1)}, u32[]{:S(2)}, u32[]{:S(2)}) collective-permute-start(bf16[192,2048]{1,0:T(8,128)(2,1)} %fusion.4), channel_id=1, source_target_pairs={{0,8},{4,20},{8,0},{12,28},{16,24},{20,4},{24,16},{28,12},{1,9},{5... | collective-permute-start | bytes 2359304 | tf_op jit(solution)/shard_map/ppermute | solution.py:121
  434.5 21.5 %collective-permute-start.46 = (bf16[2,384,768]{2,1,0:T(8,128)(2,1)}, bf16[2,384,768]{2,1,0:T(8,128)(2,1)}, u32[]{:S(2)}, u32[]{:S(2)}) collective-permute-start(bf16[2,384,768]{2,1,0:T(8,128)(2,1)} %get-tuple-element.193), channel_id=1, source_target_pairs={{0,4},{4,0},{8,12},{12,8},{16,20},{20,16},{24,28},{28,24},{1,5},{5... | collective-permute-start | bytes 3538952 | tf_op jit(solution)/shard_map/ppermute | solution.py:90
  446.5 41.3 %collective-permute-start.39 = (bf16[2,416,768]{2,1,0:T(8,128)(2,1)}, bf16[2,416,768]{2,1,0:T(8,128)(2,1)S(1)}, u32[]{:S(2)}, u32[]{:S(2)}) collective-permute-start(bf16[2,416,768]{2,1,0:T(8,128)(2,1)} %get-tuple-element.189), channel_id=1, source_target_pairs={{0,4},{4,0},{8,12},{12,8},{16,20},{20,16},{24,28},{28,24},{1,5},{5... | collective-permute-start | bytes 3833864 | tf_op jit(solution)/shard_map/ppermute | solution.py:90
  463.1 24.7 %collective-permute-start.41 = (bf16[2,416,768]{2,1,0:T(8,128)(2,1)S(1)}, bf16[2,416,768]{2,1,0:T(8,128)(2,1)S(1)}, u32[]{:S(2)}, u32[]{:S(2)}) collective-permute-start(bf16[2,416,768]{2,1,0:T(8,128)(2,1)S(1)} %add_convert_fusion.1), channel_id=1, source_target_pairs={{0,16},{4,12},{8,24},{12,4},{16,0},{20,28},{24,8},{28,20},{1,17},{... | collective-permute-start | bytes 3833864 | tf_op jit(solution)/shard_map/ppermute | solution.py:109
  (67 other events, 764.2 us)
Sparse Core Ops, SparseCore 0:
  94.3 119.3 all-gather.1
  311.6 117.2 reduce-scatter.1

commit v3 on v2

--- a/solution.py
+++ b/solution.py
@@ -105,14 +105,18 @@
 
 
 def scatter_far(sent, kept, count):
-    far = (sent[0].astype(F32) + sent[1].astype(F32)).astype(BF16)
+    far = sent[0] + sent[1]
     came = lax.ppermute(far, "wide", stage_pairs(count)[-1])
     return far, came, kept
 
 
 def scatter_near(came, kept, count):
-    held = kept[0].astype(F32) + kept[1].astype(F32) + came.astype(F32)
     *rest, last = stage_pairs(count)[-2::-1]
+    terms = (*kept, came)
+    if not rest:
+        far = sum(term[1].astype(F32) for term in terms).astype(BF16)
+        return far, lax.ppermute(far, "wide", last), sum(term[0].astype(F32) for term in terms)
+    held = sum(term.astype(F32) for term in terms)
     for pairs in rest:
         half = held.shape[0] // 2
         sent = lax.ppermute(held[half:].astype(BF16), "wide", pairs)
@@ -147,11 +151,15 @@
 
 
 def scatter_narrow(blocks, narrow, count):
-    total = pick(blocks, narrow)
-    for step in range(1, count):
-        sent = pick(blocks, narrow ^ step).astype(BF16)
-        total = total + lax.ppermute(sent, "narrow", narrow_pairs(count, step)).astype(F32)
-    return total
+    return [pick(blocks, narrow)] + [
+        lax.ppermute(pick(blocks, narrow ^ step).astype(BF16), "narrow", narrow_pairs(count, step))
+        for step in range(1, count)
+    ]
+
+
+def add_terms(terms, *others):
+    terms = lax.optimization_barrier((*terms, *others))[: len(terms)]
+    return sum(term.astype(F32) for term in terms)
 
 
 def weight_copies(places, parts, start, target, rows, sems):
@@ -170,11 +178,25 @@
     return copies
 
 
-def store_blocks(places, value_ref, start, rows, parts):
+def block_copies(places, value, start, rows, parts, sems):
     size = parts[0].shape[0]
+    copies = []
     for slot in range(len(parts) * size):
         place = pl.multiple_of(places[slot] * rows, 8)
-        parts[slot // size][slot % size, pl.ds(start, rows), :] = value_ref[pl.ds(place, rows), :]
+        copies.append(
+            pltpu.make_async_copy(
+                value.at[pl.ds(place, rows), :],
+                parts[slot // size].at[slot % size, pl.ds(start, rows), :],
+                sems.at[slot],
+            )
+        )
+    return copies
+
+
+def send_off(copies, more):
+    for copy in more:
+        copy.start()
+    copies += more
 
 
 def norm_scale(values):
@@ -200,19 +222,20 @@
 
 
 def fill_self_bias(bias, lengths):
-    count = bias.shape[1]
+    count = bias.shape[1] // 2
     places, segment = query_segments(lengths, count)
     low = jnp.zeros((1, count), jnp.int32)
     edge = jnp.int32(0)
     for pair in range(lengths.shape[0]):
         edge = edge + lengths[pair]
         low = jnp.where(segment == pair + 1, edge, low)
-    keys = lax.broadcasted_iota(jnp.int32, bias.shape, 0)
-    bias[...] = jnp.where((keys >= low) & (keys <= places), 0.0, NEGATIVE)
+    keys = lax.broadcasted_iota(jnp.int32, (bias.shape[0], count), 0)
+    one = jnp.where((keys >= low) & (keys <= places), 0.0, NEGATIVE)
+    bias[...] = jnp.concatenate([one, one], axis=1)
 
 
 def fill_cross_bias(bias, lengths, sources):
-    count = bias.shape[1]
+    count = bias.shape[1] // 2
     places, segment = query_segments(lengths, count)
     low = jnp.zeros((1, count), jnp.int32)
     high = jnp.full((1, count), bias.shape[0], jnp.int32)
@@ -221,6 +244,8 @@
         low = jnp.where(segment == pair, edge, low)
         edge = edge + sources[pair]
         high = jnp.where(segment == pair, edge, high)
+    low = jnp.concatenate([low, low], axis=1)
+    high = jnp.concatenate([high, high], axis=1)
     keys = lax.broadcasted_iota(jnp.int32, bias.shape, 0)
     bias[...] = jnp.where((keys >= low) & (keys < high), 0.0, NEGATIVE)
 
@@ -229,62 +254,53 @@
     return lax.broadcasted_iota(jnp.int32, (1, width), 1) < width // 2
 
 
-def attend(queries, keys, values, bias, outputs, totals):
+def apart(values, chosen):
+    return jnp.concatenate([jnp.where(chosen, values, 0), jnp.where(chosen, 0, values)], axis=0)
+
+
+def together(values, chosen):
+    count = values.shape[0] // 2
+    return jnp.where(chosen, values[:count], values[count:])
+
+
+def attend(queries, keys, values, bias, outputs, totals, unroll):
     width = 2 * (queries.shape[1] // HEADS)
     chosen = first_half(width)
 
     def pair_of_heads(pair, carry):
         columns = pl.ds(pl.multiple_of(pair * width, width), width)
-        query = queries[:, columns]
-        key = keys[:, columns]
-        value = values[:, columns].T
-        halves = []
-        for side in range(2):
-            own = jnp.where(chosen if side == 0 else ~chosen, query, 0)
-            scores = nt(key, own) + bias[...]
-            highest = jnp.max(scores, axis=0, keepdims=True)
-            raised = jnp.exp(scores - highest)
-            summed = jnp.sum(raised, axis=0, keepdims=True)
-            weights = (raised * (1.0 / summed)).astype(BF16)
-            totals[2 * pair + side] = highest + jnp.log(summed)
-            halves.append(nn(value[side * width // 2 : (side + 1) * width // 2], weights))
-        outputs[:, columns] = jnp.concatenate(halves, axis=0).T.astype(BF16)
+        scores = nt(keys[:, columns], apart(queries[:, columns], chosen)) + bias[...]
+        highest = jnp.max(scores, axis=0, keepdims=True)
+        raised = jnp.exp(scores - highest)
+        summed = jnp.sum(raised, axis=0, keepdims=True)
+        totals[pair] = highest + jnp.log(summed)
+        weights = (raised * (1.0 / summed)).astype(BF16)
+        mixed = nn(values[:, columns].T, weights).T
+        outputs[:, columns] = together(mixed, chosen).astype(BF16)
         return carry
 
-    lax.fori_loop(0, HEADS // 2, pair_of_heads, 0)
-
-
-def attend_back(queries, keys, values, bias, totals, grads, query_low, key_low, value_low):
+    lax.fori_loop(0, HEADS // 2, pair_of_heads, 0, unroll=unroll)
+
+
+def attend_back(
+    queries, keys, values, bias, totals, grads, query_low, key_low, value_low, first, last
+):
     width = 2 * (queries.shape[1] // HEADS)
     chosen = first_half(width)
 
-    def pair_of_heads(pair, carry):
-        columns = pl.ds(pl.multiple_of(pair * width, width), width)
-        query = queries[:, columns]
+    for pair in range(first, last):
+        columns = slice(pair * width, (pair + 1) * width)
+        result = slice((pair - first) * width, (pair - first + 1) * width)
+        query, grad = apart(queries[:, columns], chosen), apart(grads[:, columns], chosen)
         key = keys[:, columns]
-        value = values[:, columns]
-        grad = grads[:, columns]
-        key_across = key.T
-        query_parts, key_parts, value_parts = [], [], []
-        for side in range(2):
-            mine = chosen if side == 0 else ~chosen
-            scores = nt(key, jnp.where(mine, query, 0)) + bias[...]
-            probs = jnp.exp(scores - totals[2 * pair + side])
-            prob_grad = nt(value, jnp.where(mine, grad, 0))
-            value_parts.append(nn(probs.astype(BF16), grad))
-            weighted = probs * prob_grad
-            centre = jnp.sum(weighted, axis=0, keepdims=True)
-            score_grad = (weighted - probs * centre).astype(BF16)
-            key_parts.append(nn(score_grad, query))
-            query_parts.append(
-                nn(key_across[side * width // 2 : (side + 1) * width // 2], score_grad)
-            )
-        query_low[:, columns] = jnp.concatenate(query_parts, axis=0).T.astype(BF16)
-        key_low[:, columns] = jnp.where(chosen, key_parts[0], key_parts[1]).astype(BF16)
-        value_low[:, columns] = jnp.where(chosen, value_parts[0], value_parts[1]).astype(BF16)
-        return carry
-
-    lax.fori_loop(0, HEADS // 2, pair_of_heads, 0)
+        probs = jnp.exp(nt(key, query) + bias[...] - totals[pair])
+        prob_grad = nt(values[:, columns], grad)
+        value_low[:, result] = nn(probs.astype(BF16), grad).astype(BF16)
+        weighted = probs * prob_grad
+        centre = jnp.sum(weighted, axis=0, keepdims=True)
+        score_grad = (weighted - probs * centre).astype(BF16)
+        key_low[:, result] = nn(score_grad, query).astype(BF16)
+        query_low[:, result] = together(nn(key.T, score_grad).T, chosen).astype(BF16)
 
 
 def block_rows(weights, parts):
@@ -296,6 +312,23 @@
     for ref in refs[:-1]:
         refs[-1][start : start + ref.shape[0], :] = ref[...]
         start += ref.shape[0]
+
+
+def join_self_kernel(owner, lengths, gains, *refs):
+    join_kernel(*refs)
+    pack = refs[-1]
+    shard, width = gains.shape[1], pack.shape[1]
+    total = jnp.int32(0)
+    for pair in range(lengths.shape[0]):
+        total = total + lengths[pair]
+    spot = lax.broadcasted_iota(jnp.int32, (8, shard), 0)
+    high, low = (total // 16).astype(F32), (total % 16).astype(F32)
+    own = jnp.concatenate([gains[...].astype(F32), jnp.zeros((8 - gains.shape[0], shard), F32)], axis=0)
+    own = jnp.where(spot == 4, high, jnp.where(spot == 5, low, own)).astype(BF16)
+    row = lax.broadcasted_iota(jnp.int32, (shard, width), 0)
+    column = lax.broadcasted_iota(jnp.int32, (shard, width), 1)
+    spread = (row + owner[0] * shard == column).astype(BF16)
+    pack[pack.shape[0] - 8 :, :] = nn(own, spread).astype(BF16)
 
 
 def join_rows(*members):
@@ -404,7 +437,7 @@
     query[...] = nn(low, weights[0]).astype(BF16)
     key[...] = nn(low, weights[1]).astype(BF16)
     value[...] = nn(low, weights[2]).astype(BF16)
-    attend(query, key, value, bias, attended, totals)
+    attend(query, key, value, bias, attended, totals, HEADS // 2)
     stream[...] = values + nn(attended[...], weights[3])
 
 
@@ -438,7 +471,7 @@
     for copy in copies:
         copy.wait()
     query[...] = nn(low, weights[0]).astype(BF16)
-    attend(query, key, value, bias, attended, totals)
+    attend(query, key, value, bias, attended, totals, HEADS // 4)
     stream[...] = values + nn(attended[...], weights[1])
 
 
@@ -574,42 +607,46 @@
         stats[...] = jnp.where(rows == 1, 1.0, 0.0)
 
 
-def exit_grads_kernel(meta, places, *refs, vocab):
-    source, raised, across, factors = refs[:4]
-    parts = refs[4:8]
-    table_grad = refs[8]
-    table, total, token_grad, landed, table_sem, sems = refs[9:]
+def logit_grads(meta, raised, factors, first, width, vocab):
+    tile = raised.shape[0]
+    columns = jnp.concatenate(
+        [factors[...], jnp.zeros((LANES - factors.shape[0], tile), F32)], axis=0
+    ).T
+    factor, at_target = columns[:, 0:1], columns[:, 1:2]
+    wanted = columns[:, 2:3].astype(jnp.int32) - meta[META_WIDE] * vocab
+    wanted = jnp.where(wanted < vocab, wanted, -1) - first
+    lanes = lax.broadcasted_iota(jnp.int32, (tile, width), 1)
+
+    def chunk(start):
+        part = raised[:, start : start + width].astype(F32) * factor
+        return jnp.where(lanes == wanted - start, at_target, part).astype(BF16)
+
+    return chunk
+
+
+def exit_tokens_kernel(meta, places, *refs, vocab):
+    source, raised, factors = refs[:3]
+    parts = refs[3:7]
+    table, token_grad, landed, table_sem, sems = refs[7:]
     size = parts[0].shape[0]
     members = 4 * size
     count = parts[0].shape[1]
     starts, counts = META_LISTS, META_LISTS + members
     step = pl.program_id(0)
     tile = raised.shape[0]
-    width = raised.shape[1]
 
     @pl.when(step == 0)
     def load():
         whole = pltpu.make_async_copy(source, table, table_sem)
         whole.start()
-        total[...] = jnp.zeros_like(total)
         whole.wait()
 
-    @pl.when(step < meta[META_TILES] // (tile // ROW_TILE))
+    @pl.when(step < meta[META_TILES])
     def compute():
-        columns = jnp.concatenate(
-            [factors[...], jnp.zeros((LANES - factors.shape[0], tile), F32)], axis=0
-        ).T
-        factor, at_target = columns[:, 0:1], columns[:, 1:2]
-        wanted = columns[:, 2:3].astype(jnp.int32) - meta[META_WIDE] * vocab
-        wanted = jnp.where(wanted < vocab, wanted, -1)
-        lanes = lax.broadcasted_iota(jnp.int32, (tile, VOCAB_TILE), 1)
+        chunk = logit_grads(meta, raised, factors, 0, VOCAB_TILE, vocab)
         grad = jnp.zeros((tile, token_grad.shape[1]), F32)
-        for first in range(0, width, VOCAB_TILE):
-            chunk = slice(first, first + VOCAB_TILE)
-            part = raised[:, chunk].astype(F32) * factor
-            part = jnp.where(lanes == wanted - first, at_target, part).astype(BF16)
-            grad = grad + nt(part, table[:, chunk])
-            total[:, chunk] += nn(across[...], part)
+        for first in range(0, raised.shape[1], VOCAB_TILE):
+            grad = grad + nt(chunk(first), table[:, first : first + VOCAB_TILE])
         token_grad[pl.ds(pl.multiple_of(step * tile, tile), tile), :] = grad.astype(BF16)
 
     @pl.when(step == pl.num_programs(0) - 1)
@@ -628,9 +665,28 @@
             )
             copy.start()
             copies.append(copy)
-        table_grad[...] = total[...].astype(BF16)
         for copy in copies[-2:]:
             copy.wait()
+
+
+def exit_table_kernel(meta, raised, across, factors, *refs, first, vocab):
+    table_grad, total = refs[-2:]
+    step = pl.program_id(0)
+    width = min(VOCAB_TILE, raised.shape[1])
+
+    @pl.when(step == 0)
+    def clear():
+        total[...] = jnp.zeros_like(total)
+
+    @pl.when(step < meta[META_TILES])
+    def compute():
+        chunk = logit_grads(meta, raised, factors, first, width, vocab)
+        for start in range(0, raised.shape[1], width):
+            total[:, start : start + width] += nn(across[...], chunk(start))
+
+    @pl.when(step == pl.num_programs(0) - 1)
+    def finish():
+        table_grad[...] = total[...].astype(BF16)
 
 
 def mlp_backward_kernel(
@@ -639,20 +695,22 @@
     parts, down_parts = refs[:4], refs[4:8]
     stream_grad, gains = refs[8:10]
     grad_parts, down_grad_parts = refs[10:14], refs[14:18]
-    weights, down, gate_low, up_low, result, down_result, sems, down_sems = refs[18:]
+    weights, down, gate_low, up_low, result, down_result, sems, down_sems, out_sems = refs[18:]
     rows, down_rows = block_rows(weights, parts), block_rows(down, down_parts)
-    copies = weight_copies(
+    first = weight_copies(
         places, down_parts, down_parts[0].shape[1] - down_rows, down, down_rows, down_sems
     )
-    copies += weight_copies(places, parts, 0, weights, rows, sems)
-    for copy in copies:
+    last = weight_copies(places, parts, 0, weights, rows, sems)
+    for copy in first + last:
         copy.start()
     stream_back, exit_gain_grad = norm_back(stream_three[...], gain[3:4], grad_in[...])
     branch = stream_back.astype(BF16)
-    for copy in copies:
+    for copy in first:
         copy.wait()
     width = weights.shape[2]
     step = width // 4
+    normed_across = normed[...].T
+    sent = []
     for part in range(4):
         columns = pl.ds(part * step, step)
         gate_pre = gate[:, columns]
@@ -664,28 +722,38 @@
         )
         gate_low[:, columns] = (hidden_grad * up_pre * slope).astype(BF16)
         up_low[:, columns] = (hidden_grad * (0.5 * gate_pre * (1.0 + bent))).astype(BF16)
+        result[0, :, columns] = nn(normed_across, gate_low[:, columns]).astype(BF16)
+        result[1, :, columns] = nn(normed_across, up_low[:, columns]).astype(BF16)
+    for matrix in range(2):
+        send_off(
+            sent,
+            block_copies(
+                places, result.at[matrix], matrix * rows, rows, grad_parts, out_sems.at[matrix]
+            ),
+        )
+    for part in range(4):
+        columns = pl.ds(part * step, step)
+        down_result[columns, :] = nn(hidden[:, columns].T, branch).astype(BF16)
+    send_off(
+        sent, block_copies(places, down_result, 0, down_rows, down_grad_parts, out_sems.at[2])
+    )
+    for copy in last:
+        copy.wait()
     normed_grad = nt(gate_low[...], weights[0]) + nt(up_low[...], weights[1])
     branch_in, gain_grad = norm_back(stream_two[...], gain[2:3], normed_grad)
     stream_grad[...] = stream_back + branch_in
     gains[...] = jnp.concatenate(
         [gain_grad, exit_gain_grad, jnp.zeros((6, gain_grad.shape[1]), F32)], axis=0
     )
-    for matrix, low in enumerate((gate_low, up_low)):
-        for part in range(4):
-            columns = pl.ds(part * step, step)
-            result[:, columns] = tn(normed[...], low[:, columns]).astype(BF16)
-        store_blocks(places, result, matrix * rows, rows, grad_parts)
-    for part in range(4):
-        columns = pl.ds(part * step, step)
-        down_result[columns, :] = tn(hidden[:, columns], branch).astype(BF16)
-    store_blocks(places, down_result, 0, down_rows, down_grad_parts)
-
-
-def cross_attention_backward_kernel(
+    for copy in sent:
+        copy.wait()
+
+
+def cross_attention_first_kernel(
     places, lengths, sources, grad_in, query, key, value, totals, *refs,
 ):
     parts = refs[:4]
-    branch, query_low, key_low, value_low, weights, bias, attended_grad, sems = refs[4:]
+    branch, attended_grad, query_low, key_low, value_low, weights, bias, sems = refs[4:]
     rows = block_rows(weights, parts)
     copies = weight_copies(places, parts, 3 * rows, weights, rows, sems)
     for copy in copies:
@@ -696,70 +764,111 @@
         copy.wait()
     attended_grad[...] = nt(branch[...], weights[0]).astype(BF16)
     attend_back(
-        query, key, value, bias, totals, attended_grad, query_low, key_low, value_low
-    )
+        query, key, value, bias, totals, attended_grad, query_low, key_low, value_low,
+        0, HEADS // 4,
+    )
+
+
+def cross_attention_last_kernel(
+    lengths, sources, attended_grad, query, key, value, totals,
+    first_query, first_key, first_value, query_low, key_low, value_low, bias,
+):
+    middle = first_query.shape[1]
+    fill_cross_bias(bias, lengths, sources)
+    attend_back(
+        query, key, value, bias, totals, attended_grad,
+        query_low.at[:, middle:], key_low.at[:, middle:], value_low.at[:, middle:],
+        HEADS // 4, HEADS // 2,
+    )
+    query_low[:, :middle] = first_query[...]
+    key_low[:, :middle] = first_key[...]
+    value_low[:, :middle] = first_value[...]
 
 
 def cross_backward_kernel(
-    places, grad_in, stream_in, gain, normed, memory, attended,
+    places, grad_in, stream_in, gain, normed, memory, attended, self_attended,
     branch, query_low, key_low, value_low, *refs,
 ):
     parts = refs[:4]
-    stream_grad, gains, memory_grad = refs[4:7]
-    grad_parts = refs[7:11]
-    weights, result, sems = refs[11:]
+    stream_grad, gains, memory_grad, self_branch = refs[4:8]
+    grad_parts = refs[8:12]
+    weights, results, sems, out_sems = refs[12:]
     rows = block_rows(weights, parts)
     copies = weight_copies(places, parts, 0, weights, rows, sems)
     for copy in copies:
         copy.start()
-    pairs = ((normed, query_low), (memory, key_low), (memory, value_low), (attended, branch))
-    for matrix, (left, right) in enumerate(pairs):
-        result[...] = tn(left[...], right[...]).astype(BF16)
-        store_blocks(places, result, matrix * rows, rows, grad_parts)
+    sent = []
+
+    def weight_grad(matrix, left_across, right):
+        results[matrix] = nn(left_across, right[...]).astype(BF16)
+        send_off(
+            sent,
+            block_copies(
+                places, results.at[matrix], matrix * rows, rows, grad_parts, out_sems.at[matrix]
+            ),
+        )
+
+    memory_across = memory[...].T
+    weight_grad(1, memory_across, key_low)
+    weight_grad(2, memory_across, value_low)
+    weight_grad(0, normed[...].T, query_low)
+    weight_grad(3, attended[...].T, branch)
     for copy in copies:
         copy.wait()
     normed_grad = nt(query_low[...], weights[0])
     branch_in, gain_grad = norm_back(stream_in[...], gain[1:2], normed_grad)
-    stream_grad[...] = grad_in[...] + branch_in
+    total = grad_in[...] + branch_in
+    stream_grad[...] = total
+    self_branch[...] = total.astype(BF16)
+    weight_grad(4, self_attended[...].T, self_branch)
     gains[...] = jnp.broadcast_to(gain_grad, gains.shape)
     memory_grad[...] = nt(key_low[...], weights[1]) + nt(value_low[...], weights[2])
+    for copy in sent:
+        copy.wait()
 
 
 def self_attention_backward_kernel(
-    places, lengths, grad_in, query, key, value, totals, *refs,
+    places, lengths, branch, query, key, value, totals, *refs,
 ):
     parts = refs[:4]
-    branch, query_low, key_low, value_low, weights, bias, attended_grad, sems = refs[4:]
+    query_low, key_low, value_low, weights, bias, attended_grad, sems = refs[4:]
     rows = block_rows(weights, parts)
     copies = weight_copies(places, parts, 3 * rows, weights, rows, sems)
     for copy in copies:
         copy.start()
     fill_self_bias(bias, lengths)
-    branch[...] = grad_in[...].astype(BF16)
     for copy in copies:
         copy.wait()
     attended_grad[...] = nt(branch[...], weights[0]).astype(BF16)
     attend_back(
-        query, key, value, bias, totals, attended_grad, query_low, key_low, value_low
+        query, key, value, bias, totals, attended_grad, query_low, key_low, value_low,
+        0, HEADS // 2,
     )
 
 
 def self_backward_kernel(
-    places, grad_in, inputs, gain, normed, attended, cross_gains, mlp_gains,
-    branch, query_low, key_low, value_low, *refs,
+    places, grad_in, inputs, gain, normed, cross_gains, mlp_gains,
+    query_low, key_low, value_low, *refs,
 ):
     parts = refs[:4]
     stream_grad = refs[4]
     grad_parts = refs[5:9]
-    weights, result, sems = refs[9:]
+    weights, results, terms, sems, out_sems, term_sems = refs[9:]
     rows = block_rows(weights, parts)
+    size = grad_parts[0].shape[0]
     copies = weight_copies(places, parts, 0, weights, rows, sems)
     for copy in copies:
         copy.start()
-    pairs = ((normed, query_low), (normed, key_low), (normed, value_low), (attended, branch))
-    for matrix, (left, right) in enumerate(pairs):
-        result[...] = tn(left[...], right[...]).astype(BF16)
-        store_blocks(places, result, matrix * rows, rows, grad_parts)
+    sent = []
+    normed_across = normed[...].T
+    for matrix, low in enumerate((query_low, key_low, value_low)):
+        results[matrix] = nn(normed_across, low[...]).astype(BF16)
+        send_off(
+            sent,
+            block_copies(
+                places, results.at[matrix], matrix * rows, rows, grad_parts, out_sems.at[matrix]
+            ),
+        )
     for copy in copies:
         copy.wait()
     normed_grad = (
@@ -770,14 +879,25 @@
     branch_in, gain_grad = norm_back(inputs[...].astype(F32), gain[0:1], normed_grad)
     stream_grad[...] = grad_in[...] + branch_in
     spot = lax.broadcasted_iota(jnp.int32, (8, gain_grad.shape[1]), 0)
-    terms = jnp.where(spot == 0, gain_grad, 0.0)
-    terms = jnp.where(spot == 1, cross_gains[0:1], terms)
-    terms = jnp.where(spot == 2, mlp_gains[0:1], terms)
-    terms = jnp.where(spot == 3, mlp_gains[1:2], terms).astype(BF16)
-    for part in grad_parts:
-        for slot in range(part.shape[0]):
-            for start in range(4 * rows, part.shape[1], 8):
-                part[slot, start : start + 8, :] = terms
+    row = jnp.where(spot == 0, gain_grad, 0.0)
+    row = jnp.where(spot == 1, cross_gains[0:1], row)
+    row = jnp.where(spot == 2, mlp_gains[0:1], row)
+    row = jnp.where(spot == 3, mlp_gains[1:2], row).astype(BF16)
+    for start in range(0, terms.shape[0], 8):
+        terms[start : start + 8] = row
+    send_off(
+        sent,
+        [
+            pltpu.make_async_copy(
+                terms,
+                grad_parts[slot // size].at[slot % size, pl.ds(3 * rows, terms.shape[0]), :],
+                term_sems.at[slot],
+            )
+            for slot in range(4 * size)
+        ],
+    )
+    for copy in sent:
+        copy.wait()
 
 
 def per_device(
@@ -859,7 +979,7 @@
                 out_specs=VMEM,
                 out_shape=like((pieces[0].shape[0] * len(pieces), pieces[0].shape[1]), BF16),
                 compiler_params=PARAMS,
-                cost_estimate=work(1),
+                cost_estimate=work(30),
                 name="line_block",
             )(narrow[None], *pieces)
         ordered, start, members = in_line_order(pieces, narrow), 0, []
@@ -873,6 +993,16 @@
     count = jnp.sum(lengths)
     owner = wide * narrow_count + narrow
     gain_shards = jnp.stack([self_gain, cross_gain, mlp_gain, exit_gain])
+    def join_self():
+        return pl.pallas_call(
+            join_self_kernel,
+            in_specs=[SMEM] * 2 + [VMEM] * 5,
+            out_specs=VMEM,
+            out_shape=like((sum(self_sizes), model), BF16),
+            cost_estimate=work(1),
+            name="join_self",
+        )(owner[None], lengths, gain_shards, self_query, self_key, self_value, self_out)
+
     numbers = jnp.broadcast_to(
         jnp.stack([count // 16, count % 16])[:, None], (2, shard)
     ).astype(BF16)
@@ -880,7 +1010,11 @@
     own_rows = jnp.tile(own_rows, (1, model // shard))
     own_columns = jnp.arange(model, dtype=jnp.int32)[None, :] // shard == owner
     own_rows = jnp.where(own_columns, own_rows, 0)
-    self_pack = join_rows(self_query, self_key, self_value, self_out, own_rows)
+    self_pack = (
+        join_self()
+        if aligned
+        else join_rows(self_query, self_key, self_value, self_out, own_rows)
+    )
     members = (cross_query, cross_key, cross_value, cross_out, mlp_down)
     if aligned:
         wide_rows = -(-2 * hidden_width // model) * shard
@@ -918,6 +1052,8 @@
         cross_line = gather_narrow(join_rows(*members), narrow_count)
         gate_line = gather_narrow(join_rows(mlp_gate, mlp_up), narrow_count)
     self_held = gather_early(self_block)
+    if aligned:
+        self_held = tie(self_held, joined_line[1])
     self_came = lax.ppermute(self_held, "wide", last)
     if aligned:
         joined_line = lax.optimization_barrier((*joined_line, self_held))[:narrow_count]
@@ -942,7 +1078,7 @@
     cross_held = gather_early(tie(cross_block, self_came))
     cross_came = lax.ppermute(cross_held, "wide", last)
 
-    head_rows = like((HEADS, 1, tokens), F32)
+    head_rows = like((HEADS // 2, 1, 2 * tokens), F32)
     activation = like((tokens, model), BF16)
     stream_like = like((tokens, model), F32)
     matrix_sems = pltpu.SemaphoreType.DMA((kernel_count, 4))
@@ -959,7 +1095,7 @@
         scratch_shapes=[
             pltpu.VMEM((4, model, model), BF16),
             pltpu.VMEM((kernel_count, 8 * narrow_count * wide_count // kernel_count, model), BF16),
-            pltpu.VMEM((tokens, tokens), F32),
+            pltpu.VMEM((tokens, 2 * tokens), F32),
             matrix_sems,
             pltpu.SemaphoreType.DMA((kernel_count,)),
         ],
@@ -974,7 +1110,7 @@
     ).astype(jnp.int32)
     extents = (numbers + 15) // 16 * 16
     starts = jnp.sum(jnp.where(ids[None, :] < ids[:, None], extents[None, :], 0), axis=1)
-    needed = (jnp.sum(extents) + GRAD_TILE - 1) // GRAD_TILE * (GRAD_TILE // ROW_TILE)
+    needed = (jnp.sum(extents) + GRAD_TILE - 1) // GRAD_TILE * (1)
     meta = jnp.concatenate([jnp.stack([wide, needed]), starts, numbers])
     slot_of = jnp.sum(jnp.where(order, ids[None, :], 0), axis=1)
 
@@ -1007,7 +1143,7 @@
         out_shape=[activation] * 3 + [head_rows, stream_like],
         scratch_shapes=[
             pltpu.VMEM((2, model, model), BF16),
-            pltpu.VMEM((slots, tokens), F32),
+            pltpu.VMEM((slots, 2 * tokens), F32),
             pltpu.SemaphoreType.DMA((2, kernel_count, 1)),
         ],
         compiler_params=PARAMS,
@@ -1047,9 +1183,9 @@
 
     exit_parts = gather_wide(normed_four, wide_count)
     group = tokens * wide_count
-    tiles = -(-group // GRAD_TILE) * (GRAD_TILE // ROW_TILE)
+    tiles = -(-group // GRAD_TILE) * (1)
     kept = lambda i, meta: jnp.minimum(i, meta[META_TILES] - 1)
-    kept_grad = lambda i, meta: jnp.minimum(i, meta[META_TILES] * ROW_TILE // GRAD_TILE - 1)
+    kept_grad = lambda i, meta: jnp.minimum(i, meta[META_TILES] * 1 - 1)
 
     raised, tokens_across, stats = pl.pallas_call(
         functools.partial(exit_scores_kernel, vocab=vocab, scale=scale),
@@ -1078,7 +1214,7 @@
             like((8, tiles * ROW_TILE), F32),
         ],
         compiler_params=PARAMS,
-        cost_estimate=work(1),
+        cost_estimate=work(52),
         name="exit_scores",
     )(meta, slot_of, *exit_parts, table)
 
@@ -1092,51 +1228,75 @@
     log_total = joint[0] + jnp.log(joint[1])
     picked, group_weight = joint[2], stats[3]
     loss_part = jnp.full((8, LANES), jnp.sum(group_weight * (log_total - picked)), F32)
-    loss_all = loss_part
-    for step in range(1, narrow_count):
-        loss_all = loss_all + lax.ppermute(loss_part, "narrow", narrow_pairs(narrow_count, step))
-    mean_loss = loss_all[0, 0] / slot_total
 
     factor = jnp.exp(own_peak - log_total) * (group_weight * scale)
     at_target = (jnp.exp(picked - log_total) - 1.0) * (group_weight * scale)
     factors = jnp.concatenate([factor[None], at_target[None], stats[4:5], stats[3:]], axis=0)
     token_part = like((wide_count // 4, tokens, model), BF16)
-    *exit_grads, table_grad = pl.pallas_call(
-        functools.partial(exit_grads_kernel, vocab=vocab),
+    exit_grads = pl.pallas_call(
+        functools.partial(exit_tokens_kernel, vocab=vocab),
         grid_spec=pltpu.PrefetchScalarGridSpec(
             num_scalar_prefetch=2,
-            grid=(tiles * ROW_TILE // GRAD_TILE,),
+            grid=(tiles,),
             in_specs=[
                 ANY,
-                pl.BlockSpec((GRAD_TILE, padded), lambda i, meta, slots: (kept_grad(i, meta), 0)),
-                pl.BlockSpec((model, GRAD_TILE), lambda i, meta, slots: (0, kept_grad(i, meta))),
-                pl.BlockSpec((8, GRAD_TILE), lambda i, meta, slots: (0, i)),
+                pl.BlockSpec((ROW_TILE, padded), lambda i, meta, slots: (kept(i, meta), 0)),
+                pl.BlockSpec((8, ROW_TILE), lambda i, meta, slots: (0, i)),
             ],
-            out_specs=[ANY] * 4 + [pl.BlockSpec((model, padded), lambda i, meta, slots: (0, 0))],
+            out_specs=[ANY] * 4,
             scratch_shapes=[
                 pltpu.VMEM((model, padded), BF16),
-                pltpu.VMEM((model, padded), F32),
                 pltpu.VMEM((tiles * ROW_TILE, model), BF16),
                 pltpu.VMEM((2, tokens, model), BF16),
                 pltpu.SemaphoreType.DMA,
                 pltpu.SemaphoreType.DMA((2,)),
             ],
         ),
-        out_shape=[token_part] * 4 + [like((model, padded), BF16)],
+        out_shape=[token_part] * 4,
         compiler_params=PARAMS,
-        cost_estimate=work(1),
-        name="exit_grads",
-    )(meta, places, table, raised, tokens_across, factors)
-
+        cost_estimate=work(50),
+        name="exit_tokens",
+    )(meta, places, table, raised, factors)
+
+    half = padded // 2
+
+    def table_half(side, factors, *before):
+        return pl.pallas_call(
+            functools.partial(exit_table_kernel, first=side * half, vocab=vocab),
+            grid_spec=pltpu.PrefetchScalarGridSpec(
+                num_scalar_prefetch=1,
+                grid=(tiles,),
+                in_specs=[
+                    pl.BlockSpec((ROW_TILE, half), lambda i, meta: (kept(i, meta), side)),
+                    pl.BlockSpec((model, ROW_TILE), lambda i, meta: (0, kept(i, meta))),
+                    pl.BlockSpec((8, ROW_TILE), lambda i, meta: (0, i)),
+                ]
+                + [ANY] * len(before),
+                out_specs=pl.BlockSpec((model, half), lambda i, meta: (0, side)),
+                scratch_shapes=[pltpu.VMEM((model, half), F32)],
+            ),
+            out_shape=like((model, padded), BF16),
+            input_output_aliases={4: 0} if before else {},
+            compiler_params=PARAMS,
+            cost_estimate=work(30),
+            name="exit_table",
+        )(meta, raised, tokens_across, factors, *before)
+
+    exit_scatter = scatter_core(exit_grads, wide_count)
+    half_grad = table_half(0, tie(factors, *exit_grads))
+    (own, came), exit_kept = exit_scatter
+    exit_far = scatter_far((own, tie(came, half_grad)), exit_kept, wide_count)
+    table_grad = table_half(1, tie(factors, exit_far[0]), half_grad)
     table_sum = lax.psum_scatter(table_grad, "narrow", scatter_dimension=0, tiled=True)
     embedding_grad = table_sum.astype(F32).T[:vocab]
-    exit_grad = scatter_wide(exit_grads, wide_count)
+    exit_near = scatter_near(tie(exit_far[1], table_grad), exit_far[2], wide_count)
+    exit_grad = exit_near[2] + exit_near[1].astype(F32)
 
     gain_like = like((8, model), F32)
     stream_two_grad, mlp_gains, *mlp_grads = pl.pallas_call(
         mlp_backward_kernel,
         in_specs=[SMEM] + [VMEM] * 8 + [ANY] * 8,
-        out_specs=[VMEM] * 10,
+        out_specs=[VMEM] * 2 + [ANY] * 8,
         out_shape=[stream_like, gain_like]
         + [like(part.shape, BF16) for part in gate_gathered]
         + [
@@ -1148,13 +1308,14 @@
             pltpu.VMEM((1, hidden_width, model), BF16),
             pltpu.VMEM((tokens, hidden_width), BF16),
             pltpu.VMEM((tokens, hidden_width), BF16),
-            pltpu.VMEM((model, hidden_width), BF16),
+            pltpu.VMEM((2, model, hidden_width), BF16),
             pltpu.VMEM((hidden_width, model), BF16),
             pltpu.SemaphoreType.DMA((kernel_count, 2)),
             one_matrix_sems,
+            pltpu.SemaphoreType.DMA((3, kernel_count)),
         ],
         compiler_params=PARAMS,
-        cost_estimate=work(1),
+        cost_estimate=work(40),
         name="mlp_backward",
     )(
         kernel_places, exit_grad, stream_three, stream_two, gain_all, normed_three,
@@ -1163,102 +1324,94 @@
     gate_scatter = scatter_core(from_kernels(mlp_grads[:4], [rows, rows]), wide_count)
     down_scatter = scatter_core(from_kernels(mlp_grads[4:], [down_rows]), wide_count)
 
+    def go_far(scatter, *others):
+        (own, came), kept = scatter
+        return scatter_far((own, tie(came, *others)), kept, wide_count)
+
+    def go_near(state, *others):
+        _, came, kept = state
+        return scatter_near(tie(came, *others), kept, wide_count)
+
     low_like = like((slots, model), BF16)
-    branch_two, query_two_low, key_two_low, value_two_low = pl.pallas_call(
-        cross_attention_backward_kernel,
+    middle = 2 * (HEADS // 4) * (model // HEADS)
+    low_half = like((slots, middle), BF16)
+    branch_two, attended_grad, *first_lows = pl.pallas_call(
+        cross_attention_first_kernel,
         in_specs=[SMEM] * 3 + [VMEM] * 5 + [ANY] * 4,
-        out_specs=[VMEM] * 4,
-        out_shape=[activation, activation, low_like, low_like],
+        out_specs=[VMEM] * 5,
+        out_shape=[activation, activation, like((tokens, middle), BF16), low_half, low_half],
         scratch_shapes=[
             pltpu.VMEM((1, model, model), BF16),
-            pltpu.VMEM((slots, tokens), F32),
+            pltpu.VMEM((slots, 2 * tokens), F32),
+            one_matrix_sems,
+        ],
+        compiler_params=PARAMS,
+        cost_estimate=work(20),
+        name="cross_attention_first",
+    )(
+        kernel_places, lengths, sources, stream_two_grad, query_two, key_two, value_two, totals_two,
+        *cross_gathered,
+    )
+    gate_far = go_far(gate_scatter, first_lows[0])
+    down_far = go_far(down_scatter, first_lows[0])
+    query_two_low, key_two_low, value_two_low = pl.pallas_call(
+        cross_attention_last_kernel,
+        in_specs=[SMEM] * 2 + [VMEM] * 8,
+        out_specs=[VMEM] * 3,
+        out_shape=[activation, low_like, low_like],
+        scratch_shapes=[pltpu.VMEM((slots, 2 * tokens), F32)],
+        compiler_params=PARAMS,
+        cost_estimate=work(20),
+        name="cross_attention_last",
+    )(
+        lengths, sources, tie(attended_grad, gate_far[0], down_far[0]), query_two, key_two,
+        value_two, totals_two, *first_lows,
+    )
+
+    cross_matrices = like((cross_gathered[0].shape[0], 5 * model // kernel_count, model), BF16)
+    stream_one_grad, cross_gains, memory_grad, branch_one, *cross_grads = pl.pallas_call(
+        cross_backward_kernel,
+        in_specs=[SMEM] + [VMEM] * 11 + [ANY] * 4,
+        out_specs=[VMEM] * 4 + [ANY] * 4,
+        out_shape=[stream_like, gain_like, like((slots, model), F32), activation]
+        + [cross_matrices] * 4,
+        scratch_shapes=[
+            pltpu.VMEM((3, model, model), BF16),
+            pltpu.VMEM((5, model, model), BF16),
+            pltpu.SemaphoreType.DMA((kernel_count, 3)),
+            pltpu.SemaphoreType.DMA((5, kernel_count)),
+        ],
+        compiler_params=PARAMS,
+        cost_estimate=work(34),
+        name="cross_backward",
+    )(
+        kernel_places, stream_two_grad, stream_one, gain_all,
+        normed_two, memory, attended_two, attended_one, branch_two,
+        query_two_low, key_two_low, value_two_low, *cross_gathered,
+    )
+    cross_scatter = scatter_core(from_kernels(cross_grads, [rows] * 5), wide_count)
+
+    gate_near = go_near(gate_far, branch_one)
+    down_near = go_near(down_far, branch_one)
+    query_one_low, key_one_low, value_one_low = pl.pallas_call(
+        self_attention_backward_kernel,
+        in_specs=[SMEM] * 2 + [VMEM] * 5 + [ANY] * 4,
+        out_specs=[VMEM] * 3,
+        out_shape=[activation] * 3,
+        scratch_shapes=[
+            pltpu.VMEM((1, model, model), BF16),
+            pltpu.VMEM((tokens, 2 * tokens), F32),
             pltpu.VMEM((tokens, model), BF16),
             one_matrix_sems,
         ],
         compiler_params=PARAMS,
-        cost_estimate=work(1),
-        name="cross_attention_backward",
-    )(
-        kernel_places, lengths, sources, stream_two_grad, query_two, key_two, value_two, totals_two,
-        *cross_gathered,
-    )
-
-    def go_far(scatter, *others):
-        (own, came), kept = scatter
-        return scatter_far((own, tie(came, *others)), kept, wide_count)
-
-    def go_near(state, *others):
-        _, came, kept = state
-        return scatter_near(tie(came, *others), kept, wide_count)
-
-    gate_far = go_far(gate_scatter, query_two_low)
-    down_far = go_far(down_scatter, query_two_low)
-
-    cross_matrices = like((cross_gathered[0].shape[0], 4 * model // kernel_count, model), BF16)
-    stream_one_grad, cross_gains, memory_grad, *cross_grads = pl.pallas_call(
-        cross_backward_kernel,
-        in_specs=[SMEM] + [VMEM] * 10 + [ANY] * 4,
-        out_specs=[VMEM] * 7,
-        out_shape=[stream_like, gain_like, like((slots, model), F32)] + [cross_matrices] * 4,
-        scratch_shapes=[
-            pltpu.VMEM((3, model, model), BF16),
-            pltpu.VMEM((model, model), BF16),
-            pltpu.SemaphoreType.DMA((kernel_count, 3)),
-        ],
-        compiler_params=PARAMS,
-        cost_estimate=work(1),
-        name="cross_backward",
-    )(
-        kernel_places, tie(stream_two_grad, gate_far[0], down_far[0]), stream_one, gain_all,
-        normed_two, memory, attended_two, branch_two, query_two_low, key_two_low, value_two_low,
-        *cross_gathered,
-    )
-    cross_scatter = scatter_core(from_kernels(cross_grads, [rows] * 4), wide_count)
-
-    branch_one, query_one_low, key_one_low, value_one_low = pl.pallas_call(
-        self_attention_backward_kernel,
-        in_specs=[SMEM] * 2 + [VMEM] * 5 + [ANY] * 4,
-        out_specs=[VMEM] * 4,
-        out_shape=[activation] * 4,
-        scratch_shapes=[
-            pltpu.VMEM((1, model, model), BF16),
-            pltpu.VMEM((tokens, tokens), F32),
-            pltpu.VMEM((tokens, model), BF16),
-            one_matrix_sems,
-        ],
-        compiler_params=PARAMS,
-        cost_estimate=work(1),
+        cost_estimate=work(18),
         name="self_attention_backward",
     )(
-        kernel_places, lengths, tie(stream_one_grad, loss_all), query_one, key_one, value_one, totals_one,
+        kernel_places, lengths, tie(branch_one, gate_near[0], down_near[0]), query_one, key_one, value_one, totals_one,
         *self_gathered,
     )
-    gate_near = go_near(gate_far, query_one_low)
-    down_near = go_near(down_far, query_one_low)
-    cross_far = go_far(cross_scatter, query_one_low)
-
-    inputs_grad, *self_grads = pl.pallas_call(
-        self_backward_kernel,
-        in_specs=[SMEM] + [VMEM] * 11 + [ANY] * 4,
-        out_specs=[VMEM] * 5,
-        out_shape=[stream_like] + [like(part.shape, BF16) for part in self_gathered],
-        scratch_shapes=[
-            pltpu.VMEM((3, model, model), BF16),
-            pltpu.VMEM((model, model), BF16),
-            pltpu.SemaphoreType.DMA((kernel_count, 3)),
-        ],
-        compiler_params=PARAMS,
-        cost_estimate=work(1),
-        name="self_backward",
-    )(
-        kernel_places, tie(stream_one_grad, gate_near[0], down_near[0], cross_far[0]), inputs,
-        gain_all, normed_one, attended_one, cross_gains, mlp_gains, branch_one, query_one_low,
-        key_one_low, value_one_low, *self_gathered,
-    )
-    extra = narrow_count * 8
-    self_scatter = scatter_core(from_kernels(self_grads, [rows] * 4 + [extra]), wide_count)
-
-    def finish(near, matrices, *others):
+    def line_blocks(near, matrices, *others):
         _, came, held = near
         summed = held + tie(came, *others).astype(F32)
         width = summed.shape[-1]
@@ -1269,16 +1422,74 @@
         ]
         if size < summed.shape[0]:
             members.append(summed[size:].reshape(narrow_count, -1, width))
-        return scatter_narrow(jnp.concatenate(members, axis=1), narrow, narrow_count)
-
-    gate_sum = finish(gate_near, 2, inputs_grad).reshape(2, shard, hidden_width)
-    down_sum = finish(down_near, 1, inputs_grad)
+        return jnp.concatenate(members, axis=1)
+
+    def line_first(near, matrices, *others):
+        blocks = line_blocks(near, matrices, *others)
+        steps = range(0, narrow_count, 2)
+        sent = jnp.stack([pick(blocks, narrow ^ (step + 1)) for step in steps]).astype(BF16)
+        came = lax.ppermute(sent, "narrow", narrow_pairs(narrow_count, 1))
+        return sent, came, [pick(blocks, narrow ^ step) for step in steps]
+
+    def line_second(state, *others):
+        _, came, kept = state
+        came = tie(came, *others).astype(F32)
+        terms = [kept[0] + came[0]]
+        for place in range(1, len(kept)):
+            sent = (kept[place] + came[place]).astype(BF16)
+            terms.append(lax.ppermute(sent, "narrow", narrow_pairs(narrow_count, 2 * place)))
+        return terms
+
+    cross_far = go_far(cross_scatter, query_one_low)
+    gate_line = line_first(gate_near, 2, query_one_low)
+
+    extra = narrow_count * 8
+    spare = extra * wide_count // kernel_count
+    inputs_grad, *self_grads = pl.pallas_call(
+        self_backward_kernel,
+        in_specs=[SMEM] + [VMEM] * 9 + [ANY] * 4,
+        out_specs=[VMEM] + [ANY] * 4,
+        out_shape=[stream_like]
+        + [like((part.shape[0], 3 * model // kernel_count + spare, model), BF16) for part in self_gathered],
+        scratch_shapes=[
+            pltpu.VMEM((3, model, model), BF16),
+            pltpu.VMEM((3, model, model), BF16),
+            pltpu.VMEM((spare, model), BF16),
+            pltpu.SemaphoreType.DMA((kernel_count, 3)),
+            pltpu.SemaphoreType.DMA((3, kernel_count)),
+            pltpu.SemaphoreType.DMA((kernel_count,)),
+        ],
+        compiler_params=PARAMS,
+        cost_estimate=work(20),
+        name="self_backward",
+    )(
+        kernel_places, tie(stream_one_grad, gate_line[0], cross_far[0]), inputs,
+        gain_all, normed_one, cross_gains, mlp_gains, query_one_low, key_one_low, value_one_low,
+        *self_gathered,
+    )
+    self_scatter = scatter_core(from_kernels(self_grads, [rows] * 3 + [extra]), wide_count)
+
     cross_near = go_near(cross_far, inputs_grad)
-    self_far = go_far(self_scatter)
-    cross_sum = finish(cross_near, 4).reshape(4, shard, model)
-    self_sum = finish(go_near(self_far), 4)
-    gains = pick(self_sum[4 * shard :].reshape(8, model // shard, shard), owner, 1)
-    self_sum = self_sum[: 4 * shard].reshape(4, shard, model)
+    self_far = go_far(self_scatter, cross_near[0])
+    down_line = line_first(down_near, 1, self_far[0])
+    self_near = go_near(self_far, down_line[0], embedding_grad)
+    gate_terms = line_second(gate_line, self_near[0])
+    down_terms = line_second(down_line, self_near[0])
+    cross_line = line_first(cross_near, 5, self_near[0])
+    self_terms = scatter_narrow(line_blocks(self_near, 3), narrow, narrow_count)
+    cross_terms = line_second(cross_line, self_terms[0])
+    gate_sum = add_terms(gate_terms, self_terms[0]).reshape(2, shard, hidden_width)
+    down_sum = add_terms(down_terms, self_terms[0])
+    cross_sum = add_terms(cross_terms).reshape(5, shard, model)
+    self_sum = add_terms(self_terms)
+    gains = pick(self_sum[3 * shard :].reshape(8, model // shard, shard), owner, 1)
+    self_sum = self_sum[: 3 * shard].reshape(3, shard, model)
+
+    loss_part = tie(loss_part, self_near[0])
+    loss_all = loss_part
+    for step in range(1, narrow_count):
+        loss_all = loss_all + lax.ppermute(loss_part, "narrow", narrow_pairs(narrow_count, step))
+    mean_loss = loss_all[0, 0] / slot_total
 
     return (
         activations,
@@ -1289,7 +1500,7 @@
         self_sum[0],
         self_sum[1],
         self_sum[2],
-        self_sum[3],
+        cross_sum[4],
         gains[1],
         cross_sum[0],
         cross_sum[1],

time: 532 us -> 518 us (0.974)
  starting transfers between devices: 79.6 us -> 61.8 us
  waiting for transfers between devices: 175 us -> 160 us
  other arithmetic: 39.4 us -> 51.7 us
  Pallas kernels: 196 us -> 206 us
    pallas_call x5 -> x8, Pallas kernels: 85.1 us -> 104 us  [the longest x2 29.8 us: table_half(): pl.pallas_call(functools.partial(exit_table_kernel, first=side * half, vo...]
    ppermute x3, waiting for transfers between devices: 36.7 us -> 28.9 us  [gather_early(): held = jnp.concatenate([held, lax.ppermute(held, 'wide', pairs)], axis=0)]
    ppermute x17 -> x14, waiting for transfers between devices: 33.8 us -> 26.9 us  [the longest x3 8.83 us: scatter_narrow(): lax.ppermute(pick(blocks, narrow ^ step).astype(BF16), 'narrow', narrow_p...]
    add x14, other arithmetic: 12.6 us -> 18.4 us  [the longest x5 9.07 us: scatter_far(): far = sent[0] + sent[1]]
    convert_element_type x6 -> x12, other arithmetic: 6.31 us -> 11.8 us  [the longest x5 9.45 us: scatter_near(): far = sum((term[1].astype(F32) for term in terms)).astype(BF16)]
    ppermute x17 -> x14, starting transfers between devices: 31.6 us -> 26.3 us  [the longest x3 12.4 us: line_first(): came = lax.ppermute(sent, 'narrow', narrow_pairs(narrow_count, 1))]
  transfers between devices with their start and end apart: 62 -> 59, of which waited for: 28 -> 23; matrix products, arithmetic and copies ran while one was open for 7% -> 9% of each run, Pallas kernels for 25% -> 30%
where the time goes in v3:
time: 518 us; the launch traced here: 509 us
  Pallas kernels  206 us (40%)
  waiting for transfers between devices  160 us (31%)
  starting transfers between devices  61.8 us (12%)
  other arithmetic  51.7 us (10%)
  between operations  17.8 us (3%)
  local copies, waits for them, and re-layouts  11.5 us (2%)
    ppermute x6, waiting for transfers between devices, gather_narrow(): lax.ppermute(block, 'narrow', narrow_pairs(count, step))  47.1 us
    pallas_call x2, Pallas kernels, table_half(): pl.pallas_call(functools.partial(exit_table_kernel, first=side * half, vo...  29.8 us
    ppermute x3, waiting for transfers between devices, gather_early(): held = jnp.concatenate([held, lax.ppermute(held, 'wide', pairs)], axis=0)  28.9 us
    pallas_call x1, Pallas kernels, per_device(): pl.pallas_call(functools.partial(exit_scores_kernel, vocab=vocab, scale=s...  24.4 us
    pallas_call x1, Pallas kernels, per_device(): pl.pallas_call(functools.partial(exit_tokens_kernel, vocab=vocab), grid_s...  23.5 us
    pallas_call x1, Pallas kernels, per_device(): pl.pallas_call(mlp_backward_kernel, in_specs=[SMEM] + [VMEM] * 8 + [ANY]...  20.6 us
    pallas_call x1, Pallas kernels, per_device(): pl.pallas_call(cross_backward_kernel, in_specs=[SMEM] + [VMEM] * 11 + [AN...  16.9 us
    pallas_call x1, Pallas kernels, per_device(): pl.pallas_call(cross_forward_kernel, in_specs=[SMEM, SMEM, SMEM, VMEM, VM...  14 us
  transfers between devices with their start and end apart: 59, of which 23 were waited for; matrix products, arithmetic and copies ran while one was open for 9% of the time, Pallas kernels for 30%

profile of v3, /device:TPU:0, one launch (start us, length us, event | category | flops | bytes accessed | tf_op | source)
XLA Modules:
  0.0 508.7 jit_solution(5520875044211244572)
XLA Ops:
  19.9 8.3 %collective-permute-done.1.refs_2_ = bf16[104,768]{1,0:T(8,128)(2,1)S(1)} collective-permute-done((bf16[104,768]{1,0:T(8,128)(2,1)}, bf16[104,768]{1,0:T(8,128)(2,1)S(1)}, u32[]{:S(2)}, u32[]{:S(2)}) %collective-permute-start.1) | collective-permute-done | bytes 159776 | tf_op jit(solution)/shard_map/ppermute | solution.py:140
  51.0 29.9 %collective-permute-done.4.refs_2_ = bf16[304,768]{1,0:T(8,128)(2,1)S(1)} collective-permute-done((bf16[304,768]{1,0:T(8,128)(2,1)S(1)}, bf16[304,768]{1,0:T(8,128)(2,1)S(1)}, u32[]{:S(2)}, u32[]{:S(2)}) %collective-permute-start.4) | collective-permute-done | bytes 466976 | tf_op jit(solution)/shard_map/ppermute | solution.py:140
  86.4 12.6 %collective-permute-done.8 = bf16[1,640,768]{2,1,0:T(8,128)(2,1)} collective-permute-done((bf16[1,640,768]{2,1,0:T(8,128)(2,1)}, bf16[1,640,768]{2,1,0:T(8,128)(2,1)}, u32[]{:S(2)}, u32[]{:S(2)}) %collective-permute-start.8) | collective-permute-done | bytes 983072 | tf_op jit(solution)/shard_map/ppermute | solution.py:1046
  106.2 9.6 %self_forward.1 = (bf16[320,768]{1,0:T(8,128)(2,1)}, bf16[320,768]{1,0:T(8,128)(2,1)}, bf16[320,768]{1,0:T(8,128)(2,1)}, bf16[320,768]{1,0:T(8,128)(2,1)}, bf16[...) custom-call(s32[8]{0:T(128)} %fusion.43.places, s32[2]{0:T(128)} %bitcast.108, ...), custom_call_target="tpu_custom_call" | custom-call | flops 1000000000 | bytes 1000000 | tf_op jit(solution)/shard_map/self_forward/pallas_call | solution.py:1090
  115.8 10.7 %collective-permute-done.11.refs_1_.refs_5_ = bf16[2,640,768]{2,1,0:T(8,128)(2,1)} collective-permute-done((bf16[2,640,768]{2,1,0:T(8,128)(2,1)S(1)}, bf16[2,640,768]{2,1,0:T(8,128)(2,1)}, u32[]{:S(2)}, u32[]{:S(2)}) %collective-permute-start.11) | collective-permute-done | bytes 1966112 | tf_op jit(solution)/shard_map/ppermute | solution.py:1079
  127.1 11.6 %collective-permute-done.12 = bf16[1,192,2048]{2,1,0:T(8,128)(2,1)S(1)} collective-permute-done((bf16[1,192,2048]{2,1,0:T(8,128)(2,1)S(1)}, bf16[1,192,2048]{2,1,0:T(8,128)(2,1)S(1)}, u32[]{:S(2)}, u32[]{:S(2)}) %collective-permute-start.12) | collective-permute-done | bytes 786464 | tf_op jit(solution)/shard_map/ppermute | solution.py:1046
  141.5 7.0 %memory_projection.1 = (bf16[1024,768]{1,0:T(8,128)(2,1)}, bf16[1024,768]{1,0:T(8,128)(2,1)}) custom-call(s32[8]{0:T(128)} %fusion.43.places, bf16[1024,768]{1,0:T(8,128)(2,1)} %memory.3, bf16[2,640,768]{2,1,0:T(8,128)(2,1)} %copy-done, bf16[2,640,768]{2,1,0:T(8,128)(2,1)} %collective-permute-done.11.refs_1_.refs_5_, bf16[2,640,768]{2,1,0:T(8,128)(2,1)} %copy-done.1, ...), custom_call_target="tpu_custom_call" | custom-call | flops 1000000000 | bytes 1000000 | tf_op jit(solution)/shard_map/memory_projection/pallas_call | solution.py:1125
  148.6 14.0 %cross_forward.1 = (bf16[320,768]{1,0:T(8,128)(2,1)}, bf16[320,768]{1,0:T(8,128)(2,1)}, bf16[320,768]{1,0:T(8,128)(2,1)}, f32[6,1,640]{2,1,0:T(1,128)}, f32[320,768]{1,0:T(8,128)}) custom-call(s32[8]{0:T(128)} %fusion.43.places, s32[2]{0:T(128)} %bitcast.109, s32[2]{0:T(128)} %bitcast.113, f32[320,768]{1,0:T(8,128)} %get-tuple-element.151.stream_in, ...), custom_call_target="tpu_custom_call" | custom-call | flops 1000000000 | bytes 1000000 | tf_op jit(solution)/shard_map/cross_forward/pallas_call | solution.py:1139
  167.5 11.2 %mlp_forward.1 = (bf16[320,768]{1,0:T(8,128)(2,1)}, f32[320,2048]{1,0:T(8,128)}, f32[320,2048]{1,0:T(8,128)}, bf16[320,2048]{1,0:T(8,128)(2,1)}, f32[320,768]{1,...) custom-call(s32[8]{0:T(128)} %fusion.43.places, f32[320,768]{1,0:T(8,128)} %get-tuple-element.155.stream_in.stream_two, ...), custom_call_target="tpu_custom_call" | custom-call | flops 1000000000 | bytes 1000000 | tf_op jit(solution)/shard_map/mlp_forward/pallas_call | solution.py:1165
  178.8 9.2 %collective-permute-done.18 = bf16[1,328,768]{2,1,0:T(8,128)(2,1)S(1)} collective-permute-done((bf16[1,328,768]{2,1,0:T(8,128)(2,1)}, bf16[1,328,768]{2,1,0:T(8,128)(2,1)S(1)}, u32[]{:S(2)}, u32[]{:S(2)}) %collective-permute-start.18) | collective-permute-done | bytes 503840 | tf_op jit(solution)/shard_map/ppermute | solution.py:97
  191.1 12.4 %collective-permute-done.19.refs_1_ = bf16[2,328,768]{2,1,0:T(8,128)(2,1)S(1)} collective-permute-done((bf16[2,328,768]{2,1,0:T(8,128)(2,1)S(1)}, bf16[2,328,768]{2,1,0:T(8,128)(2,1)S(1)}, u32[]{:S(2)}, u32[]{:S(2)}) %collective-permute-start.19) | collective-permute-done | bytes 1007648 | tf_op jit(solution)/shard_map/ppermute | solution.py:98
  210.0 24.4 %exit_scores.1 = (bf16[2560,4096]{1,0:T(8,128)(2,1)}, bf16[768,2560]{1,0:T(8,128)(2,1)}, f32[8,2560]{1,0:T(8,128)}) custom-call(s32[18]{0:T(128)} %pad_add_fusion.meta, s32[8]{0:T(128)} %select_reduce_fusion.slot_of, bf16[2,328,768]{2,1,0:T(8,128)(2,1)} %copy-done.10, bf16[2,328,768]{2,1,0:T(8,128)(2,1)} %copy-done.34, bf16[2,328,768]{2,1,0:T(8,128)(2,1)} %copy-done.35, ...), custom_call_target="tpu_custom_call" | custom-call | flops 51999997952 | bytes 1000000 | tf_op jit(solution)/shard_map/exit_scores/pallas_call | solution.py:1190
  251.5 23.5 %exit_tokens.1 = (bf16[2,320,768]{2,1,0:T(8,128)(2,1)}, bf16[2,320,768]{2,1,0:T(8,128)(2,1)}, bf16[2,320,768]{2,1,0:T(8,128)(2,1)}, bf16[2,320,768]{2,1,0:T(8,128)(2,1)}) custom-call(s32[18]{0:T(128)} %pad_add_fusion.meta, s32[8]{0:T(128)} %fusion.43.places, bf16[768,4096]{1,0:T(8,128)(2,1)} %all-gather.2.cloned.1.call-done.refs_4_.refs_0_, ...), custom_call_target="tpu_custom_call" | custom-call | flops 49999998976 | bytes 1000000 | tf_op jit(solution)/shard_map/exit_tokens/pallas_call | solution.py:1236
  275.6 14.7 %exit_table.2.refs_0_ = bf16[768,4096]{1,0:T(8,128)(2,1)} custom-call(s32[18]{0:T(128)} %pad_add_fusion.meta, bf16[2560,4096]{1,0:T(8,128)(2,1)} %get-tuple-element.161.refs_1_.raised, bf16[768,2560]{1,0:T(8,128)(2,1)} %get-tuple-element.166.across, f32[8,2560]{1,0:T(8,128)} %maximum_maximum_fusion.2.refs_2_.factors), custom_call_target="tpu_custom_call" | custom-call | flops 30000001024 | bytes 1000000 | tf_op jit(solution)/shard_map/exit_table/pallas_call | solution.py:1264
  292.1 15.1 %exit_table.3 = bf16[768,4096]{1,0:T(8,128)(2,1)} custom-call(s32[18]{0:T(128)} %pad_add_fusion.meta, bf16[2560,4096]{1,0:T(8,128)(2,1)} %get-tuple-element.161.refs_1_.raised, bf16[768,2560]{1,0:T(8,128)(2,1)} %get-tuple-element.166.across, f32[8,2560]{1,0:T(8,128)} %maximum_maximum_fusion.2.refs_2_.factors, ...), custom_call_target="tpu_custom_call", output_to_operand_aliasing={{}: (4, {})} | custom-call | flops 30000001024 | bytes 1000000 | tf_op jit(solution)/shard_map/exit_table/pallas_call | solution.py:1264
  310.0 7.3 %collective-permute-done.28 = bf16[320,768]{1,0:T(8,128)(2,1)S(1)} collective-permute-done((bf16[320,768]{1,0:T(8,128)(2,1)S(1)}, bf16[320,768]{1,0:T(8,128)(2,1)S(1)}, u32[]{:S(2)}, u32[]{:S(2)}) %collective-permute-start.28) | collective-permute-done | bytes 491552 | tf_op jit(solution)/shard_map/ppermute | solution.py:118
  319.5 20.6 %mlp_backward.1 = (f32[320,768]{1,0:T(8,128)}, f32[8,768]{1,0:T(8,128)}, bf16[2,192,2048]{2,1,0:T(8,128)(2,1)}, bf16[2,192,2048]{2,1,0:T(8,128)(2,1)}, bf16[2,19...) custom-call(s32[8]{0:T(128)} %fusion.43.places, ...), custom_call_target="tpu_custom_call" | custom-call | flops 40000000000 | bytes 1000000 | tf_op jit(solution)/shard_map/mlp_backward/pallas_call | solution.py:1296
  341.2 10.9 %cross_attention_first.1 = (bf16[320,768]{1,0:T(8,128)(2,1)}, bf16[320,768]{1,0:T(8,128)(2,1)}, bf16[320,384]{1,0:T(8,128)(2,1)}, bf16[1024,384]{1,0:T(8,128)(2,1)}, bf16[1024,384]{1,0:T(8,128)(2,1)}) custom-call(s32[8]{0:T(128)} %fusion.43.places, s32[2]{0:T(128)} %bitcast.110, s32[2]{0:T(128)} %bitcast.114, f32[320,768]{1,0:T(8,128)} %get-tuple-element.176.grad_in, ...), custom_call_target="tpu_custom_call" | custom-call | flops 20000000000 | bytes 1000000 | tf_op jit(solution)/shard_map/cross_attention_first/pallas_call | solution.py:1338
  358.3 10.6 %cross_attention_last.1 = (bf16[320,768]{1,0:T(8,128)(2,1)}, bf16[1024,768]{1,0:T(8,128)(2,1)}, bf16[1024,768]{1,0:T(8,128)(2,1)}) custom-call(s32[2]{0:T(128)} %bitcast.111, s32[2]{0:T(128)} %bitcast.115, bf16[320,768]{1,0:T(8,128)(2,1)} %get-tuple-element.191.attended_grad, bf16[320,768]{1,0:T(8,128)(2,1)} %get-tuple-element.180.query, ...), custom_call_target="tpu_custom_call" | custom-call | flops 20000000000 | bytes 1000000 | tf_op jit(solution)/shard_map/cross_attention_last/pallas_call | solution.py:1357
  368.9 16.9 %cross_backward.1 = (f32[320,768]{1,0:T(8,128)}, f32[8,768]{1,0:T(8,128)}, f32[1024,768]{1,0:T(8,128)}, bf16[320,768]{1,0:T(8,128)(2,1)}, bf16[2,480,768]{2,1,0:...) custom-call(s32[8]{0:T(128)} %fusion.43.places, ...), custom_call_target="tpu_custom_call" | custom-call | flops 33999998976 | bytes 1000000 | tf_op jit(solution)/shard_map/cross_backward/pallas_call | solution.py:1372
  392.6 8.4 %self_attention_backward.1 = (bf16[320,768]{1,0:T(8,128)(2,1)}, bf16[320,768]{1,0:T(8,128)(2,1)}, bf16[320,768]{1,0:T(8,128)(2,1)}) custom-call(s32[8]{0:T(128)} %fusion.43.places, s32[2]{0:T(128)} %bitcast.112, bf16[320,768]{1,0:T(8,128)(2,1)} %get-tuple-element.205.branch, bf16[320,768]{1,0:T(8,128)(2,1)} %get-tuple-element.206.query, ...), custom_call_target="tpu_custom_call" | custom-call | flops 17999998976 | bytes 1000000 | tf_op jit(solution)/shard_map/self_attention_backward/pallas_call | solution.py:1396
  407.7 10.6 %self_backward.1 = (f32[320,768]{1,0:T(8,128)}, bf16[2,320,768]{2,1,0:T(8,128)(2,1)}, bf16[2,320,768]{2,1,0:T(8,128)(2,1)}, bf16[2,320,768]{2,1,0:T(8,128)(2,1)}, bf16[2,320,768]{2,1,0:T(8,128)(2,1)}) custom-call(s32[8]{0:T(128)} %fusion.43.places, f32[320,768]{1,0:T(8,128)} %get-tuple-element.215.grad_in, bf16[320,768]{1,0:T(8,128)(2,1)} %inputs.2, ...), custom_call_target="tpu_custom_call" | custom-call | flops 20000000000 | bytes 1000000 | tf_op jit(solution)/shard_map/self_backward/pallas_call | solution.py:1448
  441.6 8.9 %collective-permute-done.41 = bf16[2,320,768]{2,1,0:T(8,128)(2,1)} collective-permute-done((bf16[2,320,768]{2,1,0:T(8,128)(2,1)S(1)}, bf16[2,320,768]{2,1,0:T(8,128)(2,1)}, u32[]{:S(2)}, u32[]{:S(2)}) %collective-permute-start.41) | collective-permute-done | bytes 983072 | tf_op jit(solution)/shard_map/ppermute | solution.py:109
  485.1 8.8 %collective-permute-done.48 = bf16[80,768]{1,0:T(8,128)(2,1)S(1)} collective-permute-done((bf16[80,768]{1,0:T(8,128)(2,1)S(1)}, bf16[80,768]{1,0:T(8,128)(2,1)S(1)}, u32[]{:S(2)}, u32[]{:S(2)}) %collective-permute-start.48) | collective-permute-done | bytes 122912 | tf_op jit(solution)/shard_map/ppermute | solution.py:155
  (275 shorter events, 173.6 us)
Async XLA Ops:
  7.2 201.8 %all-gather.2.cloned.1.call-start = ((), (), s32[]{:S(2)}) async-start(), calls=%async_computation.1 | async-start | bytes 7864320 | tf_op jit(solution)/shard_map/all_gather | solution.py:1039
  46.4 38.2 %collective-permute-start.7 = (bf16[2,416,768]{2,1,0:T(8,128)(2,1)S(1)}, bf16[2,416,768]{2,1,0:T(8,128)(2,1)}, u32[]{:S(2)}, u32[]{:S(2)}) collective-permute-start(bf16[2,416,768]{2,1,0:T(8,128)(2,1)S(1)} %pad_maximum_fusion.2.refs_0_), channel_id=1, source_target_pairs={{0,16},{4,12},{8,24},{12,4},{16,0},{20,28},{24,8},{28,20},{1,17},{... | collective-permute-start | bytes 3833864 | tf_op jit(solution)/shard_map/ppermute | solution.py:1057
  46.9 34.0 %collective-permute-start.4 = (bf16[304,768]{1,0:T(8,128)(2,1)S(1)}, bf16[304,768]{1,0:T(8,128)(2,1)S(1)}, u32[]{:S(2)}, u32[]{:S(2)}) collective-permute-start(bf16[304,768]{1,0:T(8,128)(2,1)S(1)} %copy-done.36), channel_id=1, source_target_pairs={{0,2},{1,3},{2,0},{3,1},{4,6},{5,7},{6,4},{7,5},{8,10},{9,11},{10,... | collective-permute-start | bytes 1400840 | tf_op jit(solution)/shard_map/ppermute | solution.py:140
  49.8 31.9 %collective-permute-start.5 = (bf16[304,768]{1,0:T(8,128)(2,1)S(1)}, bf16[304,768]{1,0:T(8,128)(2,1)}, u32[]{:S(2)}, u32[]{:S(2)}) collective-permute-start(bf16[304,768]{1,0:T(8,128)(2,1)S(1)} %copy-done.36), channel_id=1, source_target_pairs={{0,3},{1,2},{2,1},{3,0},{4,7},{5,6},{6,5},{7,4},{8,11},{9,10},{10,... | collective-permute-start | bytes 1400840 | tf_op jit(solution)/shard_map/ppermute | solution.py:140
  86.4 351.7 %reduce-scatter.2.cloned.1.call-start = ((), (), s32[]{:S(2)}) async-start(), calls=%async_computation.2 | async-start | bytes 7864320 | tf_op jit(solution)/shard_map/reduce_scatter | solution.py:1290
  100.9 25.6 %collective-permute-start.11 = (bf16[2,640,768]{2,1,0:T(8,128)(2,1)S(1)}, bf16[2,640,768]{2,1,0:T(8,128)(2,1)}, u32[]{:S(2)}, u32[]{:S(2)}) collective-permute-start(bf16[2,640,768]{2,1,0:T(8,128)(2,1)S(1)} %pad_maximum_fusion.refs_0_.refs_4_), channel_id=1, source_target_pairs={{0,16},{4,12},{8,24},{12,4},{16,0},{20,28},{24,8},{28,20},{1,17},{... | collective-permute-start | bytes 5898248 | tf_op jit(solution)/shard_map/ppermute | solution.py:1079
  140.0 22.7 %collective-permute-start.15 = (bf16[2,192,2048]{2,1,0:T(8,128)(2,1)S(1)}, bf16[2,192,2048]{2,1,0:T(8,128)(2,1)}, u32[]{:S(2)}, u32[]{:S(2)}) collective-permute-start(bf16[2,192,2048]{2,1,0:T(8,128)(2,1)S(1)} %pad_maximum_fusion.1.refs_0_), channel_id=1, source_target_pairs={{0,16},{4,12},{8,24},{12,4},{16,0},{20,28},{24,8},{28,20},{1,17},{... | collective-permute-start | bytes 4718600 | tf_op jit(solution)/shard_map/ppermute | solution.py:1122
  140.0 23.7 %collective-permute-start.16 = (bf16[2,192,2048]{2,1,0:T(8,128)(2,1)S(1)}, bf16[2,192,2048]{2,1,0:T(8,128)(2,1)}, u32[]{:S(2)}, u32[]{:S(2)}) collective-permute-start(bf16[2,192,2048]{2,1,0:T(8,128)(2,1)S(1)} %pad_maximum_fusion.1.refs_0_), channel_id=1, source_target_pairs={{0,4},{4,0},{8,12},{12,8},{16,20},{20,16},{24,28},{28,24},{1,5},{5... | collective-permute-start | bytes 4718600 | tf_op jit(solution)/shard_map/ppermute | solution.py:90
  191.1 17.9 %collective-permute-start.20 = (bf16[2,328,768]{2,1,0:T(8,128)(2,1)S(1)}, bf16[2,328,768]{2,1,0:T(8,128)(2,1)S(1)}, u32[]{:S(2)}, u32[]{:S(2)}) collective-permute-start(bf16[2,328,768]{2,1,0:T(8,128)(2,1)S(1)} %pad_maximum_fusion.3.refs_0_), channel_id=1, source_target_pairs={{0,4},{4,0},{8,12},{12,8},{16,20},{20,16},{24,28},{28,24},{1,5},{5... | collective-permute-start | bytes 3022856 | tf_op jit(solution)/shard_map/ppermute | solution.py:90
  275.1 32.1 %collective-permute-start.25 = (bf16[2,320,768]{2,1,0:T(8,128)(2,1)}, bf16[2,320,768]{2,1,0:T(8,128)(2,1)S(1)}, u32[]{:S(2)}, u32[]{:S(2)}) collective-permute-start(bf16[2,320,768]{2,1,0:T(8,128)(2,1)} %get-tuple-element.163), channel_id=1, source_target_pairs={{0,4},{4,0},{8,12},{12,8},{16,20},{20,16},{24,28},{28,24},{1,5},{5... | collective-permute-start | bytes 2949128 | tf_op jit(solution)/shard_map/ppermute | solution.py:90
  290.5 16.6 %collective-permute-start.27 = (bf16[2,320,768]{2,1,0:T(8,128)(2,1)S(1)}, bf16[2,320,768]{2,1,0:T(8,128)(2,1)}, u32[]{:S(2)}, u32[]{:S(2)}) collective-permute-start(bf16[2,320,768]{2,1,0:T(8,128)(2,1)S(1)} %add.281), channel_id=1, source_target_pairs={{0,16},{4,12},{8,24},{12,4},{16,0},{20,28},{24,8},{28,20},{1,17},{... | collective-permute-start | bytes 2949128 | tf_op jit(solution)/shard_map/ppermute | solution.py:109
  340.7 47.8 %collective-permute-start.31 = (bf16[2,192,2048]{2,1,0:T(8,128)(2,1)}, bf16[2,192,2048]{2,1,0:T(8,128)(2,1)S(1)}, u32[]{:S(2)}, u32[]{:S(2)}) collective-permute-start(bf16[2,192,2048]{2,1,0:T(8,128)(2,1)} %get-tuple-element.199), channel_id=1, source_target_pairs={{0,4},{4,0},{8,12},{12,8},{16,20},{20,16},{24,28},{28,24},{1,5},{5... | collective-permute-start | bytes 4718600 | tf_op jit(solution)/shard_map/ppermute | solution.py:90
  340.8 45.7 %collective-permute-start.34 = (bf16[2,256,768]{2,1,0:T(8,128)(2,1)}, bf16[2,256,768]{2,1,0:T(8,128)(2,1)}, u32[]{:S(2)}, u32[]{:S(2)}) collective-permute-start(bf16[2,256,768]{2,1,0:T(8,128)(2,1)} %get-tuple-element.203), channel_id=1, source_target_pairs={{0,4},{4,0},{8,12},{12,8},{16,20},{20,16},{24,28},{28,24},{1,5},{5... | collective-permute-start | bytes 2359304 | tf_op jit(solution)/shard_map/ppermute | solution.py:90
  354.5 31.4 %collective-permute-start.35 = (bf16[2,256,768]{2,1,0:T(8,128)(2,1)}, bf16[2,256,768]{2,1,0:T(8,128)(2,1)}, u32[]{:S(2)}, u32[]{:S(2)}) collective-permute-start(bf16[2,256,768]{2,1,0:T(8,128)(2,1)} %add.288), channel_id=1, source_target_pairs={{0,16},{4,12},{8,24},{12,4},{16,0},{20,28},{24,8},{28,20},{1,17},{... | collective-permute-start | bytes 2359304 | tf_op jit(solution)/shard_map/ppermute | solution.py:109
  357.2 31.2 %collective-permute-start.32 = (bf16[2,192,2048]{2,1,0:T(8,128)(2,1)}, bf16[2,192,2048]{2,1,0:T(8,128)(2,1)}, u32[]{:S(2)}, u32[]{:S(2)}) collective-permute-start(bf16[2,192,2048]{2,1,0:T(8,128)(2,1)} %add.287), channel_id=1, source_target_pairs={{0,16},{4,12},{8,24},{12,4},{16,0},{20,28},{24,8},{28,20},{1,17},{... | collective-permute-start | bytes 4718600 | tf_op jit(solution)/shard_map/ppermute | solution.py:109
  386.0 40.2 %collective-permute-start.39 = (bf16[2,480,768]{2,1,0:T(8,128)(2,1)}, bf16[2,480,768]{2,1,0:T(8,128)(2,1)}, u32[]{:S(2)}, u32[]{:S(2)}) collective-permute-start(bf16[2,480,768]{2,1,0:T(8,128)(2,1)} %get-tuple-element.226), channel_id=1, source_target_pairs={{0,4},{4,0},{8,12},{12,8},{16,20},{20,16},{24,28},{28,24},{1,5},{5... | collective-permute-start | bytes 4423688 | tf_op jit(solution)/shard_map/ppermute | solution.py:90
  404.3 21.8 %collective-permute-start.40 = (bf16[2,480,768]{2,1,0:T(8,128)(2,1)}, bf16[2,480,768]{2,1,0:T(8,128)(2,1)}, u32[]{:S(2)}, u32[]{:S(2)}) collective-permute-start(bf16[2,480,768]{2,1,0:T(8,128)(2,1)} %add.297), channel_id=1, source_target_pairs={{0,16},{4,12},{8,24},{12,4},{16,0},{20,28},{24,8},{28,20},{1,17},{... | collective-permute-start | bytes 4423688 | tf_op jit(solution)/shard_map/ppermute | solution.py:109
  419.8 41.4 %collective-permute-start.53 = (bf16[2,48,2048]{2,1,0:T(8,128)(2,1)}, bf16[2,48,2048]{2,1,0:T(8,128)(2,1)}, u32[]{:S(2)}, u32[]{:S(2)}) collective-permute-start(bf16[2,48,2048]{2,1,0:T(8,128)(2,1)} %pad_maximum_fusion.4), channel_id=1, source_target_pairs={{0,1},{1,0},{2,3},{3,2},{4,5},{5,4},{6,7},{7,6},{8,9},{9,8},{10,11... | collective-permute-start | bytes 1179656 | tf_op jit(solution)/shard_map/ppermute | solution.py:1431
  426.1 24.3 %collective-permute-start.37 = (bf16[2,320,768]{2,1,0:T(8,128)(2,1)}, bf16[2,320,768]{2,1,0:T(8,128)(2,1)}, u32[]{:S(2)}, u32[]{:S(2)}) collective-permute-start(bf16[2,320,768]{2,1,0:T(8,128)(2,1)} %get-tuple-element.222), channel_id=1, source_target_pairs={{0,4},{4,0},{8,12},{12,8},{16,20},{20,16},{24,28},{28,24},{1,5},{5... | collective-permute-start | bytes 2949128 | tf_op jit(solution)/shard_map/ppermute | solution.py:90
  428.6 30.2 %collective-permute-start.50 = (bf16[480,768]{1,0:T(8,128)(2,1)}, bf16[480,768]{1,0:T(8,128)(2,1)}, u32[]{:S(2)}, u32[]{:S(2)}) collective-permute-start(bf16[480,768]{1,0:T(8,128)(2,1)} %fusion.1), channel_id=1, source_target_pairs={{0,8},{4,20},{8,0},{12,28},{16,24},{20,4},{24,16},{28,12},{1,9},{5... | collective-permute-start | bytes 2211848 | tf_op jit(solution)/shard_map/ppermute | solution.py:118
  430.6 19.9 %collective-permute-start.41 = (bf16[2,320,768]{2,1,0:T(8,128)(2,1)S(1)}, bf16[2,320,768]{2,1,0:T(8,128)(2,1)}, u32[]{:S(2)}, u32[]{:S(2)}) collective-permute-start(bf16[2,320,768]{2,1,0:T(8,128)(2,1)S(1)} %add.301), channel_id=1, source_target_pairs={{0,16},{4,12},{8,24},{12,4},{16,0},{20,28},{24,8},{28,20},{1,17},{... | collective-permute-start | bytes 2949128 | tf_op jit(solution)/shard_map/ppermute | solution.py:109
  432.6 31.7 %collective-permute-start.55 = (bf16[2,64,768]{2,1,0:T(8,128)(2,1)S(1)}, bf16[2,64,768]{2,1,0:T(8,128)(2,1)}, u32[]{:S(2)}, u32[]{:S(2)}) collective-permute-start(bf16[2,64,768]{2,1,0:T(8,128)(2,1)S(1)} %pad_maximum_fusion.6), channel_id=1, source_target_pairs={{0,1},{1,0},{2,3},{3,2},{4,5},{5,4},{6,7},{7,6},{8,9},{9,8},{10,11... | collective-permute-start | bytes 589832 | tf_op jit(solution)/shard_map/ppermute | solution.py:1431
  464.3 17.8 %collective-permute-start.51 = (bf16[2,120,768]{2,1,0:T(8,128)(2,1)S(1)}, bf16[2,120,768]{2,1,0:T(8,128)(2,1)S(1)}, u32[]{:S(2)}, u32[]{:S(2)}) collective-permute-start(bf16[2,120,768]{2,1,0:T(8,128)(2,1)S(1)} %pad_maximum_fusion.5), channel_id=1, source_target_pairs={{0,1},{1,0},{2,3},{3,2},{4,5},{5,4},{6,7},{7,6},{8,9},{9,8},{10,11... | collective-permute-start | bytes 1105928 | tf_op jit(solution)/shard_map/ppermute | solution.py:1431
  473.5 20.4 %collective-permute-start.48 = (bf16[80,768]{1,0:T(8,128)(2,1)S(1)}, bf16[80,768]{1,0:T(8,128)(2,1)S(1)}, u32[]{:S(2)}, u32[]{:S(2)}) collective-permute-start(bf16[80,768]{1,0:T(8,128)(2,1)S(1)} %get-tuple-element.278), channel_id=1, source_target_pairs={{0,2},{1,3},{2,0},{3,1},{4,6},{5,7},{6,4},{7,5},{8,10},{9,11},{10,... | collective-permute-start | bytes 368648 | tf_op jit(solution)/shard_map/ppermute | solution.py:155
  (77 other events, 959.4 us)
Sparse Core Ops, SparseCore 0:
  86.5 122.4 all-gather.1
  310.1 114.4 reduce-scatter.1

commit v4 on v3

--- a/solution.py
+++ b/solution.py
@@ -15,7 +15,6 @@
 BF16 = jnp.bfloat16
 LANES = 128
 ROW_TILE = 256
-GRAD_TILE = 256
 VOCAB_TILE = 512
 MIX = math.sqrt(2.0 / math.pi)
 CUBE = 0.044715
@@ -378,8 +377,8 @@
         spot += 1
 
 
-def line_wide_kernel(narrow, *refs, sizes, wide_size):
-    pieces, block, wide_block = refs[:-2], refs[-2], refs[-1]
+def line_wide_kernel(narrow, even, odd, block, wide_block, *, sizes, wide_size):
+    pieces = [(odd if step % 2 else even).at[step // 2] for step in range(2 * even.shape[0])]
     count, width = len(pieces), block.shape[1]
     start = 0
     for size in sizes:
@@ -678,11 +677,19 @@
     def clear():
         total[...] = jnp.zeros_like(total)
 
-    @pl.when(step < meta[META_TILES])
-    def compute():
+    def compute(raised, across, factors):
         chunk = logit_grads(meta, raised, factors, first, width, vocab)
         for start in range(0, raised.shape[1], width):
             total[:, start : start + width] += nn(across[...], chunk(start))
+
+    @pl.when(2 * step + 1 < meta[META_TILES])
+    def both():
+        compute(raised, across, factors)
+
+    @pl.when(2 * step + 1 == meta[META_TILES])
+    def one():
+        half = raised.shape[0] // 2
+        compute(raised.at[:half], across.at[:, :half], factors.at[:, :half])
 
     @pl.when(step == pl.num_programs(0) - 1)
     def finish():
@@ -1047,19 +1054,27 @@
         return held
 
     if aligned:
-        joined_line = gather_narrow(tie(joined_pack, *self_line), narrow_count)
+        joined_even = tie(joined_pack, *self_line)
+        joined_even = jnp.stack(
+            [joined_even]
+            + [
+                lax.ppermute(joined_even, "narrow", narrow_pairs(narrow_count, step))
+                for step in range(2, narrow_count, 2)
+            ]
+        )
+        joined_odd = lax.ppermute(joined_even, "narrow", narrow_pairs(narrow_count, 1))
     else:
         cross_line = gather_narrow(join_rows(*members), narrow_count)
         gate_line = gather_narrow(join_rows(mlp_gate, mlp_up), narrow_count)
     self_held = gather_early(self_block)
     if aligned:
-        self_held = tie(self_held, joined_line[1])
+        self_held = tie(self_held, joined_even)
     self_came = lax.ppermute(self_held, "wide", last)
     if aligned:
-        joined_line = lax.optimization_barrier((*joined_line, self_held))[:narrow_count]
+        joined_odd = tie(joined_odd, self_held)
         cross_block, gate_block = pl.pallas_call(
             functools.partial(line_wide_kernel, sizes=cross_sizes, wide_size=shard),
-            in_specs=[SMEM] + [VMEM] * narrow_count,
+            in_specs=[SMEM] + [VMEM] * 2,
             out_specs=[VMEM] * 2,
             out_shape=[
                 like((sum(cross_sizes) * narrow_count, model), BF16),
@@ -1068,7 +1083,7 @@
             compiler_params=PARAMS,
             cost_estimate=work(1),
             name="line_wide",
-        )(narrow[None], *joined_line)
+        )(narrow[None], joined_even, joined_odd)
     else:
         cross_block = line_block(cross_line, cross_sizes)
         gate_block = line_block(gate_line, gate_sizes)
@@ -1110,7 +1125,7 @@
     ).astype(jnp.int32)
     extents = (numbers + 15) // 16 * 16
     starts = jnp.sum(jnp.where(ids[None, :] < ids[:, None], extents[None, :], 0), axis=1)
-    needed = (jnp.sum(extents) + GRAD_TILE - 1) // GRAD_TILE * (1)
+    needed = (jnp.sum(extents) + ROW_TILE - 1) // ROW_TILE
     meta = jnp.concatenate([jnp.stack([wide, needed]), starts, numbers])
     slot_of = jnp.sum(jnp.where(order, ids[None, :], 0), axis=1)
 
@@ -1183,9 +1198,9 @@
 
     exit_parts = gather_wide(normed_four, wide_count)
     group = tokens * wide_count
-    tiles = -(-group // GRAD_TILE) * (1)
+    tiles = -(-group // (2 * ROW_TILE)) * 2
     kept = lambda i, meta: jnp.minimum(i, meta[META_TILES] - 1)
-    kept_grad = lambda i, meta: jnp.minimum(i, meta[META_TILES] * 1 - 1)
+    kept_pair = lambda i, meta: jnp.minimum(i, (meta[META_TILES] - 1) // 2)
 
     raised, tokens_across, stats = pl.pallas_call(
         functools.partial(exit_scores_kernel, vocab=vocab, scale=scale),
@@ -1265,11 +1280,11 @@
             functools.partial(exit_table_kernel, first=side * half, vocab=vocab),
             grid_spec=pltpu.PrefetchScalarGridSpec(
                 num_scalar_prefetch=1,
-                grid=(tiles,),
+                grid=(tiles // 2,),
                 in_specs=[
-                    pl.BlockSpec((ROW_TILE, half), lambda i, meta: (kept(i, meta), side)),
-                    pl.BlockSpec((model, ROW_TILE), lambda i, meta: (0, kept(i, meta))),
-                    pl.BlockSpec((8, ROW_TILE), lambda i, meta: (0, i)),
+                    pl.BlockSpec((2 * ROW_TILE, half), lambda i, meta: (kept_pair(i, meta), side)),
+                    pl.BlockSpec((model, 2 * ROW_TILE), lambda i, meta: (0, kept_pair(i, meta))),
+                    pl.BlockSpec((8, 2 * ROW_TILE), lambda i, meta: (0, i)),
                 ]
                 + [ANY] * len(before),
                 out_specs=pl.BlockSpec((model, half), lambda i, meta: (0, side)),
@@ -1278,7 +1293,7 @@
             out_shape=like((model, padded), BF16),
             input_output_aliases={4: 0} if before else {},
             compiler_params=PARAMS,
-            cost_estimate=work(30),
+            cost_estimate=work(15),
             name="exit_table",
         )(meta, raised, tokens_across, factors, *before)
 
@@ -1315,7 +1330,7 @@
             pltpu.SemaphoreType.DMA((3, kernel_count)),
         ],
         compiler_params=PARAMS,
-        cost_estimate=work(40),
+        cost_estimate=work(15),
         name="mlp_backward",
     )(
         kernel_places, exit_grad, stream_three, stream_two, gain_all, normed_three,
@@ -1346,7 +1361,7 @@
             one_matrix_sems,
         ],
         compiler_params=PARAMS,
-        cost_estimate=work(20),
+        cost_estimate=work(16),
         name="cross_attention_first",
     )(
         kernel_places, lengths, sources, stream_two_grad, query_two, key_two, value_two, totals_two,
@@ -1361,13 +1376,18 @@
         out_shape=[activation, low_like, low_like],
         scratch_shapes=[pltpu.VMEM((slots, 2 * tokens), F32)],
         compiler_params=PARAMS,
-        cost_estimate=work(20),
+        cost_estimate=work(16),
         name="cross_attention_last",
     )(
         lengths, sources, tie(attended_grad, gate_far[0], down_far[0]), query_two, key_two,
         value_two, totals_two, *first_lows,
     )
 
+    loss_part = tie(loss_part, query_two_low)
+    loss_all = loss_part
+    for step in range(1, narrow_count):
+        loss_all = loss_all + lax.ppermute(loss_part, "narrow", narrow_pairs(narrow_count, step))
+    mean_loss = loss_all[0, 0] / slot_total
     cross_matrices = like((cross_gathered[0].shape[0], 5 * model // kernel_count, model), BF16)
     stream_one_grad, cross_gains, memory_grad, branch_one, *cross_grads = pl.pallas_call(
         cross_backward_kernel,
@@ -1382,7 +1402,7 @@
             pltpu.SemaphoreType.DMA((5, kernel_count)),
         ],
         compiler_params=PARAMS,
-        cost_estimate=work(34),
+        cost_estimate=work(20),
         name="cross_backward",
     )(
         kernel_places, stream_two_grad, stream_one, gain_all,
@@ -1405,10 +1425,10 @@
             one_matrix_sems,
         ],
         compiler_params=PARAMS,
-        cost_estimate=work(18),
+        cost_estimate=work(10),
         name="self_attention_backward",
     )(
-        kernel_places, lengths, tie(branch_one, gate_near[0], down_near[0]), query_one, key_one, value_one, totals_one,
+        kernel_places, lengths, tie(branch_one, gate_near[0], down_near[0], loss_all), query_one, key_one, value_one, totals_one,
         *self_gathered,
     )
     def line_blocks(near, matrices, *others):
@@ -1460,7 +1480,7 @@
             pltpu.SemaphoreType.DMA((kernel_count,)),
         ],
         compiler_params=PARAMS,
-        cost_estimate=work(20),
+        cost_estimate=work(12),
         name="self_backward",
     )(
         kernel_places, tie(stream_one_grad, gate_line[0], cross_far[0]), inputs,
@@ -1472,24 +1492,20 @@
     cross_near = go_near(cross_far, inputs_grad)
     self_far = go_far(self_scatter, cross_near[0])
     down_line = line_first(down_near, 1, self_far[0])
-    self_near = go_near(self_far, down_line[0], embedding_grad)
-    gate_terms = line_second(gate_line, self_near[0])
+    gate_terms = line_second(gate_line, self_far[0])
+    cross_line = line_first(cross_near, 5, down_line[0], gate_terms[0], embedding_grad)
+    self_near = go_near(self_far, cross_line[0])
     down_terms = line_second(down_line, self_near[0])
-    cross_line = line_first(cross_near, 5, self_near[0])
-    self_terms = scatter_narrow(line_blocks(self_near, 3), narrow, narrow_count)
-    cross_terms = line_second(cross_line, self_terms[0])
-    gate_sum = add_terms(gate_terms, self_terms[0]).reshape(2, shard, hidden_width)
+    gate_sum = add_terms(gate_terms, self_near[0]).reshape(2, shard, hidden_width)
+    cross_terms = line_second(cross_line, down_terms[0], gate_sum)
+    self_terms = scatter_narrow(
+        line_blocks(self_near, 3, cross_terms[0]), narrow, narrow_count
+    )
     down_sum = add_terms(down_terms, self_terms[0])
-    cross_sum = add_terms(cross_terms).reshape(5, shard, model)
+    cross_sum = add_terms(cross_terms, self_terms[0]).reshape(5, shard, model)
     self_sum = add_terms(self_terms)
     gains = pick(self_sum[3 * shard :].reshape(8, model // shard, shard), owner, 1)
     self_sum = self_sum[: 3 * shard].reshape(3, shard, model)
-
-    loss_part = tie(loss_part, self_near[0])
-    loss_all = loss_part
-    for step in range(1, narrow_count):
-        loss_all = loss_all + lax.ppermute(loss_part, "narrow", narrow_pairs(narrow_count, step))
-    mean_loss = loss_all[0, 0] / slot_total
 
     return (
         activations,

time: 518 us -> 500 us (0.965)
  starting transfers between devices: 61.8 us -> 53.5 us
  waiting for transfers between devices: 160 us -> 153 us
    ppermute x0 -> x2, waiting for transfers between devices: none -> 42 us  [the longest x1 22.3 us: per_device(): lax.ppermute(joined_even, 'narrow', narrow_pairs(narrow_count, 1))]
    ppermute x6 -> x3, waiting for transfers between devices: 47.1 us -> 12.4 us  [gather_narrow(): lax.ppermute(block, 'narrow', narrow_pairs(count, step))]
    ppermute x3, starting transfers between devices: 12.4 us -> 0.13 us  [line_first(): came = lax.ppermute(sent, 'narrow', narrow_pairs(narrow_count, 1))]
    ppermute x3, waiting for transfers between devices: 28.9 us -> 22.1 us  [gather_early(): held = jnp.concatenate([held, lax.ppermute(held, 'wide', pairs)], axis=0)]
    ppermute x6 -> x3, starting transfers between devices: 12.2 us -> 5.62 us  [gather_narrow(): lax.ppermute(block, 'narrow', narrow_pairs(count, step))]
    ppermute x3, waiting for transfers between devices: 8.83 us -> 2.59 us  [scatter_narrow(): lax.ppermute(pick(blocks, narrow ^ step).astype(BF16), 'narrow', narrow_p...]
    ppermute x3, starting transfers between devices: 3.06 us -> 8.93 us  [line_second(): lax.ppermute(sent, 'narrow', narrow_pairs(narrow_count, 2 * place))]
  transfers between devices with their start and end apart: 59 -> 58, of which waited for: 23 -> 23; matrix products, arithmetic and copies ran while one was open for 9% -> 10% of each run, Pallas kernels for 30% -> 31%
where the time goes in v4:
time: 500 us; the launch traced here: 490 us
  Pallas kernels  203 us (41%)
  waiting for transfers between devices  153 us (31%)
  starting transfers between devices  53.5 us (11%)
  other arithmetic  52.7 us (11%)
  between operations  17.5 us (4%)
  local copies, waits for them, and re-layouts  10.6 us (2%)
    pallas_call x2, Pallas kernels, table_half(): pl.pallas_call(functools.partial(exit_table_kernel, first=side * half, vo...  26.6 us
    pallas_call x1, Pallas kernels, per_device(): pl.pallas_call(functools.partial(exit_scores_kernel, vocab=vocab, scale=s...  24.6 us
    pallas_call x1, Pallas kernels, per_device(): pl.pallas_call(functools.partial(exit_tokens_kernel, vocab=vocab), grid_s...  23.5 us
    ppermute x1, waiting for transfers between devices, per_device(): lax.ppermute(joined_even, 'narrow', narrow_pairs(narrow_count, 1))  22.3 us
    ppermute x3, waiting for transfers between devices, gather_early(): held = jnp.concatenate([held, lax.ppermute(held, 'wide', pairs)], axis=0)  22.1 us
    pallas_call x1, Pallas kernels, per_device(): pl.pallas_call(mlp_backward_kernel, in_specs=[SMEM] + [VMEM] * 8 + [ANY]...  20 us
    ppermute x1, waiting for transfers between devices, per_device(): lax.ppermute(joined_even, 'narrow', narrow_pairs(narrow_count, step))  19.7 us
    pallas_call x1, Pallas kernels, per_device(): pl.pallas_call(cross_backward_kernel, in_specs=[SMEM] + [VMEM] * 11 + [AN...  17 us
  transfers between devices with their start and end apart: 58, of which 23 were waited for; matrix products, arithmetic and copies ran while one was open for 10% of the time, Pallas kernels for 31%

profile of v4, /device:TPU:0, one launch (start us, length us, event | category | flops | bytes accessed | tf_op | source)
XLA Modules:
  0.0 489.9 jit_solution(9160191701700145310)
XLA Ops:
  19.9 8.3 %collective-permute-done.1.refs_2_ = bf16[104,768]{1,0:T(8,128)(2,1)S(1)} collective-permute-done((bf16[104,768]{1,0:T(8,128)(2,1)}, bf16[104,768]{1,0:T(8,128)(2,1)S(1)}, u32[]{:S(2)}, u32[]{:S(2)}) %collective-permute-start.1) | collective-permute-done | bytes 159776 | tf_op jit(solution)/shard_map/ppermute | solution.py:139
  37.8 19.7 %collective-permute-done.3 = bf16[304,768]{1,0:T(8,128)(2,1)S(1)} collective-permute-done((bf16[304,768]{1,0:T(8,128)(2,1)}, bf16[304,768]{1,0:T(8,128)(2,1)S(1)}, u32[]{:S(2)}, u32[]{:S(2)}) %collective-permute-start.3) | collective-permute-done | bytes 466976 | tf_op jit(solution)/shard_map/ppermute | solution.py:1061
  59.6 22.3 %collective-permute-done.4.odd = bf16[2,304,768]{2,1,0:T(8,128)(2,1)} collective-permute-done((bf16[2,304,768]{2,1,0:T(8,128)(2,1)S(1)}, bf16[2,304,768]{2,1,0:T(8,128)(2,1)}, u32[]{:S(2)}, u32[]{:S(2)}) %collective-permute-start.4) | collective-permute-done | bytes 933920 | tf_op jit(solution)/shard_map/ppermute | solution.py:1065
  87.2 12.0 %collective-permute-done.7 = bf16[1,640,768]{2,1,0:T(8,128)(2,1)} collective-permute-done((bf16[1,640,768]{2,1,0:T(8,128)(2,1)}, bf16[1,640,768]{2,1,0:T(8,128)(2,1)}, u32[]{:S(2)}, u32[]{:S(2)}) %collective-permute-start.7) | collective-permute-done | bytes 983072 | tf_op jit(solution)/shard_map/ppermute | solution.py:1053
  106.6 9.6 %self_forward.1 = (bf16[320,768]{1,0:T(8,128)(2,1)}, bf16[320,768]{1,0:T(8,128)(2,1)}, bf16[320,768]{1,0:T(8,128)(2,1)}, bf16[320,768]{1,0:T(8,128)(2,1)}, bf16[...) custom-call(s32[8]{0:T(128)} %fusion.43.places, s32[2]{0:T(128)} %bitcast.112, ...), custom_call_target="tpu_custom_call" | custom-call | flops 1000000000 | bytes 1000000 | tf_op jit(solution)/shard_map/self_forward/pallas_call | solution.py:1105
  116.2 9.7 %collective-permute-done.10.refs_1_.refs_5_ = bf16[2,640,768]{2,1,0:T(8,128)(2,1)} collective-permute-done((bf16[2,640,768]{2,1,0:T(8,128)(2,1)S(1)}, bf16[2,640,768]{2,1,0:T(8,128)(2,1)}, u32[]{:S(2)}, u32[]{:S(2)}) %collective-permute-start.10) | collective-permute-done | bytes 1966112 | tf_op jit(solution)/shard_map/ppermute | solution.py:1094
  127.9 10.1 %collective-permute-done.11 = bf16[1,192,2048]{2,1,0:T(8,128)(2,1)S(1)} collective-permute-done((bf16[1,192,2048]{2,1,0:T(8,128)(2,1)S(1)}, bf16[1,192,2048]{2,1,0:T(8,128)(2,1)S(1)}, u32[]{:S(2)}, u32[]{:S(2)}) %collective-permute-start.11) | collective-permute-done | bytes 786464 | tf_op jit(solution)/shard_map/ppermute | solution.py:1053
  141.1 7.1 %memory_projection.1 = (bf16[1024,768]{1,0:T(8,128)(2,1)}, bf16[1024,768]{1,0:T(8,128)(2,1)}) custom-call(s32[8]{0:T(128)} %fusion.43.places, bf16[1024,768]{1,0:T(8,128)(2,1)} %memory.3, bf16[2,640,768]{2,1,0:T(8,128)(2,1)} %copy-done, bf16[2,640,768]{2,1,0:T(8,128)(2,1)} %collective-permute-done.10.refs_1_.refs_5_, bf16[2,640,768]{2,1,0:T(8,128)(2,1)} %copy-done.1, ...), custom_call_target="tpu_custom_call" | custom-call | flops 1000000000 | bytes 1000000 | tf_op jit(solution)/shard_map/memory_projection/pallas_call | solution.py:1140
  148.2 14.2 %cross_forward.1 = (bf16[320,768]{1,0:T(8,128)(2,1)}, bf16[320,768]{1,0:T(8,128)(2,1)}, bf16[320,768]{1,0:T(8,128)(2,1)}, f32[6,1,640]{2,1,0:T(1,128)}, f32[320,768]{1,0:T(8,128)}) custom-call(s32[8]{0:T(128)} %fusion.43.places, s32[2]{0:T(128)} %bitcast.113, s32[2]{0:T(128)} %bitcast.117, f32[320,768]{1,0:T(8,128)} %get-tuple-element.146.stream_in, ...), custom_call_target="tpu_custom_call" | custom-call | flops 1000000000 | bytes 1000000 | tf_op jit(solution)/shard_map/cross_forward/pallas_call | solution.py:1154
  167.3 11.2 %mlp_forward.1 = (bf16[320,768]{1,0:T(8,128)(2,1)}, f32[320,2048]{1,0:T(8,128)}, f32[320,2048]{1,0:T(8,128)}, bf16[320,2048]{1,0:T(8,128)(2,1)}, f32[320,768]{1,...) custom-call(s32[8]{0:T(128)} %fusion.43.places, f32[320,768]{1,0:T(8,128)} %get-tuple-element.150.stream_in.stream_two, ...), custom_call_target="tpu_custom_call" | custom-call | flops 1000000000 | bytes 1000000 | tf_op jit(solution)/shard_map/mlp_forward/pallas_call | solution.py:1180
  180.2 7.6 %collective-permute-done.17 = bf16[1,328,768]{2,1,0:T(8,128)(2,1)S(1)} collective-permute-done((bf16[1,328,768]{2,1,0:T(8,128)(2,1)}, bf16[1,328,768]{2,1,0:T(8,128)(2,1)S(1)}, u32[]{:S(2)}, u32[]{:S(2)}) %collective-permute-start.17) | collective-permute-done | bytes 503840 | tf_op jit(solution)/shard_map/ppermute | solution.py:96
  190.5 12.8 %collective-permute-done.18.refs_1_ = bf16[2,328,768]{2,1,0:T(8,128)(2,1)S(1)} collective-permute-done((bf16[2,328,768]{2,1,0:T(8,128)(2,1)S(1)}, bf16[2,328,768]{2,1,0:T(8,128)(2,1)S(1)}, u32[]{:S(2)}, u32[]{:S(2)}) %collective-permute-start.18) | collective-permute-done | bytes 1007648 | tf_op jit(solution)/shard_map/ppermute | solution.py:97
  208.2 24.6 %exit_scores.1 = (bf16[2560,4096]{1,0:T(8,128)(2,1)}, bf16[768,2560]{1,0:T(8,128)(2,1)}, f32[8,2560]{1,0:T(8,128)}) custom-call(s32[18]{0:T(128)} %pad_add_fusion.meta, s32[8]{0:T(128)} %select_reduce_fusion.slot_of, bf16[2,328,768]{2,1,0:T(8,128)(2,1)} %copy-done.10, bf16[2,328,768]{2,1,0:T(8,128)(2,1)} %copy-done.25, bf16[2,328,768]{2,1,0:T(8,128)(2,1)} %copy-done.26, ...), custom_call_target="tpu_custom_call" | custom-call | flops 51999997952 | bytes 1000000 | tf_op jit(solution)/shard_map/exit_scores/pallas_call | solution.py:1205
  247.6 23.5 %exit_tokens.1 = (bf16[2,320,768]{2,1,0:T(8,128)(2,1)}, bf16[2,320,768]{2,1,0:T(8,128)(2,1)}, bf16[2,320,768]{2,1,0:T(8,128)(2,1)}, bf16[2,320,768]{2,1,0:T(8,128)(2,1)}) custom-call(s32[18]{0:T(128)} %pad_add_fusion.meta, s32[8]{0:T(128)} %fusion.43.places, bf16[768,4096]{1,0:T(8,128)(2,1)} %all-gather.2.cloned.1.call-done.refs_4_.refs_0_, ...), custom_call_target="tpu_custom_call" | custom-call | flops 49999998976 | bytes 1000000 | tf_op jit(solution)/shard_map/exit_tokens/pallas_call | solution.py:1251
  271.7 13.2 %exit_table.2.refs_0_ = bf16[768,4096]{1,0:T(8,128)(2,1)} custom-call(s32[18]{0:T(128)} %pad_add_fusion.meta, bf16[2560,4096]{1,0:T(8,128)(2,1)} %get-tuple-element.156.refs_1_.raised, bf16[768,2560]{1,0:T(8,128)(2,1)} %get-tuple-element.161.across, f32[8,2560]{1,0:T(8,128)} %maximum_maximum_fusion.2.refs_2_.factors), custom_call_target="tpu_custom_call" | custom-call | flops 15000000512 | bytes 1000000 | tf_op jit(solution)/shard_map/exit_table/pallas_call | solution.py:1279
  286.8 13.4 %exit_table.3 = bf16[768,4096]{1,0:T(8,128)(2,1)} custom-call(s32[18]{0:T(128)} %pad_add_fusion.meta, bf16[2560,4096]{1,0:T(8,128)(2,1)} %get-tuple-element.156.refs_1_.raised, bf16[768,2560]{1,0:T(8,128)(2,1)} %get-tuple-element.161.across, f32[8,2560]{1,0:T(8,128)} %maximum_maximum_fusion.2.refs_2_.factors, ...), custom_call_target="tpu_custom_call", output_to_operand_aliasing={{}: (4, {})} | custom-call | flops 15000000512 | bytes 1000000 | tf_op jit(solution)/shard_map/exit_table/pallas_call | solution.py:1279
  303.1 7.3 %collective-permute-done.27 = bf16[320,768]{1,0:T(8,128)(2,1)S(1)} collective-permute-done((bf16[320,768]{1,0:T(8,128)(2,1)S(1)}, bf16[320,768]{1,0:T(8,128)(2,1)S(1)}, u32[]{:S(2)}, u32[]{:S(2)}) %collective-permute-start.27) | collective-permute-done | bytes 491552 | tf_op jit(solution)/shard_map/ppermute | solution.py:117
  312.6 20.0 %mlp_backward.1 = (f32[320,768]{1,0:T(8,128)}, f32[8,768]{1,0:T(8,128)}, bf16[2,192,2048]{2,1,0:T(8,128)(2,1)}, bf16[2,192,2048]{2,1,0:T(8,128)(2,1)}, bf16[2,19...) custom-call(s32[8]{0:T(128)} %fusion.43.places, ...), custom_call_target="tpu_custom_call" | custom-call | flops 15000000512 | bytes 1000000 | tf_op jit(solution)/shard_map/mlp_backward/pallas_call | solution.py:1311
  334.3 11.0 %cross_attention_first.1 = (bf16[320,768]{1,0:T(8,128)(2,1)}, bf16[320,768]{1,0:T(8,128)(2,1)}, bf16[320,384]{1,0:T(8,128)(2,1)}, bf16[1024,384]{1,0:T(8,128)(2,1)}, bf16[1024,384]{1,0:T(8,128)(2,1)}) custom-call(s32[8]{0:T(128)} %fusion.43.places, s32[2]{0:T(128)} %bitcast.114, s32[2]{0:T(128)} %bitcast.118, f32[320,768]{1,0:T(8,128)} %get-tuple-element.171.grad_in, ...), custom_call_target="tpu_custom_call" | custom-call | flops 16000000000 | bytes 1000000 | tf_op jit(solution)/shard_map/cross_attention_first/pallas_call | solution.py:1353
  351.5 10.8 %cross_attention_last.1 = (bf16[320,768]{1,0:T(8,128)(2,1)}, bf16[1024,768]{1,0:T(8,128)(2,1)}, bf16[1024,768]{1,0:T(8,128)(2,1)}) custom-call(s32[2]{0:T(128)} %bitcast.115, s32[2]{0:T(128)} %bitcast.119, bf16[320,768]{1,0:T(8,128)(2,1)} %get-tuple-element.182.attended_grad, bf16[320,768]{1,0:T(8,128)(2,1)} %get-tuple-element.172.query, ...), custom_call_target="tpu_custom_call" | custom-call | flops 16000000000 | bytes 1000000 | tf_op jit(solution)/shard_map/cross_attention_last/pallas_call | solution.py:1372
  369.5 17.0 %cross_backward.1 = (f32[320,768]{1,0:T(8,128)}, f32[8,768]{1,0:T(8,128)}, f32[1024,768]{1,0:T(8,128)}, bf16[320,768]{1,0:T(8,128)(2,1)}, bf16[2,480,768]{2,1,0:...) custom-call(s32[8]{0:T(128)} %fusion.43.places, ...), custom_call_target="tpu_custom_call" | custom-call | flops 20000000000 | bytes 1000000 | tf_op jit(solution)/shard_map/cross_backward/pallas_call | solution.py:1392
  395.6 8.5 %self_attention_backward.1 = (bf16[320,768]{1,0:T(8,128)(2,1)}, bf16[320,768]{1,0:T(8,128)(2,1)}, bf16[320,768]{1,0:T(8,128)(2,1)}) custom-call(s32[8]{0:T(128)} %fusion.43.places, s32[2]{0:T(128)} %bitcast.116, bf16[320,768]{1,0:T(8,128)(2,1)} %get-tuple-element.201.branch, bf16[320,768]{1,0:T(8,128)(2,1)} %get-tuple-element.202.query, ...), custom_call_target="tpu_custom_call" | custom-call | flops 10000000000 | bytes 1000000 | tf_op jit(solution)/shard_map/self_attention_backward/pallas_call | solution.py:1416
  410.3 10.7 %self_backward.1 = (f32[320,768]{1,0:T(8,128)}, bf16[2,320,768]{2,1,0:T(8,128)(2,1)}, bf16[2,320,768]{2,1,0:T(8,128)(2,1)}, bf16[2,320,768]{2,1,0:T(8,128)(2,1)}, bf16[2,320,768]{2,1,0:T(8,128)(2,1)}) custom-call(s32[8]{0:T(128)} %fusion.43.places, f32[320,768]{1,0:T(8,128)} %get-tuple-element.211.grad_in, bf16[320,768]{1,0:T(8,128)(2,1)} %inputs.2, ...), custom_call_target="tpu_custom_call" | custom-call | flops 12000000000 | bytes 1000000 | tf_op jit(solution)/shard_map/self_backward/pallas_call | solution.py:1468
  422.4 7.0 %collective-permute-done.42 = bf16[2,480,768]{2,1,0:T(8,128)(2,1)} collective-permute-done((bf16[2,480,768]{2,1,0:T(8,128)(2,1)}, bf16[2,480,768]{2,1,0:T(8,128)(2,1)}, u32[]{:S(2)}, u32[]{:S(2)}) %collective-permute-start.42) | collective-permute-done | bytes 1474592 | tf_op jit(solution)/shard_map/ppermute | solution.py:108
  (250 shorter events, 161.0 us)
Async XLA Ops:
  7.2 200.0 %all-gather.2.cloned.1.call-start = ((), (), s32[]{:S(2)}) async-start(), calls=%async_computation.1 | async-start | bytes 7864320 | tf_op jit(solution)/shard_map/all_gather | solution.py:1046
  30.9 27.7 %collective-permute-start.5 = (bf16[1,416,768]{2,1,0:T(8,128)(2,1)}, bf16[1,416,768]{2,1,0:T(8,128)(2,1)S(1)}, u32[]{:S(2)}, u32[]{:S(2)}) collective-permute-start(bf16[1,416,768]{2,1,0:T(8,128)(2,1)} %bitcast.104), channel_id=1, source_target_pairs={{0,8},{4,20},{8,0},{12,28},{16,24},{20,4},{24,16},{28,12},{1,9},{5... | collective-permute-start | bytes 1916936 | tf_op jit(solution)/shard_map/ppermute | solution.py:1053
  34.3 23.2 %collective-permute-start.3 = (bf16[304,768]{1,0:T(8,128)(2,1)}, bf16[304,768]{1,0:T(8,128)(2,1)S(1)}, u32[]{:S(2)}, u32[]{:S(2)}) collective-permute-start(bf16[304,768]{1,0:T(8,128)(2,1)} %join_wide.1), channel_id=1, source_target_pairs={{0,2},{1,3},{2,0},{3,1},{4,6},{5,7},{6,4},{7,5},{8,10},{9,11},{10,... | collective-permute-start | bytes 1400840 | tf_op jit(solution)/shard_map/ppermute | solution.py:1061
  58.8 26.0 %collective-permute-start.6 = (bf16[2,416,768]{2,1,0:T(8,128)(2,1)S(1)}, bf16[2,416,768]{2,1,0:T(8,128)(2,1)}, u32[]{:S(2)}, u32[]{:S(2)}) collective-permute-start(bf16[2,416,768]{2,1,0:T(8,128)(2,1)S(1)} %pad_maximum_fusion.2.refs_0_), channel_id=1, source_target_pairs={{0,16},{4,12},{8,24},{12,4},{16,0},{20,28},{24,8},{28,20},{1,17},{... | collective-permute-start | bytes 3833864 | tf_op jit(solution)/shard_map/ppermute | solution.py:1072
  59.6 22.3 %collective-permute-start.4 = (bf16[2,304,768]{2,1,0:T(8,128)(2,1)S(1)}, bf16[2,304,768]{2,1,0:T(8,128)(2,1)}, u32[]{:S(2)}, u32[]{:S(2)}) collective-permute-start(bf16[2,304,768]{2,1,0:T(8,128)(2,1)S(1)} %pad_maximum_fusion.4.even), channel_id=1, source_target_pairs={{0,1},{1,0},{2,3},{3,2},{4,5},{5,4},{6,7},{7,6},{8,9},{9,8},{10,11... | collective-permute-start | bytes 2801672 | tf_op jit(solution)/shard_map/ppermute | solution.py:1065
  87.1 354.9 %reduce-scatter.2.cloned.1.call-start = ((), (), s32[]{:S(2)}) async-start(), calls=%async_computation.2 | async-start | bytes 7864320 | tf_op jit(solution)/shard_map/reduce_scatter | solution.py:1305
  100.9 25.0 %collective-permute-start.10 = (bf16[2,640,768]{2,1,0:T(8,128)(2,1)S(1)}, bf16[2,640,768]{2,1,0:T(8,128)(2,1)}, u32[]{:S(2)}, u32[]{:S(2)}) collective-permute-start(bf16[2,640,768]{2,1,0:T(8,128)(2,1)S(1)} %pad_maximum_fusion.refs_0_.refs_4_), channel_id=1, source_target_pairs={{0,16},{4,12},{8,24},{12,4},{16,0},{20,28},{24,8},{28,20},{1,17},{... | collective-permute-start | bytes 5898248 | tf_op jit(solution)/shard_map/ppermute | solution.py:1094
  139.2 23.1 %collective-permute-start.14 = (bf16[2,192,2048]{2,1,0:T(8,128)(2,1)S(1)}, bf16[2,192,2048]{2,1,0:T(8,128)(2,1)}, u32[]{:S(2)}, u32[]{:S(2)}) collective-permute-start(bf16[2,192,2048]{2,1,0:T(8,128)(2,1)S(1)} %pad_maximum_fusion.1.refs_0_), channel_id=1, source_target_pairs={{0,16},{4,12},{8,24},{12,4},{16,0},{20,28},{24,8},{28,20},{1,17},{... | collective-permute-start | bytes 4718600 | tf_op jit(solution)/shard_map/ppermute | solution.py:1137
  139.8 23.8 %collective-permute-start.15 = (bf16[2,192,2048]{2,1,0:T(8,128)(2,1)S(1)}, bf16[2,192,2048]{2,1,0:T(8,128)(2,1)}, u32[]{:S(2)}, u32[]{:S(2)}) collective-permute-start(bf16[2,192,2048]{2,1,0:T(8,128)(2,1)S(1)} %pad_maximum_fusion.1.refs_0_), channel_id=1, source_target_pairs={{0,4},{4,0},{8,12},{12,8},{16,20},{20,16},{24,28},{28,24},{1,5},{5... | collective-permute-start | bytes 4718600 | tf_op jit(solution)/shard_map/ppermute | solution.py:89
  190.5 16.8 %collective-permute-start.19 = (bf16[2,328,768]{2,1,0:T(8,128)(2,1)S(1)}, bf16[2,328,768]{2,1,0:T(8,128)(2,1)S(1)}, u32[]{:S(2)}, u32[]{:S(2)}) collective-permute-start(bf16[2,328,768]{2,1,0:T(8,128)(2,1)S(1)} %pad_maximum_fusion.3.refs_0_), channel_id=1, source_target_pairs={{0,4},{4,0},{8,12},{12,8},{16,20},{20,16},{24,28},{28,24},{1,5},{5... | collective-permute-start | bytes 3022856 | tf_op jit(solution)/shard_map/ppermute | solution.py:89
  271.1 29.1 %collective-permute-start.24 = (bf16[2,320,768]{2,1,0:T(8,128)(2,1)}, bf16[2,320,768]{2,1,0:T(8,128)(2,1)S(1)}, u32[]{:S(2)}, u32[]{:S(2)}) collective-permute-start(bf16[2,320,768]{2,1,0:T(8,128)(2,1)} %get-tuple-element.158), channel_id=1, source_target_pairs={{0,4},{4,0},{8,12},{12,8},{16,20},{20,16},{24,28},{28,24},{1,5},{5... | collective-permute-start | bytes 2949128 | tf_op jit(solution)/shard_map/ppermute | solution.py:89
  333.8 57.5 %collective-permute-start.33 = (bf16[2,192,2048]{2,1,0:T(8,128)(2,1)}, bf16[2,192,2048]{2,1,0:T(8,128)(2,1)S(1)}, u32[]{:S(2)}, u32[]{:S(2)}) collective-permute-start(bf16[2,192,2048]{2,1,0:T(8,128)(2,1)} %get-tuple-element.195), channel_id=1, source_target_pairs={{0,4},{4,0},{8,12},{12,8},{16,20},{20,16},{24,28},{28,24},{1,5},{5... | collective-permute-start | bytes 4718600 | tf_op jit(solution)/shard_map/ppermute | solution.py:89
  333.8 52.7 %collective-permute-start.36 = (bf16[2,256,768]{2,1,0:T(8,128)(2,1)}, bf16[2,256,768]{2,1,0:T(8,128)(2,1)}, u32[]{:S(2)}, u32[]{:S(2)}) collective-permute-start(bf16[2,256,768]{2,1,0:T(8,128)(2,1)} %get-tuple-element.199), channel_id=1, source_target_pairs={{0,4},{4,0},{8,12},{12,8},{16,20},{20,16},{24,28},{28,24},{1,5},{5... | collective-permute-start | bytes 2359304 | tf_op jit(solution)/shard_map/ppermute | solution.py:89
  347.7 38.8 %collective-permute-start.37 = (bf16[2,256,768]{2,1,0:T(8,128)(2,1)}, bf16[2,256,768]{2,1,0:T(8,128)(2,1)}, u32[]{:S(2)}, u32[]{:S(2)}) collective-permute-start(bf16[2,256,768]{2,1,0:T(8,128)(2,1)} %add.288), channel_id=1, source_target_pairs={{0,16},{4,12},{8,24},{12,4},{16,0},{20,28},{24,8},{28,20},{1,17},{... | collective-permute-start | bytes 2359304 | tf_op jit(solution)/shard_map/ppermute | solution.py:108
  350.8 40.5 %collective-permute-start.34 = (bf16[2,192,2048]{2,1,0:T(8,128)(2,1)}, bf16[2,192,2048]{2,1,0:T(8,128)(2,1)}, u32[]{:S(2)}, u32[]{:S(2)}) collective-permute-start(bf16[2,192,2048]{2,1,0:T(8,128)(2,1)} %add.287), channel_id=1, source_target_pairs={{0,16},{4,12},{8,24},{12,4},{16,0},{20,28},{24,8},{28,20},{1,17},{... | collective-permute-start | bytes 4718600 | tf_op jit(solution)/shard_map/ppermute | solution.py:108
  362.9 26.0 %collective-permute-start.32 = (f32[8,128]{1,0:T(8,128)S(1)}, f32[8,128]{1,0:T(8,128)S(1)}, u32[]{:S(2)}, u32[]{:S(2)}) collective-permute-start(f32[8,128]{1,0:T(8,128)S(1)} %broadcast_in_dim.73), channel_id=1, source_target_pairs={{0,3},{1,2},{2,1},{3,0},{4,7},{5,6},{6,5},{7,4},{8,11},{9,10},{10,... | collective-permute-start | bytes 12296 | tf_op jit(solution)/shard_map/ppermute | solution.py:1389
  391.3 38.1 %collective-permute-start.41 = (bf16[2,480,768]{2,1,0:T(8,128)(2,1)}, bf16[2,480,768]{2,1,0:T(8,128)(2,1)}, u32[]{:S(2)}, u32[]{:S(2)}) collective-permute-start(bf16[2,480,768]{2,1,0:T(8,128)(2,1)} %get-tuple-element.224), channel_id=1, source_target_pairs={{0,4},{4,0},{8,12},{12,8},{16,20},{20,16},{24,28},{28,24},{1,5},{5... | collective-permute-start | bytes 4423688 | tf_op jit(solution)/shard_map/ppermute | solution.py:89
  407.3 22.1 %collective-permute-start.42 = (bf16[2,480,768]{2,1,0:T(8,128)(2,1)}, bf16[2,480,768]{2,1,0:T(8,128)(2,1)}, u32[]{:S(2)}, u32[]{:S(2)}) collective-permute-start(bf16[2,480,768]{2,1,0:T(8,128)(2,1)} %add.300), channel_id=1, source_target_pairs={{0,16},{4,12},{8,24},{12,4},{16,0},{20,28},{24,8},{28,20},{1,17},{... | collective-permute-start | bytes 4423688 | tf_op jit(solution)/shard_map/ppermute | solution.py:108
  429.4 24.4 %collective-permute-start.39 = (bf16[2,320,768]{2,1,0:T(8,128)(2,1)}, bf16[2,320,768]{2,1,0:T(8,128)(2,1)}, u32[]{:S(2)}, u32[]{:S(2)}) collective-permute-start(bf16[2,320,768]{2,1,0:T(8,128)(2,1)} %get-tuple-element.220), channel_id=1, source_target_pairs={{0,4},{4,0},{8,12},{12,8},{16,20},{20,16},{24,28},{28,24},{1,5},{5... | collective-permute-start | bytes 2949128 | tf_op jit(solution)/shard_map/ppermute | solution.py:89
  431.9 17.5 %collective-permute-start.44 = (bf16[480,768]{1,0:T(8,128)(2,1)}, bf16[480,768]{1,0:T(8,128)(2,1)S(1)}, u32[]{:S(2)}, u32[]{:S(2)}) collective-permute-start(bf16[480,768]{1,0:T(8,128)(2,1)} %fusion.1), channel_id=1, source_target_pairs={{0,8},{4,20},{8,0},{12,28},{16,24},{20,4},{24,16},{28,12},{1,9},{5... | collective-permute-start | bytes 2211848 | tf_op jit(solution)/shard_map/ppermute | solution.py:117
  434.8 19.0 %collective-permute-start.43 = (bf16[2,320,768]{2,1,0:T(8,128)(2,1)}, bf16[2,320,768]{2,1,0:T(8,128)(2,1)}, u32[]{:S(2)}, u32[]{:S(2)}) collective-permute-start(bf16[2,320,768]{2,1,0:T(8,128)(2,1)} %add.304), channel_id=1, source_target_pairs={{0,16},{4,12},{8,24},{12,4},{16,0},{20,28},{24,8},{28,20},{1,17},{... | collective-permute-start | bytes 2949128 | tf_op jit(solution)/shard_map/ppermute | solution.py:108
  438.1 17.5 %collective-permute-start.49 = (bf16[2,64,768]{2,1,0:T(8,128)(2,1)}, bf16[2,64,768]{2,1,0:T(8,128)(2,1)}, u32[]{:S(2)}, u32[]{:S(2)}) collective-permute-start(bf16[2,64,768]{2,1,0:T(8,128)(2,1)} %pad_maximum_fusion.7), channel_id=1, source_target_pairs={{0,1},{1,0},{2,3},{3,2},{4,5},{5,4},{6,7},{7,6},{8,9},{9,8},{10,11... | collective-permute-start | bytes 589832 | tf_op jit(solution)/shard_map/ppermute | solution.py:1451
  438.8 17.8 %collective-permute-start.54 = (bf16[48,2048]{1,0:T(8,128)(2,1)}, bf16[48,2048]{1,0:T(8,128)(2,1)S(1)}, u32[]{:S(2)}, u32[]{:S(2)}) collective-permute-start(bf16[48,2048]{1,0:T(8,128)(2,1)} %get-tuple-element.262), channel_id=1, source_target_pairs={{0,2},{1,3},{2,0},{3,1},{4,6},{5,7},{6,4},{7,5},{8,10},{9,11},{10,... | collective-permute-start | bytes 589832 | tf_op jit(solution)/shard_map/ppermute | solution.py:1460
  460.7 17.0 %collective-permute-start.53 = (bf16[120,768]{1,0:T(8,128)(2,1)S(1)}, bf16[120,768]{1,0:T(8,128)(2,1)S(1)}, u32[]{:S(2)}, u32[]{:S(2)}) collective-permute-start(bf16[120,768]{1,0:T(8,128)(2,1)S(1)} %get-tuple-element.264), channel_id=1, source_target_pairs={{0,2},{1,3},{2,0},{3,1},{4,6},{5,7},{6,4},{7,5},{8,10},{9,11},{10,... | collective-permute-start | bytes 552968 | tf_op jit(solution)/shard_map/ppermute | solution.py:1460
  (64 other events, 718.9 us)
Sparse Core Ops, SparseCore 0:
  87.2 112.1 all-gather.1
  303.2 113.6 reduce-scatter.1

commit v5 on v4

--- a/solution.py
+++ b/solution.py
@@ -354,50 +354,14 @@
         start += size
 
 
-def join_wide_kernel(*refs):
-    block = refs[-1]
-    width = block.shape[1]
-    start, spot = 0, 0
-    for ref in refs[:-1]:
-        if ref.shape[1] == width:
-            block[start : start + ref.shape[0], :] = ref[...]
-            start += ref.shape[0]
-    for ref in refs[:-1]:
-        if ref.shape[1] != width:
-            for first in range(0, ref.shape[1], LANES):
-                top = start + spot // (width // LANES) * ref.shape[0]
-                left = spot % (width // LANES) * LANES
-                block[top : top + ref.shape[0], left : left + LANES] = ref[:, first : first + LANES]
-                spot += 1
-            size = ref.shape[0]
-    while spot % (width // LANES):
-        top = start + spot // (width // LANES) * size
-        left = spot % (width // LANES) * LANES
-        block[top : top + size, left : left + LANES] = jnp.zeros((size, LANES), BF16)
-        spot += 1
-
-
-def line_wide_kernel(narrow, even, odd, block, wide_block, *, sizes, wide_size):
+def line_pair_kernel(narrow, even, odd, block, *, sizes):
     pieces = [(odd if step % 2 else even).at[step // 2] for step in range(2 * even.shape[0])]
-    count, width = len(pieces), block.shape[1]
     start = 0
     for size in sizes:
         for step, piece in enumerate(pieces):
-            place = pl.multiple_of(start * count + (narrow[0] ^ step) * size, 8)
+            place = pl.multiple_of(start * len(pieces) + (narrow[0] ^ step) * size, 8)
             block[pl.ds(place, size), :] = piece[start : start + size]
         start += size
-    matrices = wide_block.shape[0] // (count * wide_size)
-    spot = 0
-    for matrix in range(matrices):
-        for first in range(0, wide_block.shape[1], LANES):
-            top = start + spot // (width // LANES) * wide_size
-            left = spot % (width // LANES) * LANES
-            for step, piece in enumerate(pieces):
-                place = pl.multiple_of((matrix * count + (narrow[0] ^ step)) * wide_size, 8)
-                wide_block[pl.ds(place, wide_size), first : first + LANES] = piece[
-                    top : top + wide_size, left : left + LANES
-                ]
-            spot += 1
 
 
 def self_forward_kernel(
@@ -1023,17 +987,6 @@
         else join_rows(self_query, self_key, self_value, self_out, own_rows)
     )
     members = (cross_query, cross_key, cross_value, cross_out, mlp_down)
-    if aligned:
-        wide_rows = -(-2 * hidden_width // model) * shard
-        joined_pack = pl.pallas_call(
-            join_wide_kernel,
-            in_specs=[VMEM] * 7,
-            out_specs=VMEM,
-            out_shape=like((sum(cross_sizes) + wide_rows, model), BF16),
-            compiler_params=PARAMS,
-            cost_estimate=work(1),
-            name="join_wide",
-        )(*members, mlp_gate, mlp_up)
     side = jnp.stack([targets // 256, targets % 256]).astype(BF16)
     side = jnp.pad(side, ((0, 6), (0, model - tokens)))
 
@@ -1047,50 +1000,62 @@
 
     *early, last = stage_pairs(wide_count)
 
-    def gather_early(block):
+    def gather_early(block, *others):
         held = block[None]
         for pairs in early:
-            held = jnp.concatenate([held, lax.ppermute(held, "wide", pairs)], axis=0)
+            came = lax.ppermute(held, "wide", pairs)
+            if others:
+                came = tie(came, *others)
+            held = jnp.concatenate([held, came], axis=0)
         return held
 
-    if aligned:
-        joined_even = tie(joined_pack, *self_line)
-        joined_even = jnp.stack(
-            [joined_even]
+    cross_pack, gate_pack = join_rows(*members), join_rows(mlp_gate, mlp_up)
+
+    def line_even(pack):
+        return jnp.stack(
+            [pack]
             + [
-                lax.ppermute(joined_even, "narrow", narrow_pairs(narrow_count, step))
+                lax.ppermute(pack, "narrow", narrow_pairs(narrow_count, step))
                 for step in range(2, narrow_count, 2)
             ]
         )
-        joined_odd = lax.ppermute(joined_even, "narrow", narrow_pairs(narrow_count, 1))
-    else:
-        cross_line = gather_narrow(join_rows(*members), narrow_count)
-        gate_line = gather_narrow(join_rows(mlp_gate, mlp_up), narrow_count)
+
+    def line_odd(even):
+        return lax.ppermute(even, "narrow", narrow_pairs(narrow_count, 1))
+
+    def line_pair(even, odd, sizes):
+        return pl.pallas_call(
+            functools.partial(line_pair_kernel, sizes=sizes),
+            in_specs=[SMEM] + [VMEM] * 2,
+            out_specs=VMEM,
+            out_shape=like((narrow_count * even.shape[1], even.shape[2]), BF16),
+            compiler_params=PARAMS,
+            cost_estimate=work(1),
+            name="line_pair",
+        )(narrow[None], even, odd)
+
     self_held = gather_early(self_block)
     if aligned:
-        self_held = tie(self_held, joined_even)
+        cross_even = line_even(tie(cross_pack, *self_line))
+        cross_odd = line_odd(cross_even)
+        gate_even = line_even(tie(gate_pack, cross_even))
+        gate_odd = line_odd(gate_even)
+        self_held = tie(self_held, cross_even)
+        cross_block = line_pair(cross_even, tie(cross_odd, self_held), cross_sizes)
+    else:
+        cross_block = line_block(gather_narrow(cross_pack, narrow_count), cross_sizes)
+        gate_block = line_block(gather_narrow(gate_pack, narrow_count), gate_sizes)
     self_came = lax.ppermute(self_held, "wide", last)
-    if aligned:
-        joined_odd = tie(joined_odd, self_held)
-        cross_block, gate_block = pl.pallas_call(
-            functools.partial(line_wide_kernel, sizes=cross_sizes, wide_size=shard),
-            in_specs=[SMEM] + [VMEM] * 2,
-            out_specs=[VMEM] * 2,
-            out_shape=[
-                like((sum(cross_sizes) * narrow_count, model), BF16),
-                like((2 * rows, hidden_width), BF16),
-            ],
-            compiler_params=PARAMS,
-            cost_estimate=work(1),
-            name="line_wide",
-        )(narrow[None], joined_even, joined_odd)
-    else:
-        cross_block = line_block(cross_line, cross_sizes)
-        gate_block = line_block(gate_line, gate_sizes)
     self_parts = (
         self_held, self_came, cross_core(self_held, wide_count), cross_core(self_came, wide_count)
     )
-    cross_held = gather_early(tie(cross_block, self_came))
+    cross_block = tie(cross_block, self_came)
+    if aligned:
+        cross_block = tie(cross_block, gate_even)
+    cross_held = gather_early(cross_block)
+    if aligned:
+        cross_held = tie(cross_held, gate_odd)
+        gate_block = line_pair(gate_even, gate_odd, gate_sizes)
     cross_came = lax.ppermute(cross_held, "wide", last)
 
     head_rows = like((HEADS // 2, 1, 2 * tokens), F32)
@@ -1133,8 +1098,6 @@
     cross_parts = (
         cross_held, cross_came, cross_core(cross_held, wide_count), cross_core(cross_came, wide_count)
     )
-    gate_held = gather_early(tie(gate_block, cross_came))
-    gate_came = lax.ppermute(gate_held, "wide", last)
     cross_gathered = for_kernels(cross_parts, [size * narrow_count for size in cross_sizes])
 
     key_two, value_two = pl.pallas_call(
@@ -1150,6 +1113,9 @@
         cost_estimate=work(1),
         name="memory_projection",
     )(kernel_places, memory, *cross_gathered)
+
+    gate_held = gather_early(tie(gate_block, cross_came), key_two)
+    gate_came = lax.ppermute(gate_held, "wide", last)
 
     normed_two, query_two, attended_two, totals_two, stream_two = pl.pallas_call(
         cross_forward_kernel,
@@ -1196,7 +1162,11 @@
         name="mlp_forward",
     )(kernel_places, stream_two, gain_all, side, *gate_gathered, *cross_gathered)
 
-    exit_parts = gather_wide(normed_four, wide_count)
+    exit_held = gather_early(normed_four)
+    exit_came = tie(lax.ppermute(exit_held, "wide", last), table)
+    exit_parts = (
+        exit_held, exit_came, cross_core(exit_held, wide_count), cross_core(exit_came, wide_count)
+    )
     group = tokens * wide_count
     tiles = -(-group // (2 * ROW_TILE)) * 2
     kept = lambda i, meta: jnp.minimum(i, meta[META_TILES] - 1)

time: 500 us -> 483 us (0.966)
  waiting for transfers between devices: 153 us -> 135 us
    ppermute x7 -> x9, waiting for transfers between devices: 84.6 us -> 45 us  [the longest x4 22.6 us: gather_early(): came = lax.ppermute(held, 'wide', pairs)]
    all_gather x1, waiting for transfers between devices: 0.01 us -> 16.8 us  [per_device(): lax.all_gather(tie(turned, *self_line), 'narrow', axis=0, tiled=True)]
    ppermute x1, waiting for transfers between devices: 0.01 us -> 5.72 us  [per_device(): gate_came = lax.ppermute(gate_held, 'wide', last)]
    ppermute x7 -> x9, starting transfers between devices: 10.6 us -> 10.5 us  [the longest x2 5.27 us: line_even(): lax.ppermute(pack, 'narrow', narrow_pairs(narrow_count, step))]
  transfers between devices with their start and end apart: 58 -> 60, of which waited for: 23 -> 26; matrix products, arithmetic and copies ran while one was open for 10% -> 11% of each run, Pallas kernels for 31% -> 33%
where the time goes in v5:
time: 483 us; the launch traced here: 473 us
  Pallas kernels  206 us (43%)
  waiting for transfers between devices  135 us (28%)
  other arithmetic  53.5 us (11%)
  starting transfers between devices  53.2 us (11%)
  between operations  17.4 us (4%)
  local copies, waits for them, and re-layouts  8.12 us (2%)
    pallas_call x2, Pallas kernels, table_half(): pl.pallas_call(functools.partial(exit_table_kernel, first=side * half, vo...  26.6 us
    pallas_call x1, Pallas kernels, per_device(): pl.pallas_call(functools.partial(exit_scores_kernel, vocab=vocab, scale=s...  24.6 us
    pallas_call x1, Pallas kernels, per_device(): pl.pallas_call(functools.partial(exit_tokens_kernel, vocab=vocab), grid_s...  23.5 us
    ppermute x4, waiting for transfers between devices, gather_early(): came = lax.ppermute(held, 'wide', pairs)  22.6 us
    ppermute x2, waiting for transfers between devices, line_even(): lax.ppermute(pack, 'narrow', narrow_pairs(narrow_count, step))  21.9 us
    pallas_call x1, Pallas kernels, per_device(): pl.pallas_call(mlp_backward_kernel, in_specs=[SMEM] + [VMEM] * 8 + [ANY]...  19.8 us
    pallas_call x1, Pallas kernels, per_device(): pl.pallas_call(cross_backward_kernel, in_specs=[SMEM] + [VMEM] * 11 + [AN...  17 us
    all_gather x1, waiting for transfers between devices, per_device(): lax.all_gather(tie(turned, *self_line), 'narrow', axis=0, tiled=True)  16.8 us
  transfers between devices with their start and end apart: 60, of which 26 were waited for; matrix products, arithmetic and copies ran while one was open for 11% of the time, Pallas kernels for 33%

profile of v5, /device:TPU:0, one launch (start us, length us, event | category | flops | bytes accessed | tf_op | source)
XLA Modules:
  0.0 473.1 jit_solution(12671824830975935085)
XLA Ops:
  19.9 8.3 %collective-permute-done.1.refs_2_ = bf16[104,768]{1,0:T(8,128)(2,1)S(1)} collective-permute-done((bf16[104,768]{1,0:T(8,128)(2,1)}, bf16[104,768]{1,0:T(8,128)(2,1)S(1)}, u32[]{:S(2)}, u32[]{:S(2)}) %collective-permute-start.1) | collective-permute-done | bytes 159776 | tf_op jit(solution)/shard_map/ppermute | solution.py:139
  37.6 10.2 %collective-permute-done.3 = bf16[160,768]{1,0:T(8,128)(2,1)S(1)} collective-permute-done((bf16[160,768]{1,0:T(8,128)(2,1)}, bf16[160,768]{1,0:T(8,128)(2,1)S(1)}, u32[]{:S(2)}, u32[]{:S(2)}) %collective-permute-start.3) | collective-permute-done | bytes 245792 | tf_op jit(solution)/shard_map/ppermute | solution.py:1018
  53.0 11.7 %collective-permute-done.7 = bf16[48,2048]{1,0:T(8,128)(2,1)S(1)} collective-permute-done((bf16[48,2048]{1,0:T(8,128)(2,1)}, bf16[48,2048]{1,0:T(8,128)(2,1)S(1)}, u32[]{:S(2)}, u32[]{:S(2)}) %collective-permute-start.7) | collective-permute-done | bytes 196640 | tf_op jit(solution)/shard_map/ppermute | solution.py:1018
  72.3 11.2 %collective-permute-done.8 = bf16[1,640,768]{2,1,0:T(8,128)(2,1)} collective-permute-done((bf16[1,640,768]{2,1,0:T(8,128)(2,1)}, bf16[1,640,768]{2,1,0:T(8,128)(2,1)}, u32[]{:S(2)}, u32[]{:S(2)}) %collective-permute-start.8) | collective-permute-done | bytes 983072 | tf_op jit(solution)/shard_map/ppermute | solution.py:1006
  92.5 9.6 %self_forward.1 = (bf16[320,768]{1,0:T(8,128)(2,1)}, bf16[320,768]{1,0:T(8,128)(2,1)}, bf16[320,768]{1,0:T(8,128)(2,1)}, bf16[320,768]{1,0:T(8,128)(2,1)}, bf16[...) custom-call(s32[8]{0:T(128)} %fusion.43.places, s32[2]{0:T(128)} %bitcast.116, ...), custom_call_target="tpu_custom_call" | custom-call | flops 1000000000 | bytes 1000000 | tf_op jit(solution)/shard_map/self_forward/pallas_call | solution.py:1070
  102.1 8.0 %collective-permute-done.12.refs_1_.refs_5_ = bf16[2,640,768]{2,1,0:T(8,128)(2,1)} collective-permute-done((bf16[2,640,768]{2,1,0:T(8,128)(2,1)S(1)}, bf16[2,640,768]{2,1,0:T(8,128)(2,1)}, u32[]{:S(2)}, u32[]{:S(2)}) %collective-permute-start.12) | collective-permute-done | bytes 1966112 | tf_op jit(solution)/shard_map/ppermute | solution.py:1059
  114.4 7.0 %memory_projection.1 = (bf16[1024,768]{1,0:T(8,128)(2,1)}, bf16[1024,768]{1,0:T(8,128)(2,1)}) custom-call(s32[8]{0:T(128)} %fusion.43.places, bf16[1024,768]{1,0:T(8,128)(2,1)} %memory.3, bf16[2,640,768]{2,1,0:T(8,128)(2,1)} %copy-done, bf16[2,640,768]{2,1,0:T(8,128)(2,1)} %collective-permute-done.12.refs_1_.refs_5_, ...), custom_call_target="tpu_custom_call" | custom-call | flops 1000000000 | bytes 1000000 | tf_op jit(solution)/shard_map/memory_projection/pallas_call | solution.py:1103
  125.1 14.1 %cross_forward.1 = (bf16[320,768]{1,0:T(8,128)(2,1)}, bf16[320,768]{1,0:T(8,128)(2,1)}, bf16[320,768]{1,0:T(8,128)(2,1)}, f32[6,1,640]{2,1,0:T(1,128)}, f32[320,768]{1,0:T(8,128)}) custom-call(s32[8]{0:T(128)} %fusion.43.places, s32[2]{0:T(128)} %bitcast.117, s32[2]{0:T(128)} %bitcast.121, f32[320,768]{1,0:T(8,128)} %get-tuple-element.152.stream_in, ...), custom_call_target="tpu_custom_call" | custom-call | flops 1000000000 | bytes 1000000 | tf_op jit(solution)/shard_map/cross_forward/pallas_call | solution.py:1120
  148.5 11.2 %mlp_forward.1 = (bf16[320,768]{1,0:T(8,128)(2,1)}, f32[320,2048]{1,0:T(8,128)}, f32[320,2048]{1,0:T(8,128)}, bf16[320,2048]{1,0:T(8,128)(2,1)}, f32[320,768]{1,...) custom-call(s32[8]{0:T(128)} %fusion.43.places, f32[320,768]{1,0:T(8,128)} %get-tuple-element.155.stream_in.stream_two, ...), custom_call_target="tpu_custom_call" | custom-call | flops 1000000000 | bytes 1000000 | tf_op jit(solution)/shard_map/mlp_forward/pallas_call | solution.py:1146
  160.4 8.6 %collective-permute-done.19 = bf16[1,328,768]{2,1,0:T(8,128)(2,1)S(1)} collective-permute-done((bf16[1,328,768]{2,1,0:T(8,128)(2,1)}, bf16[1,328,768]{2,1,0:T(8,128)(2,1)S(1)}, u32[]{:S(2)}, u32[]{:S(2)}) %collective-permute-start.19) | collective-permute-done | bytes 503840 | tf_op jit(solution)/shard_map/ppermute | solution.py:1006
  170.7 16.8 %all-gather.2.cloned.1.call-done.refs_4_.refs_0_ = bf16[768,4096]{1,0:T(8,128)(2,1)} async-done(((bf16[192,4096]{1,0:T(8,128)(2,1)}), bf16[768,4096]{1,0:T(8,128)(2,1)}) %all-gather.2.cloned.1.call-update) | async-done | bytes 6291472 | tf_op jit(solution)/shard_map/all_gather | solution.py:999
  192.5 24.6 %exit_scores.1 = (bf16[2560,4096]{1,0:T(8,128)(2,1)}, bf16[768,2560]{1,0:T(8,128)(2,1)}, f32[8,2560]{1,0:T(8,128)}) custom-call(s32[18]{0:T(128)} %pad_add_fusion.meta, s32[8]{0:T(128)} %select_reduce_fusion.slot_of, bf16[2,328,768]{2,1,0:T(8,128)(2,1)} %copy-done.9, bf16[2,328,768]{2,1,0:T(8,128)(2,1)} %copy-done.24, bf16[2,328,768]{2,1,0:T(8,128)(2,1)} %copy-done.25, ...), custom_call_target="tpu_custom_call" | custom-call | flops 51999997952 | bytes 1000000 | tf_op jit(solution)/shard_map/exit_scores/pallas_call | solution.py:1175
  231.9 23.5 %exit_tokens.1 = (bf16[2,320,768]{2,1,0:T(8,128)(2,1)}, bf16[2,320,768]{2,1,0:T(8,128)(2,1)}, bf16[2,320,768]{2,1,0:T(8,128)(2,1)}, bf16[2,320,768]{2,1,0:T(8,128)(2,1)}) custom-call(s32[18]{0:T(128)} %pad_add_fusion.meta, s32[8]{0:T(128)} %fusion.43.places, bf16[768,4096]{1,0:T(8,128)(2,1)} %all-gather.2.cloned.1.call-done.refs_4_.refs_0_, ...), custom_call_target="tpu_custom_call" | custom-call | flops 49999998976 | bytes 1000000 | tf_op jit(solution)/shard_map/exit_tokens/pallas_call | solution.py:1221
  256.0 13.2 %exit_table.2.refs_0_ = bf16[768,4096]{1,0:T(8,128)(2,1)} custom-call(s32[18]{0:T(128)} %pad_add_fusion.meta, bf16[2560,4096]{1,0:T(8,128)(2,1)} %get-tuple-element.162.refs_1_.raised, bf16[768,2560]{1,0:T(8,128)(2,1)} %get-tuple-element.167.across, f32[8,2560]{1,0:T(8,128)} %maximum_maximum_fusion.2.refs_2_.factors), custom_call_target="tpu_custom_call" | custom-call | flops 15000000512 | bytes 1000000 | tf_op jit(solution)/shard_map/exit_table/pallas_call | solution.py:1249
  271.0 13.4 %exit_table.3 = bf16[768,4096]{1,0:T(8,128)(2,1)} custom-call(s32[18]{0:T(128)} %pad_add_fusion.meta, bf16[2560,4096]{1,0:T(8,128)(2,1)} %get-tuple-element.162.refs_1_.raised, bf16[768,2560]{1,0:T(8,128)(2,1)} %get-tuple-element.167.across, f32[8,2560]{1,0:T(8,128)} %maximum_maximum_fusion.2.refs_2_.factors, ...), custom_call_target="tpu_custom_call", output_to_operand_aliasing={{}: (4, {})} | custom-call | flops 15000000512 | bytes 1000000 | tf_op jit(solution)/shard_map/exit_table/pallas_call | solution.py:1249
  287.3 7.3 %collective-permute-done.29 = bf16[320,768]{1,0:T(8,128)(2,1)S(1)} collective-permute-done((bf16[320,768]{1,0:T(8,128)(2,1)S(1)}, bf16[320,768]{1,0:T(8,128)(2,1)S(1)}, u32[]{:S(2)}, u32[]{:S(2)}) %collective-permute-start.29) | collective-permute-done | bytes 491552 | tf_op jit(solution)/shard_map/ppermute | solution.py:117
  296.9 19.8 %mlp_backward.1 = (f32[320,768]{1,0:T(8,128)}, f32[8,768]{1,0:T(8,128)}, bf16[2,192,2048]{2,1,0:T(8,128)(2,1)}, bf16[2,192,2048]{2,1,0:T(8,128)(2,1)}, bf16[2,19...) custom-call(s32[8]{0:T(128)} %fusion.43.places, ...), custom_call_target="tpu_custom_call" | custom-call | flops 15000000512 | bytes 1000000 | tf_op jit(solution)/shard_map/mlp_backward/pallas_call | solution.py:1281
  318.4 11.0 %cross_attention_first.1 = (bf16[320,768]{1,0:T(8,128)(2,1)}, bf16[320,768]{1,0:T(8,128)(2,1)}, bf16[320,384]{1,0:T(8,128)(2,1)}, bf16[1024,384]{1,0:T(8,128)(2,1)}, bf16[1024,384]{1,0:T(8,128)(2,1)}) custom-call(s32[8]{0:T(128)} %fusion.43.places, s32[2]{0:T(128)} %bitcast.118, s32[2]{0:T(128)} %bitcast.122, f32[320,768]{1,0:T(8,128)} %get-tuple-element.177.grad_in, ...), custom_call_target="tpu_custom_call" | custom-call | flops 16000000000 | bytes 1000000 | tf_op jit(solution)/shard_map/cross_attention_first/pallas_call | solution.py:1323
  335.6 10.9 %cross_attention_last.1 = (bf16[320,768]{1,0:T(8,128)(2,1)}, bf16[1024,768]{1,0:T(8,128)(2,1)}, bf16[1024,768]{1,0:T(8,128)(2,1)}) custom-call(s32[2]{0:T(128)} %bitcast.119, s32[2]{0:T(128)} %bitcast.123, bf16[320,768]{1,0:T(8,128)(2,1)} %get-tuple-element.188.attended_grad, bf16[320,768]{1,0:T(8,128)(2,1)} %get-tuple-element.178.query, ...), custom_call_target="tpu_custom_call" | custom-call | flops 16000000000 | bytes 1000000 | tf_op jit(solution)/shard_map/cross_attention_last/pallas_call | solution.py:1342
  347.1 5.8 %collective-permute-start.34 = (f32[8,128]{1,0:T(8,128)S(1)}, f32[8,128]{1,0:T(8,128)S(1)}, u32[]{:S(2)}, u32[]{:S(2)}) collective-permute-start(f32[8,128]{1,0:T(8,128)S(1)} %broadcast_in_dim.74), channel_id=1, source_target_pairs={{0,3},{1,2},{2,1},{3,0},{4,7},{5,6},{6,5},{7,4},{8,11},{9,10},{10,... | collective-permute-start | bytes 12296 | tf_op jit(solution)/shard_map/ppermute | solution.py:1359
  352.9 17.0 %cross_backward.1 = (f32[320,768]{1,0:T(8,128)}, f32[8,768]{1,0:T(8,128)}, f32[1024,768]{1,0:T(8,128)}, bf16[320,768]{1,0:T(8,128)(2,1)}, bf16[2,480,768]{2,1,0:...) custom-call(s32[8]{0:T(128)} %fusion.43.places, ...), custom_call_target="tpu_custom_call" | custom-call | flops 20000000000 | bytes 1000000 | tf_op jit(solution)/shard_map/cross_backward/pallas_call | solution.py:1362
  378.7 8.5 %self_attention_backward.1 = (bf16[320,768]{1,0:T(8,128)(2,1)}, bf16[320,768]{1,0:T(8,128)(2,1)}, bf16[320,768]{1,0:T(8,128)(2,1)}) custom-call(s32[8]{0:T(128)} %fusion.43.places, s32[2]{0:T(128)} %bitcast.120, bf16[320,768]{1,0:T(8,128)(2,1)} %get-tuple-element.207.branch, bf16[320,768]{1,0:T(8,128)(2,1)} %get-tuple-element.208.query, ...), custom_call_target="tpu_custom_call" | custom-call | flops 10000000000 | bytes 1000000 | tf_op jit(solution)/shard_map/self_attention_backward/pallas_call | solution.py:1386
  393.8 10.7 %self_backward.1 = (f32[320,768]{1,0:T(8,128)}, bf16[2,320,768]{2,1,0:T(8,128)(2,1)}, bf16[2,320,768]{2,1,0:T(8,128)(2,1)}, bf16[2,320,768]{2,1,0:T(8,128)(2,1)}, bf16[2,320,768]{2,1,0:T(8,128)(2,1)}) custom-call(s32[8]{0:T(128)} %fusion.43.places, f32[320,768]{1,0:T(8,128)} %get-tuple-element.217.grad_in, bf16[320,768]{1,0:T(8,128)(2,1)} %inputs.2, ...), custom_call_target="tpu_custom_call" | custom-call | flops 12000000000 | bytes 1000000 | tf_op jit(solution)/shard_map/self_backward/pallas_call | solution.py:1438
  453.6 7.2 %collective-permute-done.55 = bf16[120,768]{1,0:T(8,128)(2,1)S(1)} collective-permute-done((bf16[120,768]{1,0:T(8,128)(2,1)S(1)}, bf16[120,768]{1,0:T(8,128)(2,1)S(1)}, u32[]{:S(2)}, u32[]{:S(2)}) %collective-permute-start.55) | collective-permute-done | bytes 184352 | tf_op jit(solution)/shard_map/ppermute | solution.py:1430
  (255 shorter events, 166.4 us)
Async XLA Ops:
  7.2 180.3 %all-gather.2.cloned.1.call-start = ((), (), s32[]{:S(2)}) async-start(), calls=%async_computation.1 | async-start | bytes 7864320 | tf_op jit(solution)/shard_map/all_gather | solution.py:999
  30.9 17.9 %collective-permute-start.5 = (bf16[1,416,768]{2,1,0:T(8,128)(2,1)}, bf16[1,416,768]{2,1,0:T(8,128)(2,1)S(1)}, u32[]{:S(2)}, u32[]{:S(2)}) collective-permute-start(bf16[1,416,768]{2,1,0:T(8,128)(2,1)} %bitcast.106), channel_id=1, source_target_pairs={{0,8},{4,20},{8,0},{12,28},{16,24},{20,4},{24,16},{28,12},{1,9},{5... | collective-permute-start | bytes 1916936 | tf_op jit(solution)/shard_map/ppermute | solution.py:1006
  49.0 20.0 %collective-permute-start.6 = (bf16[2,416,768]{2,1,0:T(8,128)(2,1)S(1)}, bf16[2,416,768]{2,1,0:T(8,128)(2,1)}, u32[]{:S(2)}, u32[]{:S(2)}) collective-permute-start(bf16[2,416,768]{2,1,0:T(8,128)(2,1)S(1)} %pad_maximum_fusion.2.refs_0_), channel_id=1, source_target_pairs={{0,16},{4,12},{8,24},{12,4},{16,0},{20,28},{24,8},{28,20},{1,17},{... | collective-permute-start | bytes 3833864 | tf_op jit(solution)/shard_map/ppermute | solution.py:1048
  72.3 352.6 %reduce-scatter.2.cloned.1.call-start = ((), (), s32[]{:S(2)}) async-start(), calls=%async_computation.2 | async-start | bytes 7864320 | tf_op jit(solution)/shard_map/reduce_scatter | solution.py:1275
  85.3 24.8 %collective-permute-start.12 = (bf16[2,640,768]{2,1,0:T(8,128)(2,1)S(1)}, bf16[2,640,768]{2,1,0:T(8,128)(2,1)}, u32[]{:S(2)}, u32[]{:S(2)}) collective-permute-start(bf16[2,640,768]{2,1,0:T(8,128)(2,1)S(1)} %pad_maximum_fusion.refs_0_.refs_4_), channel_id=1, source_target_pairs={{0,16},{4,12},{8,24},{12,4},{16,0},{20,28},{24,8},{28,20},{1,17},{... | collective-permute-start | bytes 5898248 | tf_op jit(solution)/shard_map/ppermute | solution.py:1059
  86.9 25.8 %collective-permute-start.14 = (bf16[2,640,768]{2,1,0:T(8,128)(2,1)S(1)}, bf16[2,640,768]{2,1,0:T(8,128)(2,1)}, u32[]{:S(2)}, u32[]{:S(2)}) collective-permute-start(bf16[2,640,768]{2,1,0:T(8,128)(2,1)S(1)} %pad_maximum_fusion.refs_0_.refs_4_), channel_id=1, source_target_pairs={{0,4},{4,0},{8,12},{12,8},{16,20},{20,16},{24,28},{28,24},{1,5},{5... | collective-permute-start | bytes 5898248 | tf_op jit(solution)/shard_map/ppermute | solution.py:89
  124.5 20.5 %collective-permute-start.16 = (bf16[2,192,2048]{2,1,0:T(8,128)(2,1)S(1)}, bf16[2,192,2048]{2,1,0:T(8,128)(2,1)S(1)}, u32[]{:S(2)}, u32[]{:S(2)}) collective-permute-start(bf16[2,192,2048]{2,1,0:T(8,128)(2,1)S(1)} %pad_maximum_fusion.1.refs_0_), channel_id=1, source_target_pairs={{0,16},{4,12},{8,24},{12,4},{16,0},{20,28},{24,8},{28,20},{1,17},{... | collective-permute-start | bytes 4718600 | tf_op jit(solution)/shard_map/ppermute | solution.py:1118
  125.1 20.6 %collective-permute-start.17 = (bf16[2,192,2048]{2,1,0:T(8,128)(2,1)S(1)}, bf16[2,192,2048]{2,1,0:T(8,128)(2,1)}, u32[]{:S(2)}, u32[]{:S(2)}) collective-permute-start(bf16[2,192,2048]{2,1,0:T(8,128)(2,1)S(1)} %pad_maximum_fusion.1.refs_0_), channel_id=1, source_target_pairs={{0,4},{4,0},{8,12},{12,8},{16,20},{20,16},{24,28},{28,24},{1,5},{5... | collective-permute-start | bytes 4718600 | tf_op jit(solution)/shard_map/ppermute | solution.py:89
  170.1 17.4 %collective-permute-start.20 = (bf16[2,328,768]{2,1,0:T(8,128)(2,1)S(1)}, bf16[2,328,768]{2,1,0:T(8,128)(2,1)S(1)}, u32[]{:S(2)}, u32[]{:S(2)}) collective-permute-start(bf16[2,328,768]{2,1,0:T(8,128)(2,1)S(1)} %pad_maximum_fusion.3.refs_0_), channel_id=1, source_target_pairs={{0,16},{4,12},{8,24},{12,4},{16,0},{20,28},{24,8},{28,20},{1,17},{... | collective-permute-start | bytes 3022856 | tf_op jit(solution)/shard_map/ppermute | solution.py:1166
  170.7 20.8 %collective-permute-start.21 = (bf16[2,328,768]{2,1,0:T(8,128)(2,1)S(1)}, bf16[2,328,768]{2,1,0:T(8,128)(2,1)S(1)}, u32[]{:S(2)}, u32[]{:S(2)}) collective-permute-start(bf16[2,328,768]{2,1,0:T(8,128)(2,1)S(1)} %pad_maximum_fusion.3.refs_0_), channel_id=1, source_target_pairs={{0,4},{4,0},{8,12},{12,8},{16,20},{20,16},{24,28},{28,24},{1,5},{5... | collective-permute-start | bytes 3022856 | tf_op jit(solution)/shard_map/ppermute | solution.py:89
  255.4 29.0 %collective-permute-start.26 = (bf16[2,320,768]{2,1,0:T(8,128)(2,1)}, bf16[2,320,768]{2,1,0:T(8,128)(2,1)S(1)}, u32[]{:S(2)}, u32[]{:S(2)}) collective-permute-start(bf16[2,320,768]{2,1,0:T(8,128)(2,1)} %get-tuple-element.164), channel_id=1, source_target_pairs={{0,4},{4,0},{8,12},{12,8},{16,20},{20,16},{24,28},{28,24},{1,5},{5... | collective-permute-start | bytes 2949128 | tf_op jit(solution)/shard_map/ppermute | solution.py:89
  317.9 56.9 %collective-permute-start.35 = (bf16[2,192,2048]{2,1,0:T(8,128)(2,1)}, bf16[2,192,2048]{2,1,0:T(8,128)(2,1)S(1)}, u32[]{:S(2)}, u32[]{:S(2)}) collective-permute-start(bf16[2,192,2048]{2,1,0:T(8,128)(2,1)} %get-tuple-element.201), channel_id=1, source_target_pairs={{0,4},{4,0},{8,12},{12,8},{16,20},{20,16},{24,28},{28,24},{1,5},{5... | collective-permute-start | bytes 4718600 | tf_op jit(solution)/shard_map/ppermute | solution.py:89
  317.9 52.0 %collective-permute-start.38 = (bf16[2,256,768]{2,1,0:T(8,128)(2,1)}, bf16[2,256,768]{2,1,0:T(8,128)(2,1)}, u32[]{:S(2)}, u32[]{:S(2)}) collective-permute-start(bf16[2,256,768]{2,1,0:T(8,128)(2,1)} %get-tuple-element.205), channel_id=1, source_target_pairs={{0,4},{4,0},{8,12},{12,8},{16,20},{20,16},{24,28},{28,24},{1,5},{5... | collective-permute-start | bytes 2359304 | tf_op jit(solution)/shard_map/ppermute | solution.py:89
  331.8 38.1 %collective-permute-start.39 = (bf16[2,256,768]{2,1,0:T(8,128)(2,1)}, bf16[2,256,768]{2,1,0:T(8,128)(2,1)}, u32[]{:S(2)}, u32[]{:S(2)}) collective-permute-start(bf16[2,256,768]{2,1,0:T(8,128)(2,1)} %add.288), channel_id=1, source_target_pairs={{0,16},{4,12},{8,24},{12,4},{16,0},{20,28},{24,8},{28,20},{1,17},{... | collective-permute-start | bytes 2359304 | tf_op jit(solution)/shard_map/ppermute | solution.py:108
  334.4 40.3 %collective-permute-start.36 = (bf16[2,192,2048]{2,1,0:T(8,128)(2,1)}, bf16[2,192,2048]{2,1,0:T(8,128)(2,1)}, u32[]{:S(2)}, u32[]{:S(2)}) collective-permute-start(bf16[2,192,2048]{2,1,0:T(8,128)(2,1)} %add.287), channel_id=1, source_target_pairs={{0,16},{4,12},{8,24},{12,4},{16,0},{20,28},{24,8},{28,20},{1,17},{... | collective-permute-start | bytes 4718600 | tf_op jit(solution)/shard_map/ppermute | solution.py:108
  347.1 25.4 %collective-permute-start.34 = (f32[8,128]{1,0:T(8,128)S(1)}, f32[8,128]{1,0:T(8,128)S(1)}, u32[]{:S(2)}, u32[]{:S(2)}) collective-permute-start(f32[8,128]{1,0:T(8,128)S(1)} %broadcast_in_dim.74), channel_id=1, source_target_pairs={{0,3},{1,2},{2,1},{3,0},{4,7},{5,6},{6,5},{7,4},{8,11},{9,10},{10,... | collective-permute-start | bytes 12296 | tf_op jit(solution)/shard_map/ppermute | solution.py:1359
  374.7 37.4 %collective-permute-start.43 = (bf16[2,480,768]{2,1,0:T(8,128)(2,1)}, bf16[2,480,768]{2,1,0:T(8,128)(2,1)}, u32[]{:S(2)}, u32[]{:S(2)}) collective-permute-start(bf16[2,480,768]{2,1,0:T(8,128)(2,1)} %get-tuple-element.230), channel_id=1, source_target_pairs={{0,4},{4,0},{8,12},{12,8},{16,20},{20,16},{24,28},{28,24},{1,5},{5... | collective-permute-start | bytes 4423688 | tf_op jit(solution)/shard_map/ppermute | solution.py:89
  390.4 21.7 %collective-permute-start.44 = (bf16[2,480,768]{2,1,0:T(8,128)(2,1)}, bf16[2,480,768]{2,1,0:T(8,128)(2,1)}, u32[]{:S(2)}, u32[]{:S(2)}) collective-permute-start(bf16[2,480,768]{2,1,0:T(8,128)(2,1)} %add.300), channel_id=1, source_target_pairs={{0,16},{4,12},{8,24},{12,4},{16,0},{20,28},{24,8},{28,20},{1,17},{... | collective-permute-start | bytes 4423688 | tf_op jit(solution)/shard_map/ppermute | solution.py:108
  412.2 24.4 %collective-permute-start.41 = (bf16[2,320,768]{2,1,0:T(8,128)(2,1)}, bf16[2,320,768]{2,1,0:T(8,128)(2,1)}, u32[]{:S(2)}, u32[]{:S(2)}) collective-permute-start(bf16[2,320,768]{2,1,0:T(8,128)(2,1)} %get-tuple-element.226), channel_id=1, source_target_pairs={{0,4},{4,0},{8,12},{12,8},{16,20},{20,16},{24,28},{28,24},{1,5},{5... | collective-permute-start | bytes 2949128 | tf_op jit(solution)/shard_map/ppermute | solution.py:89
  414.7 17.5 %collective-permute-start.46 = (bf16[480,768]{1,0:T(8,128)(2,1)}, bf16[480,768]{1,0:T(8,128)(2,1)S(1)}, u32[]{:S(2)}, u32[]{:S(2)}) collective-permute-start(bf16[480,768]{1,0:T(8,128)(2,1)} %fusion.1), channel_id=1, source_target_pairs={{0,8},{4,20},{8,0},{12,28},{16,24},{20,4},{24,16},{28,12},{1,9},{5... | collective-permute-start | bytes 2211848 | tf_op jit(solution)/shard_map/ppermute | solution.py:117
  418.2 18.4 %collective-permute-start.45 = (bf16[2,320,768]{2,1,0:T(8,128)(2,1)}, bf16[2,320,768]{2,1,0:T(8,128)(2,1)}, u32[]{:S(2)}, u32[]{:S(2)}) collective-permute-start(bf16[2,320,768]{2,1,0:T(8,128)(2,1)} %add.304), channel_id=1, source_target_pairs={{0,16},{4,12},{8,24},{12,4},{16,0},{20,28},{24,8},{28,20},{1,17},{... | collective-permute-start | bytes 2949128 | tf_op jit(solution)/shard_map/ppermute | solution.py:108
  421.4 17.5 %collective-permute-start.51 = (bf16[2,64,768]{2,1,0:T(8,128)(2,1)}, bf16[2,64,768]{2,1,0:T(8,128)(2,1)}, u32[]{:S(2)}, u32[]{:S(2)}) collective-permute-start(bf16[2,64,768]{2,1,0:T(8,128)(2,1)} %pad_maximum_fusion.8), channel_id=1, source_target_pairs={{0,1},{1,0},{2,3},{3,2},{4,5},{5,4},{6,7},{7,6},{8,9},{9,8},{10,11... | collective-permute-start | bytes 589832 | tf_op jit(solution)/shard_map/ppermute | solution.py:1421
  422.6 17.4 %collective-permute-start.56 = (bf16[48,2048]{1,0:T(8,128)(2,1)}, bf16[48,2048]{1,0:T(8,128)(2,1)S(1)}, u32[]{:S(2)}, u32[]{:S(2)}) collective-permute-start(bf16[48,2048]{1,0:T(8,128)(2,1)} %get-tuple-element.268), channel_id=1, source_target_pairs={{0,2},{1,3},{2,0},{3,1},{4,6},{5,7},{6,4},{7,5},{8,10},{9,11},{10,... | collective-permute-start | bytes 589832 | tf_op jit(solution)/shard_map/ppermute | solution.py:1430
  443.1 17.7 %collective-permute-start.55 = (bf16[120,768]{1,0:T(8,128)(2,1)S(1)}, bf16[120,768]{1,0:T(8,128)(2,1)S(1)}, u32[]{:S(2)}, u32[]{:S(2)}) collective-permute-start(bf16[120,768]{1,0:T(8,128)(2,1)S(1)} %get-tuple-element.270), channel_id=1, source_target_pairs={{0,2},{1,3},{2,0},{3,1},{4,6},{5,7},{6,4},{7,5},{8,10},{9,11},{10,... | collective-permute-start | bytes 552968 | tf_op jit(solution)/shard_map/ppermute | solution.py:1430
  (65 other events, 707.0 us)
Sparse Core Ops, SparseCore 0:
  72.4 115.0 all-gather.1
  287.4 112.5 reduce-scatter.1
